TPU v7x, 128 devices: a whole 4x4x4 slice. The times are simulated.
128 devices in a mesh: dp: 8 (over x_hi, y), expert: 16 (over z, x_lo, core).
Axes of the slice: x: 4 (x_hi: 2, x_lo: 2; x = x_hi * 2 + x_lo), y: 4, z: 4, core: 2. Of those that a mesh axis runs over, the one named last changes fastest.
Arguments:
- tokens: bfloat16 [32768, 2048], P(('dp', 'expert')), may hold values from -24 to 24
- cotangent: bfloat16 [32768, 2048], P(('dp', 'expert')), may hold values from -6 to 6
- route_gates: float32 [32768, 2], P(('dp', 'expert')), may hold values from 0.2 to 1
- w_gate_up: bfloat16 [16, 2048, 1536], P('expert'), may hold values from -0.125 to 0.125
- w_down: bfloat16 [16, 768, 2048], P('expert'), may hold values from -0.21875 to 0.21875
- expert_ids: int32 [32768, 2], P(('dp', 'expert')), may hold values from 0 to 15, as said below
- dest_ranks: int32 [32768, 2], P(('dp', 'expert')), may hold values from 0 to 15, as said below
- slot_ids: int32 [32768, 2], P(('dp', 'expert')), may hold values from -1 to 19, as said below
Outputs:
- mixed: bfloat16 [32768, 2048], P(('dp', 'expert'))
- token_grad: bfloat16 [32768, 2048], P(('dp', 'expert'))
- grad_gate_up: float32 [16, 2048, 1536], P('expert', 'dp')
- grad_down: float32 [16, 768, 2048], P('expert', 'dp')
Inputs may be any that keep to these rules, and one draw needn't show every extreme that they name: `expert_ids`: the 2 routes of a token name different experts. `dest_ranks`: each route's serving device is its expert's own index or, for one hot expert that is the same for all tokens, one of 4 helper devices, the same for all tokens and different from the hot expert's own. `slot_ids`: A served route's row lies in the block that its token's device fills for one serving device and one copy (home or replica); no two routes of one device share a row of one block. For the hot expert, every device fills each of its blocks, at home and at every helper, with 20 routes.
All inputs are finite; a program needn't handle non-finite values.
Results may differ from a plain program's by a relative error of at most 0.015.
Values may be sent and summed in bfloat16 or wider, within the bound.
No kernel may reach another device: no remote copies, remote signals or barrier semaphores. Data moves between devices by JAX's collectives and lax.ppermute only.
A program may use at most 192 MiB of HBM per device.

v0:
```python
import jax
import jax.numpy as jnp
from jax import lax
from jax.sharding import PartitionSpec as P


def from_root(block, axis, holder):
    block = jnp.where(lax.axis_index(axis) == holder, block, jnp.zeros_like(block))
    return lax.psum(block, axis)


def swiglu_pass(rows_in, rows_cot, weight_in, weight_out):
    unit_count = weight_out.shape[0]
    hidden = jnp.dot(rows_in, weight_in, preferred_element_type=jnp.float32)
    gate_part = hidden[:, :unit_count]
    up_part = hidden[:, unit_count:]
    sig_gate = jax.nn.sigmoid(gate_part)
    silu_gate = gate_part * sig_gate
    active = (silu_gate * up_part).astype(jnp.bfloat16)
    expert_out = jnp.dot(active, weight_out, preferred_element_type=jnp.float32).astype(
        jnp.bfloat16
    )
    grad_active = lax.dot_general(
        rows_cot, weight_out, (((1,), (1,)), ((), ())), preferred_element_type=jnp.float32
    )
    grad_out = lax.dot_general(
        active, rows_cot, (((0,), (0,)), ((), ())), preferred_element_type=jnp.float32
    ).astype(jnp.bfloat16)
    grad_gate_act = grad_active * up_part * sig_gate * (1.0 + gate_part * (1.0 - sig_gate))
    grad_up_act = grad_active * silu_gate
    grad_hidden = jnp.concatenate([grad_gate_act, grad_up_act], axis=1).astype(jnp.bfloat16)
    back_rows = lax.dot_general(
        grad_hidden, weight_in, (((1,), (1,)), ((), ())), preferred_element_type=jnp.float32
    ).astype(jnp.bfloat16)
    grad_in = lax.dot_general(
        rows_in, grad_hidden, (((0,), (0,)), ((), ())), preferred_element_type=jnp.float32
    ).astype(jnp.bfloat16)
    return (expert_out, back_rows, grad_in, grad_out)


def shards(tokens, cotangent, route_gates, w_gate_up, w_down, expert_ids, dest_ranks, slot_ids):
    groups = lax.axis_size("expert")
    my_rank = lax.axis_index("expert")
    tok_rows, model_width = tokens.shape
    fanout = expert_ids.shape[1]
    capacity = tok_rows * fanout * 5 // (8 * groups)
    served = slot_ids >= 0
    copy_flag = (expert_ids != dest_ranks).astype(jnp.int32)
    hot_expert = jnp.max(jnp.where(served & (copy_flag > 0), expert_ids, -1))
    buffer_len = 2 * groups * capacity
    position = (copy_flag * groups + dest_ranks) * capacity + slot_ids
    send_pos = jnp.where(served, position, buffer_len).reshape(-1)
    route_index = jnp.arange(tok_rows * fanout, dtype=jnp.int32)
    route_table = jnp.full((buffer_len,), -1, jnp.int32).at[send_pos].set(route_index, mode="drop")
    filled = route_table >= 0
    source = jnp.where(filled, route_table, 0)
    source_tok = source // fanout
    x_rows = jnp.where(filled[:, None], tokens[source_tok], jnp.zeros((), jnp.bfloat16))
    gate_flat = route_gates.reshape(-1)
    scaled = gate_flat[source][:, None] * cotangent[source_tok].astype(jnp.float32)
    g_rows = jnp.where(filled[:, None], scaled, 0.0).astype(jnp.bfloat16)
    x_rows = x_rows.reshape(2, groups, capacity, model_width)
    g_rows = g_rows.reshape(2, groups, capacity, model_width)
    rep_in, rep_out = (
        from_root(w_gate_up, "expert", hot_expert),
        from_root(w_down, "expert", hot_expert),
    )
    recv_rows, recv_cots = (
        lax.all_to_all(x_rows, "expert", split_axis=1, concat_axis=1, tiled=True),
        lax.all_to_all(g_rows, "expert", split_axis=1, concat_axis=1, tiled=True),
    )
    home_part = swiglu_pass(
        recv_rows[0].reshape(-1, model_width),
        recv_cots[0].reshape(-1, model_width),
        w_gate_up[0],
        w_down[0],
    )
    replica_part = swiglu_pass(
        recv_rows[1].reshape(-1, model_width),
        recv_cots[1].reshape(-1, model_width),
        rep_in[0],
        rep_out[0],
    )
    out_stack = jnp.stack([home_part[0], replica_part[0]]).reshape(2, groups, capacity, model_width)
    back_stack = jnp.stack([home_part[1], replica_part[1]]).reshape(
        2, groups, capacity, model_width
    )
    ret_out, ret_back = (
        lax.all_to_all(out_stack, "expert", split_axis=1, concat_axis=1, tiled=True),
        lax.all_to_all(back_stack, "expert", split_axis=1, concat_axis=1, tiled=True),
    )
    ret_out = ret_out.reshape(-1, model_width)
    ret_back = ret_back.reshape(-1, model_width)
    pick_pos = jnp.where(served, position, 0).reshape(-1)
    weights = jnp.where(served, route_gates, 0.0)
    picked_out = ret_out[pick_pos].astype(jnp.float32).reshape(tok_rows, fanout, model_width)
    mixed = jnp.sum(weights[..., None] * picked_out, axis=1).astype(jnp.bfloat16)
    picked_back = ret_back[pick_pos].astype(jnp.float32).reshape(tok_rows, fanout, model_width)
    token_grad = jnp.sum(jnp.where(served[..., None], picked_back, 0.0), axis=1).astype(
        jnp.bfloat16
    )
    is_home = my_rank == hot_expert
    summed = (
        lax.psum_scatter(home_part[2], "dp", scatter_dimension=0, tiled=True).astype(jnp.float32),
        lax.psum_scatter(home_part[3], "dp", scatter_dimension=0, tiled=True).astype(jnp.float32),
        lax.psum_scatter(replica_part[2], "dp", scatter_dimension=0, tiled=True).astype(
            jnp.float32
        ),
        lax.psum_scatter(replica_part[3], "dp", scatter_dimension=0, tiled=True).astype(
            jnp.float32
        ),
    )
    spare_in, spare_down = (
        lax.psum(summed[2].astype(jnp.bfloat16), "expert").astype(jnp.float32),
        lax.psum(summed[3].astype(jnp.bfloat16), "expert").astype(jnp.float32),
    )
    home_in = summed[0]
    home_down = summed[1]
    grad_gate_up = home_in + jnp.where(is_home, spare_in, 0.0)
    grad_down = home_down + jnp.where(is_home, spare_down, 0.0)
    return (mixed, token_grad, grad_gate_up[None], grad_down[None])


def solution(mesh):
    return jax.shard_map(
        shards,
        mesh=mesh,
        in_specs=(
            P(("dp", "expert"), None),
            P(("dp", "expert"), None),
            P(("dp", "expert"), None),
            P("expert", None, None),
            P("expert", None, None),
            P(("dp", "expert"), None),
            P(("dp", "expert"), None),
            P(("dp", "expert"), None),
        ),
        out_specs=(
            P(("dp", "expert"), None),
            P(("dp", "expert"), None),
            P("expert", "dp", None),
            P("expert", "dp", None),
        ),
        check_vma=False,
    )
```

profile of v0, /device:TPU:1, one launch (start us, length us, event | category | flops | bytes accessed | tf_op | source)
XLA Modules:
  0.0 810.2 jit_solution(6654567336487628587)
XLA Ops:
  7.2 0.8 broadcast_select_fusion.1
  8.0 1.4 broadcast_select_fusion.2
  10.0 6.0 select_bitcast_fusion
  16.0 1.9 select_bitcast_fusion.1
  18.2 2.4 scatter_custom_fusion
  20.7 4.1 gather_fusion
  24.9 3.6 gather.18
  28.7 3.1 copy_select_fusion
  31.8 4.3 copy.47
  36.1 5.3 all-to-all-start
  41.6 4.1 gather_fusion.3
  45.7 5.5 reshape.127
  51.3 4.3 gather_fusion.2
  55.9 6.3 fusion.5
  62.2 4.2 copy.55
  66.4 36.2 %all-to-all-done = bf16[2,16,20,2048]{3,0,2,1:T(2,128)(2,1)} async-done(((bf16[2,16,20,2048]{3,0,2,1:T(2,128)(2,1)}), bf16[2,16,20,2048]{3,0,2,1:T(2,128)(2,1)}, u32[]{:S(2)}, u32[]{:S(2)}) %all-to-all-start) | async-done | bytes 2621472 | tf_op jit(solution)/shard_map/all_to_all | solution.py:69
  102.5 4.3 all-to-all-start.2
  107.1 14.5 %slice_reduce_fusion.3 = (bf16[16,20,2048]{2,1,0:T(8,128)(2,1)}, bf16[16,20,2048]{2,1,0:T(8,128)(2,1)}) fusion(bf16[2,16,20,2048]{3,0,2,1:T(2,128)(2,1)} %all-to-all-done), kind=kLoop, calls=%fused_computation.34 | loop fusion | bytes 5242880 | tf_op jit(solution)/shard_map/slice | solution.py:73
  121.6 3.3 reshape_squeeze.13
  124.9 43.3 %all-to-all-done.2 = bf16[2,16,20,2048]{3,0,2,1:T(2,128)(2,1)S(1)} async-done(((bf16[2,16,20,2048]{3,0,2,1:T(2,128)(2,1)}), bf16[2,16,20,2048]{3,0,2,1:T(2,128)(2,1)S(1)}, u32[]{:S(2)}, u32[]{:S(2)}) %all-to-all-start.2) | async-done | bytes 2621472 | tf_op jit(solution)/shard_map/all_to_all | solution.py:70
  168.2 15.0 %slice_reduce_fusion.1 = (bf16[16,20,2048]{2,1,0:T(8,128)(2,1)}, bf16[16,20,2048]{2,1,0:T(8,128)(2,1)}) fusion(bf16[2,16,20,2048]{3,0,2,1:T(2,128)(2,1)S(1)} %all-to-all-done.2), kind=kLoop, calls=%fused_computation.32 | loop fusion | bytes 5242880 | tf_op jit(solution)/shard_map/slice | solution.py:74
  183.1 2.4 reshape_squeeze.15
  185.5 104.2 %all-reduce.7.cloned.1.call-done = (bf16[2048,1536]{1,0:T(8,128)(2,1)}, bf16[768,2048]{1,0:T(8,128)(2,1)}) async-done(((bf16[2048,1536]{1,0:T(8,128)(2,1)}, bf16[768,2048]{1,0:T(8,128)(2,1)}), (bf16[2048,1536]{1,0:T(8,128)(2,1)}, bf16[768,2048]{1,0:T(8,128)(2,1)})) %all-reduce.7.cloned.1.call-update) | async-done | bytes 9437200 | tf_op jit(solution)/shard_map/psum | solution.py:9
  289.7 5.1 fusion.27
  294.8 2.5 multiply_convert_fusion.1
  297.4 3.5 convolution_convert_fusion.2
  302.0 5.5 convolution_convert_fusion
  307.6 1.3 copy-done.5
  308.9 1.2 reshape_squeeze.14
  310.5 5.2 fusion.2
  315.7 1.6 multiply_convert_fusion.3
  317.3 0.8 copy-done.14
  318.1 3.5 convolution_convert_fusion.3
  321.6 57.8 %reduce-scatter.11.cloned.1.call-done = bf16[96,2048]{1,0:T(8,128)(2,1)} async-done(((bf16[768,2048]{1,0:T(8,128)(2,1)}), bf16[96,2048]{1,0:T(8,128)(2,1)}) %reduce-scatter.11.cloned.1.call-update) | async-done | bytes 393232 | tf_op jit(solution)/shard_map/reduce_scatter | solution.py:109
  379.5 101.6 %reduce-scatter.7.cloned.1.call-done = bf16[256,1536]{1,0:T(8,128)(2,1)} async-done(((bf16[2048,1536]{1,0:T(8,128)(2,1)}), bf16[256,1536]{1,0:T(8,128)(2,1)}) %reduce-scatter.7.cloned.1.call-update) | async-done | bytes 786448 | tf_op jit(solution)/shard_map/reduce_scatter | solution.py:106
  481.6 5.5 convolution_convert_fusion.1
  487.1 5.0 fusion.10
  492.5 6.6 convolution_convert_fusion.4
  499.1 2.2 stack.22
  501.7 4.2 copy.56
  505.9 6.1 all-to-all-start.3
  512.0 4.2 fusion.13
  516.2 3.3 stack.18
  519.5 4.1 convolution_convert_fusion.5
  523.6 3.2 stack.19
  526.8 2.2 pad_maximum_fusion
  529.0 4.2 copy.48
  533.2 20.1 %all-to-all-done.3 = bf16[2,16,20,2048]{3,0,2,1:T(2,128)(2,1)S(1)} async-done(((bf16[2,16,20,2048]{3,0,2,1:T(2,128)(2,1)}), bf16[2,16,20,2048]{3,0,2,1:T(2,128)(2,1)S(1)}, u32[]{:S(2)}, u32[]{:S(2)}) %all-to-all-start.3) | async-done | bytes 2621472 | tf_op jit(solution)/shard_map/all_to_all | solution.py:90
  553.3 5.1 all-to-all-start.1
  559.0 2.9 copy.57
  561.9 3.7 reshape.125
  565.6 3.3 gather_fusion.4
  568.9 5.5 reshape.128
  574.4 19.7 %all-to-all-done.1 = bf16[2,16,20,2048]{3,0,2,1:T(2,128)(2,1)} async-done(((bf16[2,16,20,2048]{3,0,2,1:T(2,128)(2,1)}), bf16[2,16,20,2048]{3,0,2,1:T(2,128)(2,1)}, u32[]{:S(2)}, u32[]{:S(2)}) %all-to-all-start.1) | async-done | bytes 2621472 | tf_op jit(solution)/shard_map/all_to_all | solution.py:89
  594.1 4.6 copy.49
  598.7 3.6 reshape.122
  602.4 3.3 gather_fusion.1
  605.7 5.6 reshape.126
  611.4 10.0 %multiply_reduce_fusion = bf16[256,2048]{1,0:T(8,128)(2,1)} fusion(f32[256,2,2048]{2,1,0:T(2,128)} %reshape.126, f32[256,2]{1,0:T(8,128)S(1)} %copy.43), kind=kLoop, calls=%fused_computation.17 | loop fusion | flops 1572864 | bytes 5244928 | tf_op jit(solution)/shard_map/reduce_sum | solution.py:97
  621.4 11.1 %select_reduce_fusion = bf16[256,2048]{1,0:T(8,128)(2,1)} fusion(f32[256,2,2048]{2,1,0:T(2,128)S(1)} %copy-done.3, pred[256,2]{1,0:T(8,128)(4,1)S(1)} %copy.51), kind=kLoop, calls=%fused_computation.16 | loop fusion | flops 1572864 | bytes 5243392 | tf_op jit(solution)/shard_map/reduce_sum | solution.py:99
  632.5 65.3 %all-reduce.5.cloned.1.call-done = (bf16[256,1536]{1,0:T(8,128)(2,1)}, bf16[96,2048]{1,0:T(8,128)(2,1)}) async-done(((bf16[256,1536]{1,0:T(8,128)(2,1)}, bf16[96,2048]{1,0:T(8,128)(2,1)}), (bf16[256,1536]{1,0:T(8,128)(2,1)}, bf16[96,2048]{1,0:T(8,128)(2,1)})) %all-reduce.5.cloned.1.call-update) | async-done | bytes 1179664 | tf_op jit(solution)/shard_map/psum | solution.py:114
  697.8 2.1 add_bitcast_fusion.1
  699.9 100.2 %reduce-scatter.5.cloned.1.call-done = bf16[256,1536]{1,0:T(8,128)(2,1)} async-done(((bf16[2048,1536]{1,0:T(8,128)(2,1)}), bf16[256,1536]{1,0:T(8,128)(2,1)}) %reduce-scatter.5.cloned.1.call-update) | async-done | bytes 786448 | tf_op jit(solution)/shard_map/reduce_scatter | solution.py:104
  800.1 2.7 add_bitcast_fusion
  (69 shorter events, 4.7 us)
Async XLA Ops:
  7.2 13.6 %copy-start = (bf16[256,2048]{1,0:T(8,128)(2,1)S(1)}, bf16[256,2048]{1,0:T(8,128)(2,1)}, u32[]{:S(2)}) copy-start(bf16[256,2048]{1,0:T(8,128)(2,1)} %param.8) | copy-start | bytes 3145732
  7.2 282.5 %all-reduce.7.cloned.1.call-start = ((), (), s32[]{:S(2)}) async-start(), calls=%async_computation.13 | async-start | bytes 18874368 | tf_op jit(solution)/shard_map/psum | solution.py:9
  10.0 6.0 copy-start.6
  36.1 5.3 copy-start.10
  36.1 5.5 copy-start.2
  36.1 66.5 %all-to-all-start = ((bf16[2,16,20,2048]{3,0,2,1:T(2,128)(2,1)}), bf16[2,16,20,2048]{3,0,2,1:T(2,128)(2,1)}, u32[]{:S(2)}, u32[]{:S(2)}) async-start(bf16[2,16,20,2048]{3,0,2,1:T(2,128)(2,1)} %copy.47), calls=%async_computation | async-start | bytes 5242880 | tf_op jit(solution)/shard_map/all_to_all | solution.py:69
  102.5 65.6 %all-to-all-start.2 = ((bf16[2,16,20,2048]{3,0,2,1:T(2,128)(2,1)}), bf16[2,16,20,2048]{3,0,2,1:T(2,128)(2,1)S(1)}, u32[]{:S(2)}, u32[]{:S(2)}) async-start(bf16[2,16,20,2048]{3,0,2,1:T(2,128)(2,1)} %copy.55), calls=%async_computation.2 | async-start | bytes 5242880 | tf_op jit(solution)/shard_map/all_to_all | solution.py:70
  106.8 272.6 %reduce-scatter.11.cloned.1.call-start = ((), (), s32[]{:S(2)}) async-start(), calls=%async_computation.11 | async-start | bytes 3538944 | tf_op jit(solution)/shard_map/reduce_scatter | solution.py:109
  183.1 106.6 %copy-start.8 = (bf16[320,2048]{1,0:T(8,128)(2,1)S(1)}, bf16[320,2048]{1,0:T(8,128)(2,1)}, u32[]{:S(2)}) copy-start(bf16[320,2048]{1,0:T(8,128)(2,1)} %reshape_squeeze.13) | copy-start | bytes 3932164
  289.7 5.1 copy-start.11
  297.4 3.5 copy-start.12
  300.9 1.0 copy-start.16
  300.9 1.2 copy-start.17
  300.9 180.2 %reduce-scatter.7.cloned.1.call-start = ((), (), s32[]{:S(2)}) async-start(), calls=%async_computation.9 | async-start | bytes 7077888 | tf_op jit(solution)/shard_map/reduce_scatter | solution.py:106
  307.5 1.4 copy-start.5
  307.6 2.6 copy-start.4
  307.6 325.0 %reduce-scatter.9.cloned.1.call-start = ((), (), s32[]{:S(2)}) async-start(), calls=%async_computation.10 | async-start | bytes 3538944 | tf_op jit(solution)/shard_map/reduce_scatter | solution.py:105
  310.5 5.2 copy-start.7
  310.5 5.2 copy-start.9
  317.2 0.8 copy-start.14
  321.6 376.2 %all-reduce.5.cloned.1.call-start = ((), (), s32[]{:S(2)}) async-start(), calls=%async_computation.12 | async-start | bytes 2359296 | tf_op jit(solution)/shard_map/psum | solution.py:114
  481.1 319.0 %reduce-scatter.5.cloned.1.call-start = ((), (), s32[]{:S(2)}) async-start(), calls=%async_computation.8 | async-start | bytes 7077888 | tf_op jit(solution)/shard_map/reduce_scatter | solution.py:104
  505.9 6.2 copy-start.15
  505.9 47.4 %all-to-all-start.3 = ((bf16[2,16,20,2048]{3,0,2,1:T(2,128)(2,1)}), bf16[2,16,20,2048]{3,0,2,1:T(2,128)(2,1)S(1)}, u32[]{:S(2)}, u32[]{:S(2)}) async-start(bf16[2,16,20,2048]{3,0,2,1:T(2,128)(2,1)} %copy.56), calls=%async_computation.3 | async-start | bytes 5242880 | tf_op jit(solution)/shard_map/all_to_all | solution.py:90
  516.2 3.3 copy-start.13
  553.3 40.8 %all-to-all-start.1 = ((bf16[2,16,20,2048]{3,0,2,1:T(2,128)(2,1)}), bf16[2,16,20,2048]{3,0,2,1:T(2,128)(2,1)}, u32[]{:S(2)}, u32[]{:S(2)}) async-start(bf16[2,16,20,2048]{3,0,2,1:T(2,128)(2,1)} %copy.48), calls=%async_computation.1 | async-start | bytes 5242880 | tf_op jit(solution)/shard_map/all_to_all | solution.py:89
  611.3 10.1 %copy-start.3 = (f32[256,2,2048]{2,1,0:T(2,128)S(1)}, f32[256,2,2048]{2,1,0:T(2,128)}, u32[]{:S(2)}) copy-start(f32[256,2,2048]{2,1,0:T(2,128)} %reshape.128) | copy-start | bytes 12582916
  621.4 181.5 %copy-start.1 = (bf16[256,2048]{1,0:T(8,128)(2,1)S(1)}, bf16[256,2048]{1,0:T(8,128)(2,1)}, u32[]{:S(2)}) copy-start(bf16[256,2048]{1,0:T(8,128)(2,1)} %param.8) | copy-start | bytes 3145732
Sparse Core Ops, SparseCore 0:
  18.0 271.6 all-reduce.6
  301.0 78.4 reduce-scatter.10
  383.3 97.7 reduce-scatter.6
  484.8 89.9 reduce-scatter.8
  577.1 120.6 all-reduce.4
  701.5 98.5 reduce-scatter.4
where the time goes:
time: 819 us; the launch traced here: 810 us
  waiting for transfers between devices  548 us (67%)
  local copies, waits for them, and re-layouts  124 us (15%)
  matrix products  52.3 us (6%)
  other arithmetic  48 us (6%)
  starting transfers between devices  22 us (3%)
  between operations  15.6 us (2%)
    psum x1, waiting for transfers between devices, from_root(): return lax.psum(block, axis)  104 us
    reduce_scatter x1, waiting for transfers between devices, shards(): lax.psum_scatter(replica_part[2], 'dp', scatter_dimension=0, tiled=True)  102 us
    reduce_scatter x1, waiting for transfers between devices, shards(): lax.psum_scatter(home_part[2], 'dp', scatter_dimension=0, tiled=True)  100 us
    psum x1, waiting for transfers between devices, shards(): lax.psum(summed[2].astype(jnp.bfloat16), 'expert').astype(jnp.float32)  65.3 us
    reduce_scatter x1, waiting for transfers between devices, shards(): lax.psum_scatter(replica_part[3], 'dp', scatter_dimension=0, tiled=True)  57.8 us
    all_to_all x1, waiting for transfers between devices, shards(): lax.all_to_all(g_rows, 'expert', split_axis=1, concat_axis=1, tiled=True)  43.3 us
    all_to_all x1, waiting for transfers between devices, shards(): lax.all_to_all(x_rows, 'expert', split_axis=1, concat_axis=1, tiled=True)  36.2 us
    all_to_all x1, waiting for transfers between devices, shards(): lax.all_to_all(back_stack, 'expert', split_axis=1, concat_axis=1, tiled=T...  20.1 us
  transfers between devices with their start and end apart: 10, of which 9 were waited for; matrix products, arithmetic and copies ran while one was open for 24% of the time, Pallas kernels for 0%

commit v1 on v0

v1 whole, which is shorter than its diff:
```python
import functools

import jax
import jax.numpy as jnp
from jax import lax
from jax.experimental import pallas as pl
from jax.experimental.pallas import tpu as pltpu
from jax.sharding import PartitionSpec as P

AXES = ("dp", "expert")
BF = jnp.bfloat16
F32 = jnp.float32


def hop(x, dh=0, dy=0, dz=0, dl=0, dc=0):
    pairs = []
    for i in range(128):
        dp, ex = divmod(i, 16)
        h, y = divmod(dp, 4)
        z, l, c = ex // 4, (ex // 2) % 2, ex % 2
        j_dp = ((h + dh) % 2) * 4 + (y + dy) % 4
        j_ex = ((z + dz) % 4) * 4 + ((l + dl) % 2) * 2 + (c + dc) % 2
        pairs.append((i, j_dp * 16 + j_ex))
    return lax.ppermute(x, AXES, pairs)


def dot(a, b, ca=1, cb=0):
    return lax.dot_general(a, b, (((ca,), (cb,)), ((), ())), preferred_element_type=F32)


def total(*parts, dtype=BF):
    out = parts[0].astype(F32)
    for part in parts[1:]:
        out = out + part.astype(F32)
    return out.astype(dtype)


VMEM = pl.BlockSpec(memory_space=pltpu.VMEM)
SMEM = pl.BlockSpec(memory_space=pltpu.SMEM)
AFTER = pl.BlockSpec(memory_space=pl.ANY)


def call(kernel, name, outs, args, scratch=(), in_specs=None, out_specs=None):
    return pl.pallas_call(
        kernel,
        out_shape=outs,
        in_specs=in_specs or [VMEM] * len(args),
        out_specs=out_specs or (VMEM,) * len(outs),
        scratch_shapes=list(scratch),
        compiler_params=pltpu.CompilerParams(vmem_limit_bytes=48 * 2**20),
        cost_estimate=pl.CostEstimate(flops=10**6, bytes_accessed=10**5, transcendentals=0),
        name=name,
    )(*args)


def shape(*dims, dtype=BF):
    return jax.ShapeDtypeStruct(dims, dtype)


def sum_kernel(count, *refs):
    out = refs[0][...].astype(F32)
    for ref in refs[1:count]:
        out = out + ref[...].astype(F32)
    refs[-1][...] = out.astype(BF)


def stack_kernel(*refs):
    for k in range(4):
        refs[-1][k] = refs[k][...]


def sum_after(parts, after, name):
    return call(
        functools.partial(sum_kernel, len(parts)),
        name,
        (shape(*parts[0].shape),),
        (*parts, *after),
        in_specs=[VMEM] * len(parts) + [AFTER] * len(after),
    )[0]


def select(pos, gates, rows, shift):
    row = lax.broadcasted_iota(jnp.int32, (rows, 256), 0) + shift
    m0 = row == pos[0:1, :]
    m1 = row == pos[1:2, :]
    pick = jnp.where(m0 | m1, 1.0, 0.0).astype(BF)
    gate = jnp.where(m0, gates[0:1, :], 0.0) + jnp.where(m1, gates[1:2, :], 0.0)
    return pick, jnp.sum(gate, axis=1, keepdims=True)


def route_kernel(
    here_ref, ids_ref, dest_ref, slot_ref, gate_ref, tok_ref, cot_ref, in_ref, out_ref, pick_ref,
    parts_ref, hot_ref, pos_ref, top_ref,
):
    l, c = here_ref[3], here_ref[4]
    pick = pick_ref[...]
    gate_w = dot(pick, in_ref[:, :768], 0, 1).astype(BF)
    up_w = dot(pick, in_ref[:, 768:], 0, 1).astype(BF)
    down_w = dot(pick, out_ref[...], 0, 0).astype(BF)
    for q in range(4):
        units = slice(192 * q, 192 * q + 192)
        rows = jnp.concatenate([gate_w[units], up_w[units], down_w[units]], axis=0)
        parts_ref[(q // 2 + c) % 2, (q % 2 + l) % 2] = rows

    ids, dest, slot = ids_ref[...], dest_ref[...], slot_ref[...]
    served = slot >= 0
    replica = served & (ids != dest)
    top_ref[0, 0] = jnp.max(jnp.where(replica, ids, -1))
    order = jnp.zeros_like(dest)
    for e in range(15):
        found = jnp.where(replica & (dest == e), 1, 0)
        found = jnp.max(jnp.max(found, axis=1, keepdims=True), axis=0, keepdims=True)
        order = order + jnp.where(dest > e, found, 0)
    pos = jnp.where(replica, 640 + order * 20 + slot, dest * 40 + slot)
    pos = jnp.where(served, pos, -1000)
    pos_ref[...] = pos
    hot_x, hot_gate = select(pos, gate_ref[...], 80, 640)
    for j in range(4):
        cols = pl.ds(j * 512, 512)
        hot_ref[0:80, cols] = dot(hot_x, tok_ref[:, cols]).astype(BF)
        hot_ref[80:160, cols] = (hot_gate * dot(hot_x, cot_ref[:, cols])).astype(BF)


def route(here, tables, rows, weights, pick):
    i32 = jnp.int32
    whole = lambda *dims: pl.BlockSpec(dims, lambda i, d: (0,) * len(dims))
    return pl.pallas_call(
        route_kernel,
        out_shape=(
            shape(2, 2, 576, 256),
            shape(160, 2048),
            shape(2, 256, dtype=i32),
            shape(1, 1, dtype=i32),
        ),
        grid_spec=pltpu.PrefetchScalarGridSpec(
            num_scalar_prefetch=1,
            grid=(1,),
            in_specs=[whole(2, 256)] * 4
            + [whole(256, 2048)] * 2
            + [
                pl.BlockSpec((256, 1536), lambda i, d: (d[0] * 4 + d[1], 0)),
                pl.BlockSpec((768, 256), lambda i, d: (0, d[0] * 4 + d[1])),
                whole(768, 768),
            ],
            out_specs=(whole(2, 2, 576, 256), whole(160, 2048), whole(2, 256), SMEM),
        ),
        compiler_params=pltpu.CompilerParams(vmem_limit_bytes=40 * 2**20),
        cost_estimate=pl.CostEstimate(flops=10**6, bytes_accessed=10**5, transcendentals=0),
        name="route",
    )(here, *tables, *rows, *weights, pick)


def pack_kernel(pos_ref, gate_ref, tok_ref, cot_ref, *refs):
    send_ref = refs[-1]
    home_x, _ = select(pos_ref[...], gate_ref[...], 640, 0)
    home_g, home_gate = select(pos_ref[...], gate_ref[...], 640, -20)
    for j in range(4):
        cols = pl.ds(j * 512, 512)
        rows = dot(home_x, tok_ref[:, cols]) + home_gate * dot(home_g, cot_ref[:, cols])
        send_ref[:, cols] = rows.astype(BF)


def unpack_kernel(pos_ref, gate_ref, ret_ref, hot_a_ref, hot_b_ref, mixed_ref, grad_ref):
    def select(k, rows, shift):
        row = lax.broadcasted_iota(jnp.int32, (rows, 256), 0) + shift
        return jnp.where(row == pos_ref[k : k + 1, :], 1.0, 0.0).astype(BF)

    out0, out1 = select(0, 640, 0), select(1, 640, 0)
    back = select(0, 640, -20) + select(1, 640, -20)
    hot0, hot1 = select(0, 80, 640), select(1, 80, 640)
    hot_back = hot0 + hot1
    gate0, gate1 = gate_ref[:, 0:1], gate_ref[:, 1:2]
    for j in range(4):
        cols = pl.ds(j * 512, 512)
        ret = ret_ref[:, cols]
        hot = (hot_a_ref[0, :, cols].astype(F32) + hot_b_ref[:, cols].astype(F32)).astype(BF)
        first = dot(out0, ret, 0, 0) + dot(hot0, hot[:80], 0, 0)
        second = dot(out1, ret, 0, 0) + dot(hot1, hot[:80], 0, 0)
        mixed_ref[:, cols] = (gate0 * first + gate1 * second).astype(BF)
        grads = dot(back, ret, 0, 0) + dot(hot_back, hot[80:], 0, 0)
        grad_ref[:, cols] = grads.astype(BF)


def swiglu(gate, up, grad_active):
    sig = 1.0 / (1.0 + jnp.exp(-gate))
    silu = gate * sig
    active = silu * up
    grad_gate = grad_active * up * sig * (1.0 + gate * (1.0 - sig))
    return active.astype(BF), grad_gate.astype(BF), (grad_active * silu).astype(BF)


def home_kernel(
    recv_ref, pick_x_ref, pick_g_ref, in_ref, out_ref, after_ref, act_ref, gh_ref, x_ref, g_ref
):
    for k in range(4):
        recv = recv_ref[160 * k : 160 * k + 160, :]
        x_ref[80 * k : 80 * k + 80, :] = dot(pick_x_ref[...], recv).astype(BF)
        g_ref[80 * k : 80 * k + 80, :] = dot(pick_g_ref[...], recv).astype(BF)

    def unit_tile(n, carry):
        lo = pl.ds(pl.multiple_of(n * 256, 256), 256)
        hi = pl.ds(pl.multiple_of(768 + n * 256, 256), 256)
        gate = dot(x_ref[...], in_ref[:, lo])
        up = dot(x_ref[...], in_ref[:, hi])
        grad_active = dot(g_ref[...], out_ref[lo, :], 1, 1)
        active, grad_gate, grad_up = swiglu(gate, up, grad_active)
        act_ref[:, lo] = active
        gh_ref[:, lo] = grad_gate
        gh_ref[:, hi] = grad_up
        return carry

    lax.fori_loop(0, 3, unit_tile, 0)


def grads_kernel(here_ref, act_ref, gh_ref, x_ref, g_ref, *refs):
    own_ref, up_ref, dn_ref, to_up_ref, to_dn_ref, out_own_ref, out_far_ref = refs[-7:]
    h, y = here_ref[0], here_ref[1]
    pieces = (
        (own_ref, own_ref),
        (up_ref, to_up_ref.at[1]),
        (to_up_ref.at[0], to_dn_ref.at[1]),
        (to_dn_ref.at[0], dn_ref),
    )

    def side(r, carry):
        hh = h + r - 2 * h * r
        for s, (first, second) in enumerate(pieces):
            block = hh * 4 + (y + s) % 4
            rows = x_ref[:, pl.ds(pl.multiple_of(block * 256, 256), 256)]
            grad = dot(rows, gh_ref[...], 0, 0).astype(BF)
            if s == 0:
                own_ref[r] = grad
            else:
                first[r] = grad[:, :768]
                second[r] = grad[:, 768:]
        return carry

    lax.fori_loop(0, 2, side, 0)
    for r, dst in enumerate((out_own_ref, out_far_ref)):
        hh = h if r == 0 else 1 - h
        units = act_ref[:, pl.ds(pl.multiple_of(hh * 384, 128), 384)]
        for j in range(4):
            cols = pl.ds(j * 512, 512)
            grad = dot(units, g_ref[:, cols], 0, 0).astype(BF)
            for k in range(4):
                dst[(k + 4 - y) % 4, :, cols] = grad[96 * k : 96 * k + 96]


def result_kernel(
    act_ref, gh_ref, pick_x_ref, pick_g_ref, in_ref, out_ref, after_ref, res_ref
):
    def tile(j, carry):
        cols = pl.ds(pl.multiple_of(j * 512, 512), 512)
        out = dot(act_ref[...], out_ref[:, cols]).astype(BF)
        back = dot(gh_ref[...], in_ref[cols, :], 1, 1).astype(BF)
        both_rows = dot(pick_x_ref[...], out, 0, 0) + dot(pick_g_ref[...], back, 0, 0)
        res_ref[:, cols] = both_rows.astype(BF)
        return carry

    lax.fori_loop(0, 4, tile, 0)


def hot_kernel(
    here_ref, own_ref, near_ref, far_ref, w0_ref, w1_ref, w2_ref, w3_ref, after_ref,
    mine_ref, theirs_ref, p0_ref, p1_ref, p2_ref, p3_ref, x_ref, g_ref, t_ref,
):
    h, y, z = here_ref[0], here_ref[1], here_ref[2]
    for k, rows in enumerate((own_ref, near_ref, far_ref.at[0], far_ref.at[1])):
        x_ref[80 * k : 80 * k + 80, :] = rows[0:80, :]
        g_ref[80 * k : 80 * k + 80, :] = rows[80:160, :]
    blocks = []
    for s, w in enumerate((w0_ref, w1_ref, w2_ref, w3_ref)):
        for r in range(2):
            d = (h if r == 0 else 1 - h) * 4 + (y + 4 - s) % 4
            blocks.append((d, pl.ds(pl.multiple_of(d * 256, 256), 256), w.at[r]))
    hidden = jnp.zeros((320, 384), F32)
    grad_active = jnp.zeros((320, 192), F32)
    for d, cols, w in blocks:
        hidden = hidden + dot(x_ref[:, cols], w[0:384, :], 1, 1)
        grad_active = grad_active + dot(g_ref[:, cols], w[384:576, :], 1, 1)
    active, grad_gate, grad_up = swiglu(hidden[:, :192], hidden[:, 192:], grad_active)
    grad_hidden = jnp.concatenate([grad_gate, grad_up], axis=1)
    for b in range(8):
        down = dot(active, g_ref[:, 256 * b : 256 * b + 256], 0, 0).astype(BF)
        for d in range(8):
            t_ref[d, 384 + 24 * b : 408 + 24 * b, :] = down[24 * d : 24 * d + 24, :]
    for d, cols, w in blocks:
        t_ref[d, 0:384, :] = dot(grad_hidden, x_ref[:, cols], 0, 0).astype(BF)
        out = dot(active, w[384:576, :]).astype(BF)
        back = dot(grad_hidden, w[0:384, :]).astype(BF)
        for k, dst in enumerate((mine_ref.at[0], mine_ref.at[1], theirs_ref.at[0], theirs_ref.at[1])):
            dst[0:80, cols] = out[80 * k : 80 * k + 80]
            dst[80:160, cols] = back[80 * k : 80 * k + 80]
    for n, p in enumerate((p0_ref, p1_ref, p2_ref, p3_ref)):
        rows = pl.ds(pl.multiple_of((z + n) % 4 * 144, 16), 144)
        for s in range(4):
            for r in range(2):
                p[r, s] = t_ref[(h if r == 0 else 1 - h) * 4 + (y + s) % 4, rows, :]


def finish_kernel(
    here_ref, spare_ref, more_ref, pick_ref, in_ref, in_got_ref, d0_ref, d1_ref, d2_ref, d3_ref,
    after_ref, out_in_ref, out_down_ref, t_ref,
):
    z, l, c = here_ref[2], here_ref[3], here_ref[4]
    flag = here_ref[5].astype(F32)
    for rc, src in enumerate((spare_ref, more_ref)):
        for rl in range(2):
            q = 2 * (c if rc == 0 else 1 - c) + (l if rl == 0 else 1 - l)
            for s in range(4):
                rows = pl.ds(pl.multiple_of((z + 4 - s) % 4 * 144, 16), 144)
                t_ref[q, rows, :] = src[rl, s]
    pick = pick_ref[...]
    for part in range(2):
        rows = jnp.concatenate(
            [t_ref[q, 192 * part : 192 * part + 192, :] for q in range(4)], axis=0
        )
        cols = slice(768 * part, 768 * part + 768)
        home = in_ref[:, cols].astype(F32) + in_got_ref[:, cols].astype(F32)
        out_in_ref[:, cols] = home + flag * dot(rows, pick, 0, 1)
    for q in range(4):
        for b in range(8):
            rows, cols = slice(24 * q, 24 * q + 24), slice(256 * b, 256 * b + 256)
            home = d0_ref[rows, cols].astype(F32) + d1_ref[rows, cols].astype(F32)
            home = home + d2_ref[rows, cols].astype(F32) + d3_ref[rows, cols].astype(F32)
            piece = t_ref[q, 384 + 24 * b : 408 + 24 * b, :].astype(F32)
            out_down_ref[rows, cols] = home + flag * piece


def shards(tokens, cotangent, route_gates, w_gate_up, w_down, expert_ids, dest_ranks, slot_ids):
    dp, ex = lax.axis_index("dp"), lax.axis_index("expert")
    h, y = dp // 4, dp % 4
    z, l, c = ex // 4, (ex // 2) % 2, ex % 2
    w_in, w_out = w_gate_up[0], w_down[0]
    i32 = jnp.int32

    unit = jnp.arange(768, dtype=i32)
    place = unit % 192 // 24 * 96 + unit // 192 * 24 + unit % 24
    pick = (unit[:, None] == place[None, :]).astype(BF)
    here = jnp.stack([h, y, z, l, c]).astype(i32)
    tables = (expert_ids.T, dest_ranks.T, slot_ids.T, route_gates.T)
    parts, hot_rows, pos, hot = route(here, tables, (tokens, cotangent), (w_in, w_out), pick)
    hot = hot[0, 0]
    hz, hl, hc = hot // 4, (hot // 2) % 2, hot % 2
    here = jnp.concatenate([here, (ex == hot).astype(i32).reshape(1)])

    got = hop(parts[1], dc=1)
    piece = jnp.where(c == hc, parts[0], got)
    near_w = hop(piece[1], dl=1)
    piece = jnp.where(l == hl, piece[0], near_w)
    got = [hop(piece, dz=s) for s in (1, 2, 3)]
    away = (z - hz) % 4
    piece = jnp.where(
        away == 0, piece, jnp.where(away == 1, got[0], jnp.where(away == 2, got[1], got[2]))
    )
    hot_rows = sum_after([hot_rows], [near_w], "keep_rows")
    near_rows = hop(hot_rows, dl=1)
    far_rows = hop(jnp.stack([hot_rows, near_rows]), dc=1)
    piece = jnp.stack([piece, hop(piece, dh=1)])

    (send,) = call(
        pack_kernel,
        "pack_rows",
        (shape(640, 2048),),
        (pos, tables[3], tokens, cotangent, piece, near_rows),
        in_specs=[VMEM] * 4 + [AFTER] * 2,
    )
    recv = lax.all_to_all(send, "expert", split_axis=0, concat_axis=0, tiled=True)
    hot_w = [piece] + [hop(piece, dy=s) for s in (1, 2, 3)]

    mine, theirs, *spares = call(
        hot_kernel,
        "hot_expert",
        (shape(2, 160, 2048), shape(2, 160, 2048)) + (shape(2, 4, 144, 256),) * 4,
        (here, hot_rows, near_rows, far_rows, *hot_w, recv),
        scratch=(
            pltpu.VMEM((320, 2048), BF),
            pltpu.VMEM((320, 2048), BF),
            pltpu.VMEM((8, 576, 256), BF),
        ),
        in_specs=[SMEM] + [VMEM] * 7 + [AFTER],
    )
    mine = total(mine, hop(theirs, dc=1))
    near_part = hop(mine[1], dl=1)

    def picks(rows, stride):
        compact = jnp.arange(rows, dtype=i32)
        spread = compact // 20 * stride + compact % 20
        row = jnp.arange(rows // 20 * stride, dtype=i32)
        return [(spread[:, None] + shift == row).astype(BF) for shift in (0, 20)]

    pick_x, pick_g = picks(80, 40)
    back_x, back_g = picks(320, 40)
    active, grad_hidden, rows_x, rows_g = call(
        home_kernel,
        "home_hidden",
        (shape(320, 768), shape(320, 1536), shape(320, 2048), shape(320, 2048)),
        (recv, pick_x, pick_g, w_in, w_out, spares[0]),
        in_specs=[VMEM] * 5 + [AFTER],
    )
    (result,) = call(
        result_kernel,
        "home_rows",
        (shape(640, 2048),),
        (active, grad_hidden, back_x, back_g, w_in, w_out, near_part),
        in_specs=[VMEM] * 6 + [AFTER],
    )
    returned = lax.all_to_all(result, "expert", split_axis=0, concat_axis=0, tiled=True)
    spare = sum_after(
        [spares[0]] + [hop(spares[s], dz=s) for s in (1, 2, 3)], [result], "sum_z"
    )
    spare = total(spare[0], hop(spare[1], dh=1))
    spare = total(spare[0], *[hop(spare[s], dy=s) for s in (1, 2, 3)])
    half = shape(2, 256, 768)
    in_own, up_a, dn_b, to_up, to_dn, out_own, out_far = call(
        grads_kernel,
        "home_grads",
        (shape(2, 256, 1536),) + (half,) * 2 + (shape(2, 2, 256, 768),) * 2 + (shape(4, 96, 2048),) * 2,
        (here, active, grad_hidden, rows_x, rows_g, spare),
        in_specs=[SMEM] + [VMEM] * 4 + [AFTER],
    )

    from_dn, from_up = hop(to_up, dy=1), hop(to_dn, dy=3)
    out_far = hop(out_far, dh=1)
    mixed, token_grad = call(
        unpack_kernel,
        "unpack_rows",
        (shape(256, 2048), shape(256, 2048)),
        (pos, route_gates, returned, mine, near_part),
    )

    (spare,) = call(
        stack_kernel,
        "stack_z",
        (shape(4, 144, 256),),
        (spare, *[hop(spare, dz=s) for s in (1, 2, 3)]),
        in_specs=[VMEM] * 4,
    )
    spare = jnp.stack([spare, hop(spare, dl=1)])
    more = hop(spare, dc=1)
    up_a = hop(sum_after([up_a, from_dn[0]], [returned], "sum_up"), dy=1)
    dn_b = hop(sum_after([dn_b, from_up[1]], [returned], "sum_down"), dy=3)
    up_b, dn_a = from_dn[1], from_up[0]
    in_sum = total(
        in_own, jnp.concatenate([up_a, up_b], axis=2), jnp.concatenate([dn_a, dn_b], axis=2)
    )
    in_got = hop(in_sum[1], dh=1)
    out_sum = total(out_own, out_far)
    out_parts = [out_sum[0]] + [hop(out_sum[s], dy=s) for s in (1, 2, 3)]

    grad_gate_up, grad_down = call(
        finish_kernel,
        "finish_grads",
        (shape(256, 1536, dtype=F32), shape(96, 2048, dtype=F32)),
        (here, spare, more, pick, in_sum[0], in_got, *out_parts, mixed),
        scratch=(pltpu.VMEM((4, 576, 256), BF),),
        in_specs=[SMEM] + [VMEM] * 9 + [AFTER],
    )
    return mixed, token_grad, grad_gate_up[None], grad_down[None]


def solution(mesh):
    rows = P(AXES, None)
    weights = P("expert", None, None)
    grads = P("expert", "dp", None)
    return jax.shard_map(
        shards,
        mesh=mesh,
        in_specs=(rows, rows, rows, weights, weights, rows, rows, rows),
        out_specs=(rows, rows, grads, grads),
        check_vma=False,
    )
```

time: 819 us -> 261 us (0.32)
  waiting for transfers between devices: 548 us -> 109 us
  local copies, waits for them, and re-layouts: 124 us -> 24.9 us
  Pallas kernels: 0 us -> 52.7 us
  matrix products: 52.3 us -> 0 us
  other arithmetic: 48 us -> 12.5 us
  starting transfers between devices: 22 us -> 55.8 us
  between operations: 15.6 us -> 4.75 us
    reduce_scatter x4 -> x0, waiting for transfers between devices: 260 us -> none  [the longest x1 102 us: shards(): lax.psum_scatter(replica_part[2], 'dp', scatter_dimension=0, tiled=True)]
    psum x2 -> x0, waiting for transfers between devices: 169 us -> none  [the longest x1 104 us: from_root(): return lax.psum(block, axis)]
    all_to_all x4 -> x2, waiting for transfers between devices: 119 us -> 1.38 us  [the longest x1 1.38 us: shards(): lax.all_to_all(send, 'expert', split_axis=0, concat_axis=0, tiled=True)]
    ppermute x0 -> x34, waiting for transfers between devices: none -> 108 us  [hop(): return lax.ppermute(x, AXES, pairs)]
    pallas_call x0 -> x13, Pallas kernels: none -> 52.7 us  [the longest x12 49.7 us: call(): pl.pallas_call(kernel, out_shape=outs, in_specs=in_specs or [VMEM] * len(...]
    dot_general x12 -> x0, matrix products: 52.3 us -> none  [the longest x2 11.6 us: swiglu_pass(): lax.dot_general(grad_hidden, weight_in, (((1,), (1,)), ((), ())), preferr...]
    ppermute x0 -> x34, starting transfers between devices: none -> 44.2 us  [hop(): return lax.ppermute(x, AXES, pairs)]
    slice x2 -> x0, local copies, waits for them, and re-layouts: 29.5 us -> none  [the longest x1 15 us: shards(): recv_cots[0].reshape(-1, model_width)]
  transfers between devices with their start and end apart: 10 -> 36, of which waited for: 9 -> 18; matrix products, arithmetic and copies ran while one was open for 24% -> 6% of each run, Pallas kernels for 0% -> 13%
where the time goes in v1:
time: 261 us; the launch traced here: 260 us
  waiting for transfers between devices  109 us (42%)
  starting transfers between devices  55.8 us (21%)
  Pallas kernels  52.7 us (20%)
  local copies, waits for them, and re-layouts  24.9 us (10%)
  other arithmetic  12.5 us (5%)
  between operations  4.75 us (2%)
    ppermute x34, waiting for transfers between devices, hop(): return lax.ppermute(x, AXES, pairs)  108 us
    pallas_call x12, Pallas kernels, call(): pl.pallas_call(kernel, out_shape=outs, in_specs=in_specs or [VMEM] * len(...  49.7 us
    ppermute x34, starting transfers between devices, hop(): return lax.ppermute(x, AXES, pairs)  44.2 us
    unnamed x71, local copies, waits for them, and re-layouts  19.1 us
    all_to_all x1, starting transfers between devices, shards(): lax.all_to_all(send, 'expert', split_axis=0, concat_axis=0, tiled=True)  6.12 us
    convert_element_type x5, other arithmetic, total(): return out.astype(dtype)  5.65 us
    all_to_all x1, starting transfers between devices, shards(): lax.all_to_all(result, 'expert', split_axis=0, concat_axis=0, tiled=True)  5.54 us
  transfers between devices with their start and end apart: 36, of which 18 were waited for; matrix products, arithmetic and copies ran while one was open for 6% of the time, Pallas kernels for 13%

profile of v1, /device:TPU:1, one launch (start us, length us, event | category | flops | bytes accessed | tf_op | source)
XLA Modules:
  0.0 259.9 jit_solution(17980378318953195071)
XLA Ops:
  1.9 2.8 %copy-done = bf16[1,2048,1536]{2,1,0:T(8,128)(2,1)S(1)} copy-done((bf16[1,2048,1536]{2,1,0:T(8,128)(2,1)S(1)}, bf16[1,2048,1536]{2,1,0:T(8,128)(2,1)}, u32[]{:S(2)}) %copy-start) | copy-done | bytes 6291480
  4.6 1.9 copy-done.1
  6.5 1.2 copy-done.7
  10.5 3.0 %route.1 = (bf16[2,2,576,256]{3,2,1,0:T(8,128)(2,1)}, bf16[160,2048]{1,0:T(8,128)(2,1)S(1)}, s32[2,256]{1,0:T(2,128)S(1)}, s32[1,1]{1,0:T(1,128)}) custom-call(s32[5]{0:T(128)S(1)} %stack.50.here_ref, s32[2,256]{1,0:T(2,128)S(1)} %bitcast.89, s32[2,256]{1,0:T(2,128)S(1)} %bitcast.90, s32[2,256]{1,0:T(2,128)S(1)} %bitcast.91, f32[2,256]{1,0:T(2,128)S(1)} %bitcast.87, ...), custom_call_target="tpu_custom_call" | custom-call | flops 1000000 | bytes 100000 | tf_op jit(solution)/shard_map/route/pallas_call | solution.py:127
  13.5 1.1 slice_bitcast_fusion.7
  14.6 1.5 collective-permute-start
  18.2 1.1 bitcast_select_fusion
  19.4 1.4 collective-permute-start.1
  21.5 6.6 %collective-permute-done.1.refs_1_ = bf16[576,256]{1,0:T(8,128)(2,1)S(1)} collective-permute-done((bf16[576,256]{1,0:T(8,128)(2,1)S(1)}, bf16[576,256]{1,0:T(8,128)(2,1)S(1)}, u32[]{:S(2)}, u32[]{:S(2)}) %collective-permute-start.1) | collective-permute-done | bytes 294944 | tf_op jit(solution)/shard_map/ppermute | solution.py:24
  28.8 1.7 collective-permute-start.2
  30.6 3.3 %collective-permute-start.3 = (bf16[576,256]{1,0:T(8,128)(2,1)}, bf16[576,256]{1,0:T(8,128)(2,1)}, u32[]{:S(2)}, u32[]{:S(2)}) collective-permute-start(bf16[576,256]{1,0:T(8,128)(2,1)} %fusion.4), channel_id=1, source_target_pairs={{0,8},{1,9},{2,10},{3,11},{4,12},{5,13},{6,14},{7,15},{8,0},{9,1},... | collective-permute-start | bytes 884744 | tf_op jit(solution)/shard_map/ppermute | solution.py:24
  34.7 1.3 collective-permute-start.6
  36.0 3.5 %collective-permute-done.2 = bf16[576,256]{1,0:T(8,128)(2,1)S(1)} collective-permute-done((bf16[576,256]{1,0:T(8,128)(2,1)}, bf16[576,256]{1,0:T(8,128)(2,1)S(1)}, u32[]{:S(2)}, u32[]{:S(2)}) %collective-permute-start.2) | collective-permute-done | bytes 294944 | tf_op jit(solution)/shard_map/ppermute | solution.py:24
  39.5 7.3 %collective-permute-done.3 = bf16[576,256]{1,0:T(8,128)(2,1)} collective-permute-done((bf16[576,256]{1,0:T(8,128)(2,1)}, bf16[576,256]{1,0:T(8,128)(2,1)}, u32[]{:S(2)}, u32[]{:S(2)}) %collective-permute-start.3) | collective-permute-done | bytes 294944 | tf_op jit(solution)/shard_map/ppermute | solution.py:24
  47.8 2.8 %collective-permute-start.5 = (bf16[576,256]{1,0:T(8,128)(2,1)S(1)}, bf16[576,256]{1,0:T(8,128)(2,1)S(1)}, u32[]{:S(2)}, u32[]{:S(2)}) collective-permute-start(bf16[576,256]{1,0:T(8,128)(2,1)S(1)} %select_select_fusion), channel_id=1, source_target_pairs={{0,64},{1,65},{2,66},{3,67},{4,68},{5,69},{6,70},{7,71},{8,72},{9,... | collective-permute-start | bytes 884744 | tf_op jit(solution)/shard_map/ppermute | solution.py:24
  50.6 7.9 %collective-permute-done.5 = bf16[576,256]{1,0:T(8,128)(2,1)S(1)} collective-permute-done((bf16[576,256]{1,0:T(8,128)(2,1)S(1)}, bf16[576,256]{1,0:T(8,128)(2,1)S(1)}, u32[]{:S(2)}, u32[]{:S(2)}) %collective-permute-start.5) | collective-permute-done | bytes 294944 | tf_op jit(solution)/shard_map/ppermute | solution.py:24
  58.6 3.1 %pack_rows.1 = bf16[640,2048]{1,0:T(8,128)(2,1)} custom-call(s32[2,256]{1,0:T(2,128)S(1)} %get-tuple-element.29.pos_ref, f32[2,256]{1,0:T(2,128)S(1)} %bitcast.88, bf16[256,2048]{1,0:T(8,128)(2,1)S(1)} %copy-done.6, bf16[256,2048]{1,0:T(8,128)(2,1)S(1)} %copy-done.8, bf16[2,576,256]{2,1,0:T(8,128)(2,1)S(1)} %pad_maximum_fusion.1.refs_0_.w0_ref, ...), custom_call_target="tpu_custom_call" | custom-call | flops 1000000 | bytes 100000 | tf_op jit(solution)/shard_map/pack_rows/pallas_call | solution.py:44
  61.7 6.1 %all-to-all-start = ((bf16[16,40,2048]{2,1,0:T(8,128)(2,1)}), bf16[16,40,2048]{2,1,0:T(8,128)(2,1)}, u32[]{:S(2)}, u32[]{:S(2)}) async-start(bf16[16,40,2048]{2,1,0:T(8,128)(2,1)} %bitcast.18), calls=%async_computation | async-start | bytes 5242880 | tf_op jit(solution)/shard_map/all_to_all | solution.py:368
  67.8 1.2 pad_maximum_fusion
  69.2 2.7 %collective-permute-start.10 = (bf16[2,576,256]{2,1,0:T(8,128)(2,1)S(1)}, bf16[2,576,256]{2,1,0:T(8,128)(2,1)S(1)}, u32[]{:S(2)}, u32[]{:S(2)}) collective-permute-start(bf16[2,576,256]{2,1,0:T(8,128)(2,1)S(1)} %pad_maximum_fusion.1.refs_0_.w0_ref), channel_id=1, source_target_pairs={{0,48},{1,49},{2,50},{3,51},{4,52},{5,53},{6,54},{7,55},{8,56},{9,... | collective-permute-start | bytes 1769480 | tf_op jit(solution)/shard_map/ppermute | solution.py:24
  72.0 1.6 collective-permute-start.9
  74.4 22.6 %collective-permute-done.10.w3_ref = bf16[2,576,256]{2,1,0:T(8,128)(2,1)S(1)} collective-permute-done((bf16[2,576,256]{2,1,0:T(8,128)(2,1)S(1)}, bf16[2,576,256]{2,1,0:T(8,128)(2,1)S(1)}, u32[]{:S(2)}, u32[]{:S(2)}) %collective-permute-start.10) | collective-permute-done | bytes 589856 | tf_op jit(solution)/shard_map/ppermute | solution.py:24
  97.0 2.3 collective-permute-done.9.w2_ref
  99.3 1.4 all-to-all-done
  100.7 7.6 %hot_expert.1 = (bf16[2,160,2048]{2,1,0:T(8,128)(2,1)}, bf16[2,160,2048]{2,1,0:T(8,128)(2,1)}, bf16[2,4,144,256]{3,2,1,0:T(8,128)(2,1)S(1)}, bf16[2,4,144,256]{3...) custom-call(s32[6]{0:T(128)S(1)} %concatenate.10.here_ref, ...), custom_call_target="tpu_custom_call" | custom-call | flops 1000000 | bytes 100000 | tf_op jit(solution)/shard_map/hot_expert/pallas_call | solution.py:44
  109.2 1.6 collective-permute-start.13
  110.8 2.4 collective-permute-start.14
  113.2 1.2 collective-permute-start.15
  114.4 1.8 add_convert_fusion.2.hot_a_ref
  116.3 1.1 copy-done.4
  117.4 1.2 collective-permute-start.12
  118.9 9.0 %home_hidden.1 = (bf16[320,768]{1,0:T(8,128)(2,1)S(1)}, bf16[320,1536]{1,0:T(8,128)(2,1)S(1)}, bf16[320,2048]{1,0:T(8,128)(2,1)S(1)}, bf16[320,2048]{1,0:T(8,128)(2,1)S(1)}) custom-call(bf16[640,2048]{1,0:T(8,128)(2,1)} %bitcast.19.after_ref.recv_ref, bf16[80,160]{1,0:T(8,128)(2,1)S(1)} %get-tuple-element.67.pick_x_ref, ...), custom_call_target="tpu_custom_call" | custom-call | flops 1000000 | bytes 100000 | tf_op jit(solution)/shard_map/home_hidden/pallas_call | solution.py:44
  128.0 4.8 %collective-permute-done.12.after_ref.hot_b_ref = bf16[160,2048]{1,0:T(8,128)(2,1)S(1)} collective-permute-done((bf16[160,2048]{1,0:T(8,128)(2,1)S(1)}, bf16[160,2048]{1,0:T(8,128)(2,1)S(1)}, u32[]{:S(2)}, u32[]{:S(2)}) %collective-permute-start.12) | collective-permute-done | bytes 655392 | tf_op jit(solution)/shard_map/ppermute | solution.py:24
  132.8 10.9 %home_rows.1.refs_4_ = bf16[640,2048]{1,0:T(8,128)(2,1)S(1)} custom-call(bf16[320,768]{1,0:T(8,128)(2,1)S(1)} %get-tuple-element.34.act_ref, bf16[320,1536]{1,0:T(8,128)(2,1)S(1)} %get-tuple-element.35.gh_ref, bf16[320,640]{1,0:T(8,128)(2,1)S(1)} %get-tuple-element.69.pick_x_ref, bf16[320,640]{1,0:T(8,128)(2,1)S(1)} %get-tuple-element.70.pick_g_ref, ...), custom_call_target="tpu_custom_call" | custom-call | flops 1000000 | bytes 100000 | tf_op jit(solution)/shard_map/home_rows/pallas_call | solution.py:44
  144.0 1.1 copy-done.2
  145.2 2.2 collective-permute-start.16
  147.3 5.5 %all-to-all-start.1 = ((bf16[16,40,2048]{2,1,0:T(8,128)(2,1)}), bf16[16,40,2048]{2,1,0:T(8,128)(2,1)S(1)}, u32[]{:S(2)}, u32[]{:S(2)}) async-start(bf16[16,40,2048]{2,1,0:T(8,128)(2,1)} %bitcast.84), calls=%async_computation.1 | async-start | bytes 5242880 | tf_op jit(solution)/shard_map/all_to_all | solution.py:408
  154.8 1.9 collective-permute-start.18
  156.7 1.1 collective-permute-start.19
  157.8 2.5 collective-permute-done.17
  160.9 1.3 copy-done.18
  162.2 1.3 copy-done.20
  163.5 8.6 %home_grads.1 = (bf16[2,256,1536]{2,1,0:T(8,128)(2,1)}, bf16[2,256,768]{2,1,0:T(8,128)(2,1)S(1)}, bf16[2,256,768]{2,1,0:T(8,128)(2,1)S(1)}, bf16[2,2,256,768]{3,...) custom-call(s32[6]{0:T(128)S(1)} %concatenate.10.here_ref, ...), custom_call_target="tpu_custom_call" | custom-call | flops 1000000 | bytes 100000 | tf_op jit(solution)/shard_map/home_grads/pallas_call | solution.py:44
  172.1 2.4 collective-permute-start.27
  174.5 1.9 collective-permute-start.30
  176.8 2.5 collective-permute-start.21
  179.3 7.9 %collective-permute-done.20.refs_1_ = bf16[144,256]{1,0:T(8,128)(2,1)S(1)} collective-permute-done((bf16[144,256]{1,0:T(8,128)(2,1)S(1)}, bf16[144,256]{1,0:T(8,128)(2,1)S(1)}, u32[]{:S(2)}, u32[]{:S(2)}) %collective-permute-start.20) | collective-permute-done | bytes 73760 | tf_op jit(solution)/shard_map/ppermute | solution.py:24
  187.2 3.6 %collective-permute-done.22.refs_3_ = bf16[144,256]{1,0:T(8,128)(2,1)S(1)} collective-permute-done((bf16[144,256]{1,0:T(8,128)(2,1)S(1)}, bf16[144,256]{1,0:T(8,128)(2,1)S(1)}, u32[]{:S(2)}, u32[]{:S(2)}) %collective-permute-start.22) | collective-permute-done | bytes 73760 | tf_op jit(solution)/shard_map/ppermute | solution.py:24
  191.7 12.9 %collective-permute-done.27 = bf16[2,2,256,768]{3,2,1,0:T(8,128)(2,1)S(1)} collective-permute-done((bf16[2,2,256,768]{3,2,1,0:T(8,128)(2,1)}, bf16[2,2,256,768]{3,2,1,0:T(8,128)(2,1)S(1)}, u32[]{:S(2)}, u32[]{:S(2)}) %collective-permute-start.27) | collective-permute-done | bytes 1572896 | tf_op jit(solution)/shard_map/ppermute | solution.py:24
  205.6 2.1 collective-permute-done.25
  207.7 1.2 slice_bitcast_fusion.5
  209.0 1.1 copy-done.25
  210.3 1.4 collective-permute-start.28
  212.1 12.6 %collective-permute-done.23 = bf16[4,144,256]{2,1,0:T(8,128)(2,1)} collective-permute-done((bf16[4,144,256]{2,1,0:T(8,128)(2,1)}, bf16[4,144,256]{2,1,0:T(8,128)(2,1)}, u32[]{:S(2)}, u32[]{:S(2)}) %collective-permute-start.23) | collective-permute-done | bytes 294944 | tf_op jit(solution)/shard_map/ppermute | solution.py:24
  224.7 1.9 pad_maximum_fusion.2.spare_ref
  227.5 2.2 add_convert_fusion
  232.5 1.2 slice_bitcast_fusion.8
  233.7 2.4 collective-permute-start.32
  237.3 1.3 copy-done.5
  239.7 4.6 %unpack_rows.1 = (bf16[256,2048]{1,0:T(8,128)(2,1)}, bf16[256,2048]{1,0:T(8,128)(2,1)}) custom-call(s32[2,256]{1,0:T(2,128)S(1)} %get-tuple-element.29.pos_ref, f32[256,2]{1,0:T(8,128)S(1)} %copy.12.gate_ref, bf16[640,2048]{1,0:T(8,128)(2,1)S(1)} %bitcast.80, bf16[2,160,2048]{2,1,0:T(8,128)(2,1)S(1)} %copy-done.5, bf16[160,2048]{1,0:T(8,128)(2,1)S(1)} %copy-done.13), custom_call_target="tpu_custom_call" | custom-call | flops 1000000 | bytes 100000 | tf_op jit(solution)/shard_map/unpack_rows/pallas_call | solution.py:44
  244.2 7.2 %collective-permute-done.32.d2_ref = bf16[96,2048]{1,0:T(8,128)(2,1)} collective-permute-done((bf16[96,2048]{1,0:T(8,128)(2,1)}, bf16[96,2048]{1,0:T(8,128)(2,1)}, u32[]{:S(2)}, u32[]{:S(2)}) %collective-permute-start.32) | collective-permute-done | bytes 393248 | tf_op jit(solution)/shard_map/ppermute | solution.py:24
  251.4 2.8 %collective-permute-done.33.d3_ref = bf16[96,2048]{1,0:T(8,128)(2,1)} collective-permute-done((bf16[96,2048]{1,0:T(8,128)(2,1)}, bf16[96,2048]{1,0:T(8,128)(2,1)}, u32[]{:S(2)}, u32[]{:S(2)}) %collective-permute-start.33) | collective-permute-done | bytes 393248 | tf_op jit(solution)/shard_map/ppermute | solution.py:24
  254.2 1.2 copy-done.21
  255.4 4.5 %finish_grads.1 = (f32[256,1536]{1,0:T(8,128)}, f32[96,2048]{1,0:T(8,128)}) custom-call(s32[6]{0:T(128)S(1)} %concatenate.10.here_ref, bf16[2,4,144,256]{3,2,1,0:T(8,128)(2,1)} %pad_maximum_fusion.2.spare_ref, bf16[2,4,144,256]{3,2,1,0:T(8,128)(2,1)} %collective-permute-done.24.more_ref, bf16[768,768]{1,0:T(8,128)(2,1)} %copy-done.3, ...), custom_call_target="tpu_custom_call" | custom-call | flops 1000000 | bytes 100000 | tf_op jit(solution)/shard_map/finish_grads/pallas_call | solution.py:44
  (122 shorter events, 19.7 us)
Async XLA Ops:
  0.6 1.2 copy-start.6
  1.2 12.3 %copy-start.3 = (bf16[768,768]{1,0:T(8,128)(2,1)}, bf16[768,768]{1,0:T(8,128)(2,1)S(1)}, u32[]{:S(2)}) copy-start(bf16[768,768]{1,0:T(8,128)(2,1)S(1)} %fusion.pick_ref) | copy-start | bytes 3538948
  1.9 2.8 %copy-start = (bf16[1,2048,1536]{2,1,0:T(8,128)(2,1)S(1)}, bf16[1,2048,1536]{2,1,0:T(8,128)(2,1)}, u32[]{:S(2)}) copy-start(bf16[1,2048,1536]{2,1,0:T(8,128)(2,1)} %param.11) | copy-start | bytes 18874372
  4.6 1.9 copy-start.1
  6.5 1.2 copy-start.7
  14.6 3.6 %collective-permute-start = (bf16[2,576,256]{2,1,0:T(8,128)(2,1)S(1)}, bf16[2,576,256]{2,1,0:T(8,128)(2,1)S(1)}, u32[]{:S(2)}, u32[]{:S(2)}) collective-permute-start(bf16[2,576,256]{2,1,0:T(8,128)(2,1)S(1)} %slice_bitcast_fusion.7), channel_id=1, source_target_pairs={{0,1},{1,0},{2,3},{3,2},{4,5},{5,4},{6,7},{7,6},{8,9},{9,8},{10,11... | collective-permute-start | bytes 1769480 | tf_op jit(solution)/shard_map/ppermute | solution.py:24
  19.4 8.7 %collective-permute-start.1 = (bf16[576,256]{1,0:T(8,128)(2,1)S(1)}, bf16[576,256]{1,0:T(8,128)(2,1)S(1)}, u32[]{:S(2)}, u32[]{:S(2)}) collective-permute-start(bf16[576,256]{1,0:T(8,128)(2,1)S(1)} %slice_bitcast_fusion.14), channel_id=1, source_target_pairs={{0,2},{1,3},{2,0},{3,1},{4,6},{5,7},{6,4},{7,5},{8,10},{9,11},{10,... | collective-permute-start | bytes 884744 | tf_op jit(solution)/shard_map/ppermute | solution.py:24
  28.8 10.6 %collective-permute-start.2 = (bf16[576,256]{1,0:T(8,128)(2,1)}, bf16[576,256]{1,0:T(8,128)(2,1)S(1)}, u32[]{:S(2)}, u32[]{:S(2)}) collective-permute-start(bf16[576,256]{1,0:T(8,128)(2,1)} %fusion.4), channel_id=1, source_target_pairs={{0,4},{1,5},{2,6},{3,7},{4,8},{5,9},{6,10},{7,11},{8,12},{9,13},{1... | collective-permute-start | bytes 884744 | tf_op jit(solution)/shard_map/ppermute | solution.py:24
  30.6 16.2 %collective-permute-start.3 = (bf16[576,256]{1,0:T(8,128)(2,1)}, bf16[576,256]{1,0:T(8,128)(2,1)}, u32[]{:S(2)}, u32[]{:S(2)}) collective-permute-start(bf16[576,256]{1,0:T(8,128)(2,1)} %fusion.4), channel_id=1, source_target_pairs={{0,8},{1,9},{2,10},{3,11},{4,12},{5,13},{6,14},{7,15},{8,0},{9,1},... | collective-permute-start | bytes 884744 | tf_op jit(solution)/shard_map/ppermute | solution.py:24
  33.9 12.9 %collective-permute-start.4 = (bf16[576,256]{1,0:T(8,128)(2,1)}, bf16[576,256]{1,0:T(8,128)(2,1)}, u32[]{:S(2)}, u32[]{:S(2)}) collective-permute-start(bf16[576,256]{1,0:T(8,128)(2,1)} %fusion.4), channel_id=1, source_target_pairs={{0,12},{1,13},{2,14},{3,15},{4,0},{5,1},{6,2},{7,3},{8,4},{9,5},{1... | collective-permute-start | bytes 884744 | tf_op jit(solution)/shard_map/ppermute | solution.py:24
  34.6 23.9 %copy-start.8 = (bf16[256,2048]{1,0:T(8,128)(2,1)S(1)}, bf16[256,2048]{1,0:T(8,128)(2,1)}, u32[]{:S(2)}) copy-start(bf16[256,2048]{1,0:T(8,128)(2,1)} %cot_ref.3) | copy-start | bytes 3145732
  34.7 23.9 %copy-start.27 = (f32[256,2]{0,1:T(2,128)S(1)}, f32[256,2]{0,1:T(2,128)}, u32[]{:S(2)}) copy-start(f32[256,2]{0,1:T(2,128)} %param.10) | copy-start | bytes 6148
  34.7 23.9 %collective-permute-start.6 = (bf16[160,2048]{1,0:T(8,128)(2,1)S(1)}, bf16[160,2048]{1,0:T(8,128)(2,1)S(1)}, u32[]{:S(2)}, u32[]{:S(2)}) collective-permute-start(bf16[160,2048]{1,0:T(8,128)(2,1)S(1)} %keep_rows.1.own_ref), channel_id=1, source_target_pairs={{0,2},{1,3},{2,0},{3,1},{4,6},{5,7},{6,4},{7,5},{8,10},{9,11},{10,... | collective-permute-start | bytes 1966088 | tf_op jit(solution)/shard_map/ppermute | solution.py:24
  47.8 10.7 %collective-permute-start.5 = (bf16[576,256]{1,0:T(8,128)(2,1)S(1)}, bf16[576,256]{1,0:T(8,128)(2,1)S(1)}, u32[]{:S(2)}, u32[]{:S(2)}) collective-permute-start(bf16[576,256]{1,0:T(8,128)(2,1)S(1)} %select_select_fusion), channel_id=1, source_target_pairs={{0,64},{1,65},{2,66},{3,67},{4,68},{5,69},{6,70},{7,71},{8,72},{9,... | collective-permute-start | bytes 884744 | tf_op jit(solution)/shard_map/ppermute | solution.py:24
  61.7 39.0 %all-to-all-start = ((bf16[16,40,2048]{2,1,0:T(8,128)(2,1)}), bf16[16,40,2048]{2,1,0:T(8,128)(2,1)}, u32[]{:S(2)}, u32[]{:S(2)}) async-start(bf16[16,40,2048]{2,1,0:T(8,128)(2,1)} %bitcast.18), calls=%async_computation | async-start | bytes 5242880 | tf_op jit(solution)/shard_map/all_to_all | solution.py:368
  69.0 30.4 %collective-permute-start.7 = (bf16[2,160,2048]{2,1,0:T(8,128)(2,1)}, bf16[2,160,2048]{2,1,0:T(8,128)(2,1)}, u32[]{:S(2)}, u32[]{:S(2)}) collective-permute-start(bf16[2,160,2048]{2,1,0:T(8,128)(2,1)} %pad_maximum_fusion), channel_id=1, source_target_pairs={{0,1},{1,0},{2,3},{3,2},{4,5},{5,4},{6,7},{7,6},{8,9},{9,8},{10,11... | collective-permute-start | bytes 3932168 | tf_op jit(solution)/shard_map/ppermute | solution.py:24
  69.2 27.7 %collective-permute-start.10 = (bf16[2,576,256]{2,1,0:T(8,128)(2,1)S(1)}, bf16[2,576,256]{2,1,0:T(8,128)(2,1)S(1)}, u32[]{:S(2)}, u32[]{:S(2)}) collective-permute-start(bf16[2,576,256]{2,1,0:T(8,128)(2,1)S(1)} %pad_maximum_fusion.1.refs_0_.w0_ref), channel_id=1, source_target_pairs={{0,48},{1,49},{2,50},{3,51},{4,52},{5,53},{6,54},{7,55},{8,56},{9,... | collective-permute-start | bytes 1769480 | tf_op jit(solution)/shard_map/ppermute | solution.py:24
  72.0 25.0 %collective-permute-start.8 = (bf16[2,576,256]{2,1,0:T(8,128)(2,1)S(1)}, bf16[2,576,256]{2,1,0:T(8,128)(2,1)S(1)}, u32[]{:S(2)}, u32[]{:S(2)}) collective-permute-start(bf16[2,576,256]{2,1,0:T(8,128)(2,1)S(1)} %pad_maximum_fusion.1.refs_0_.w0_ref), channel_id=1, source_target_pairs={{0,16},{1,17},{2,18},{3,19},{4,20},{5,21},{6,22},{7,23},{8,24},{9,... | collective-permute-start | bytes 1769480 | tf_op jit(solution)/shard_map/ppermute | solution.py:24
  72.0 27.3 %collective-permute-start.9 = (bf16[2,576,256]{2,1,0:T(8,128)(2,1)S(1)}, bf16[2,576,256]{2,1,0:T(8,128)(2,1)}, u32[]{:S(2)}, u32[]{:S(2)}) collective-permute-start(bf16[2,576,256]{2,1,0:T(8,128)(2,1)S(1)} %pad_maximum_fusion.1.refs_0_.w0_ref), channel_id=1, source_target_pairs={{0,32},{1,33},{2,34},{3,35},{4,36},{5,37},{6,38},{7,39},{8,40},{9,... | collective-permute-start | bytes 1769480 | tf_op jit(solution)/shard_map/ppermute | solution.py:24
  108.3 6.1 %collective-permute-start.11 = (bf16[2,160,2048]{2,1,0:T(8,128)(2,1)}, bf16[2,160,2048]{2,1,0:T(8,128)(2,1)S(1)}, u32[]{:S(2)}, u32[]{:S(2)}) collective-permute-start(bf16[2,160,2048]{2,1,0:T(8,128)(2,1)} %get-tuple-element.37), channel_id=1, source_target_pairs={{0,1},{1,0},{2,3},{3,2},{4,5},{5,4},{6,7},{7,6},{8,9},{9,8},{10,11... | collective-permute-start | bytes 3932168 | tf_op jit(solution)/shard_map/ppermute | solution.py:24
  109.2 34.5 %collective-permute-start.13 = (bf16[2,4,144,256]{3,2,1,0:T(8,128)(2,1)S(1)}, bf16[2,4,144,256]{3,2,1,0:T(8,128)(2,1)S(1)}, u32[]{:S(2)}, u32[]{:S(2)}) collective-permute-start(bf16[2,4,144,256]{3,2,1,0:T(8,128)(2,1)S(1)} %get-tuple-element.40), channel_id=1, source_target_pairs={{0,4},{1,5},{2,6},{3,7},{4,8},{5,9},{6,10},{7,11},{8,12},{9,13},{1... | collective-permute-start | bytes 1769480 | tf_op jit(solution)/shard_map/ppermute | solution.py:24
  110.8 32.9 %collective-permute-start.14 = (bf16[2,4,144,256]{3,2,1,0:T(8,128)(2,1)S(1)}, bf16[2,4,144,256]{3,2,1,0:T(8,128)(2,1)S(1)}, u32[]{:S(2)}, u32[]{:S(2)}) collective-permute-start(bf16[2,4,144,256]{3,2,1,0:T(8,128)(2,1)S(1)} %get-tuple-element.41), channel_id=1, source_target_pairs={{0,8},{1,9},{2,10},{3,11},{4,12},{5,13},{6,14},{7,15},{8,0},{9,1},... | collective-permute-start | bytes 1769480 | tf_op jit(solution)/shard_map/ppermute | solution.py:24
  113.2 30.5 %collective-permute-start.15 = (bf16[2,4,144,256]{3,2,1,0:T(8,128)(2,1)S(1)}, bf16[2,4,144,256]{3,2,1,0:T(8,128)(2,1)S(1)}, u32[]{:S(2)}, u32[]{:S(2)}) collective-permute-start(bf16[2,4,144,256]{3,2,1,0:T(8,128)(2,1)S(1)} %get-tuple-element.42), channel_id=1, source_target_pairs={{0,12},{1,13},{2,14},{3,15},{4,0},{5,1},{6,2},{7,3},{8,4},{9,5},{1... | collective-permute-start | bytes 1769480 | tf_op jit(solution)/shard_map/ppermute | solution.py:24
  117.4 15.4 %collective-permute-start.12 = (bf16[160,2048]{1,0:T(8,128)(2,1)S(1)}, bf16[160,2048]{1,0:T(8,128)(2,1)S(1)}, u32[]{:S(2)}, u32[]{:S(2)}) collective-permute-start(bf16[160,2048]{1,0:T(8,128)(2,1)S(1)} %slice_bitcast_fusion.6), channel_id=1, source_target_pairs={{0,2},{1,3},{2,0},{3,1},{4,6},{5,7},{6,4},{7,5},{8,10},{9,11},{10,... | collective-permute-start | bytes 1966088 | tf_op jit(solution)/shard_map/ppermute | solution.py:24
  127.9 15.7 %copy-start.9 = (bf16[320,1536]{1,0:T(8,128)(2,1)}, bf16[320,1536]{1,0:T(8,128)(2,1)S(1)}, u32[]{:S(2)}) copy-start(bf16[320,1536]{1,0:T(8,128)(2,1)S(1)} %get-tuple-element.35.gh_ref) | copy-start | bytes 2949124
  128.0 15.7 %copy-start.14 = (bf16[320,768]{1,0:T(8,128)(2,1)}, bf16[320,768]{1,0:T(8,128)(2,1)S(1)}, u32[]{:S(2)}) copy-start(bf16[320,768]{1,0:T(8,128)(2,1)S(1)} %get-tuple-element.34.act_ref) | copy-start | bytes 1474564
  128.0 15.7 %copy-start.17 = (bf16[320,2048]{1,0:T(8,128)(2,1)}, bf16[320,2048]{1,0:T(8,128)(2,1)S(1)}, u32[]{:S(2)}) copy-start(bf16[320,2048]{1,0:T(8,128)(2,1)S(1)} %get-tuple-element.43.x_ref) | copy-start | bytes 3932164
  128.0 15.7 %copy-start.19 = (bf16[320,2048]{1,0:T(8,128)(2,1)}, bf16[320,2048]{1,0:T(8,128)(2,1)S(1)}, u32[]{:S(2)}) copy-start(bf16[320,2048]{1,0:T(8,128)(2,1)S(1)} %get-tuple-element.44.g_ref) | copy-start | bytes 3932164
  132.8 10.9 %copy-start.12 = (bf16[160,2048]{1,0:T(8,128)(2,1)}, bf16[160,2048]{1,0:T(8,128)(2,1)S(1)}, u32[]{:S(2)}) copy-start(bf16[160,2048]{1,0:T(8,128)(2,1)S(1)} %collective-permute-done.12.after_ref.hot_b_ref) | copy-start | bytes 1966084
  143.7 1.5 copy-start.2
  145.2 8.5 %collective-permute-start.16 = (bf16[4,144,256]{2,1,0:T(8,128)(2,1)S(1)}, bf16[4,144,256]{2,1,0:T(8,128)(2,1)}, u32[]{:S(2)}, u32[]{:S(2)}) collective-permute-start(bf16[4,144,256]{2,1,0:T(8,128)(2,1)S(1)} %slice_bitcast_fusion.12), channel_id=1, source_target_pairs={{0,64},{1,65},{2,66},{3,67},{4,68},{5,69},{6,70},{7,71},{8,72},{9,... | collective-permute-start | bytes 884744 | tf_op jit(solution)/shard_map/ppermute | solution.py:24
  147.3 61.6 %all-to-all-start.1 = ((bf16[16,40,2048]{2,1,0:T(8,128)(2,1)}), bf16[16,40,2048]{2,1,0:T(8,128)(2,1)S(1)}, u32[]{:S(2)}, u32[]{:S(2)}) async-start(bf16[16,40,2048]{2,1,0:T(8,128)(2,1)} %bitcast.84), calls=%async_computation.1 | async-start | bytes 5242880 | tf_op jit(solution)/shard_map/all_to_all | solution.py:408
  152.9 8.0 %copy-start.10 = (bf16[320,1536]{1,0:T(8,128)(2,1)S(1)}, bf16[320,1536]{1,0:T(8,128)(2,1)}, u32[]{:S(2)}) copy-start(bf16[320,1536]{1,0:T(8,128)(2,1)} %copy-done.9) | copy-start | bytes 2949124
  152.9 8.0 %copy-start.15 = (bf16[320,768]{1,0:T(8,128)(2,1)S(1)}, bf16[320,768]{1,0:T(8,128)(2,1)}, u32[]{:S(2)}) copy-start(bf16[320,768]{1,0:T(8,128)(2,1)} %copy-done.14) | copy-start | bytes 1474564
  154.7 5.6 %collective-permute-start.17 = (bf16[144,256]{1,0:T(8,128)(2,1)S(1)}, bf16[144,256]{1,0:T(8,128)(2,1)S(1)}, u32[]{:S(2)}, u32[]{:S(2)}) collective-permute-start(bf16[144,256]{1,0:T(8,128)(2,1)S(1)} %get-tuple-element.64), channel_id=1, source_target_pairs={{0,16},{1,17},{2,18},{3,19},{4,20},{5,21},{6,22},{7,23},{8,24},{9,... | collective-permute-start | bytes 221192 | tf_op jit(solution)/shard_map/ppermute | solution.py:24
  154.8 5.5 %collective-permute-start.18 = (bf16[144,256]{1,0:T(8,128)(2,1)S(1)}, bf16[144,256]{1,0:T(8,128)(2,1)S(1)}, u32[]{:S(2)}, u32[]{:S(2)}) collective-permute-start(bf16[144,256]{1,0:T(8,128)(2,1)S(1)} %get-tuple-element.66), channel_id=1, source_target_pairs={{0,32},{1,33},{2,34},{3,35},{4,36},{5,37},{6,38},{7,39},{8,40},{9,... | collective-permute-start | bytes 221192 | tf_op jit(solution)/shard_map/ppermute | solution.py:24
  156.7 4.2 %collective-permute-start.19 = (bf16[144,256]{1,0:T(8,128)(2,1)S(1)}, bf16[144,256]{1,0:T(8,128)(2,1)S(1)}, u32[]{:S(2)}, u32[]{:S(2)}) collective-permute-start(bf16[144,256]{1,0:T(8,128)(2,1)S(1)} %get-tuple-element.65), channel_id=1, source_target_pairs={{0,48},{1,49},{2,50},{3,51},{4,52},{5,53},{6,54},{7,55},{8,56},{9,... | collective-permute-start | bytes 221192 | tf_op jit(solution)/shard_map/ppermute | solution.py:24
  160.9 1.3 copy-start.18
  162.2 1.3 copy-start.20
  172.1 33.5 %copy-start.22 = (bf16[2,256,768]{2,1,0:T(8,128)(2,1)}, bf16[2,256,768]{2,1,0:T(8,128)(2,1)S(1)}, u32[]{:S(2)}) copy-start(bf16[2,256,768]{2,1,0:T(8,128)(2,1)S(1)} %get-tuple-element.46.refs_0_) | copy-start | bytes 2359300
  172.1 33.5 %copy-start.24 = (bf16[2,256,768]{2,1,0:T(8,128)(2,1)}, bf16[2,256,768]{2,1,0:T(8,128)(2,1)S(1)}, u32[]{:S(2)}) copy-start(bf16[2,256,768]{2,1,0:T(8,128)(2,1)S(1)} %get-tuple-element.49.refs_0_) | copy-start | bytes 2359300
  172.1 32.5 %collective-permute-start.27 = (bf16[2,2,256,768]{3,2,1,0:T(8,128)(2,1)}, bf16[2,2,256,768]{3,2,1,0:T(8,128)(2,1)S(1)}, u32[]{:S(2)}, u32[]{:S(2)}) collective-permute-start(bf16[2,2,256,768]{3,2,1,0:T(8,128)(2,1)} %get-tuple-element.48), channel_id=1, source_target_pairs={{0,48},{1,49},{2,50},{3,51},{4,52},{5,53},{6,54},{7,55},{8,56},{9,... | collective-permute-start | bytes 4718600 | tf_op jit(solution)/shard_map/ppermute | solution.py:24
  174.5 33.2 %collective-permute-start.25 = (bf16[2,2,256,768]{3,2,1,0:T(8,128)(2,1)}, bf16[2,2,256,768]{3,2,1,0:T(8,128)(2,1)S(1)}, u32[]{:S(2)}, u32[]{:S(2)}) collective-permute-start(bf16[2,2,256,768]{3,2,1,0:T(8,128)(2,1)} %get-tuple-element.47), channel_id=1, source_target_pairs={{0,16},{1,17},{2,18},{3,19},{4,20},{5,21},{6,22},{7,23},{8,24},{9,... | collective-permute-start | bytes 4718600 | tf_op jit(solution)/shard_map/ppermute | solution.py:24
  174.5 53.0 %collective-permute-start.30 = (bf16[4,96,2048]{2,1,0:T(8,128)(2,1)}, bf16[4,96,2048]{2,1,0:T(8,128)(2,1)}, u32[]{:S(2)}, u32[]{:S(2)}) collective-permute-start(bf16[4,96,2048]{2,1,0:T(8,128)(2,1)} %get-tuple-element.51), channel_id=1, source_target_pairs={{0,64},{1,65},{2,66},{3,67},{4,68},{5,69},{6,70},{7,71},{8,72},{9,... | collective-permute-start | bytes 4718600 | tf_op jit(solution)/shard_map/ppermute | solution.py:24
  176.4 10.8 %collective-permute-start.20 = (bf16[144,256]{1,0:T(8,128)(2,1)S(1)}, bf16[144,256]{1,0:T(8,128)(2,1)S(1)}, u32[]{:S(2)}, u32[]{:S(2)}) collective-permute-start(bf16[144,256]{1,0:T(8,128)(2,1)S(1)} %fusion.7.refs_0_), channel_id=1, source_target_pairs={{0,4},{1,5},{2,6},{3,7},{4,8},{5,9},{6,10},{7,11},{8,12},{9,13},{1... | collective-permute-start | bytes 221192 | tf_op jit(solution)/shard_map/ppermute | solution.py:24
  176.8 10.5 %collective-permute-start.21 = (bf16[144,256]{1,0:T(8,128)(2,1)S(1)}, bf16[144,256]{1,0:T(8,128)(2,1)S(1)}, u32[]{:S(2)}, u32[]{:S(2)}) collective-permute-start(bf16[144,256]{1,0:T(8,128)(2,1)S(1)} %fusion.7.refs_0_), channel_id=1, source_target_pairs={{0,8},{1,9},{2,10},{3,11},{4,12},{5,13},{6,14},{7,15},{8,0},{9,1},... | collective-permute-start | bytes 221192 | tf_op jit(solution)/shard_map/ppermute | solution.py:24
  187.2 3.6 %collective-permute-start.22 = (bf16[144,256]{1,0:T(8,128)(2,1)S(1)}, bf16[144,256]{1,0:T(8,128)(2,1)S(1)}, u32[]{:S(2)}, u32[]{:S(2)}) collective-permute-start(bf16[144,256]{1,0:T(8,128)(2,1)S(1)} %fusion.7.refs_0_), channel_id=1, source_target_pairs={{0,12},{1,13},{2,14},{3,15},{4,0},{5,1},{6,2},{7,3},{8,4},{9,5},{1... | collective-permute-start | bytes 221192 | tf_op jit(solution)/shard_map/ppermute | solution.py:24
  191.6 33.1 %collective-permute-start.23 = (bf16[4,144,256]{2,1,0:T(8,128)(2,1)}, bf16[4,144,256]{2,1,0:T(8,128)(2,1)}, u32[]{:S(2)}, u32[]{:S(2)}) collective-permute-start(bf16[4,144,256]{2,1,0:T(8,128)(2,1)} %stack_z.1), channel_id=1, source_target_pairs={{0,2},{1,3},{2,0},{3,1},{4,6},{5,7},{6,4},{7,5},{8,10},{9,11},{10,... | collective-permute-start | bytes 884744 | tf_op jit(solution)/shard_map/ppermute | solution.py:24
  210.1 1.6 copy-start.11
  210.1 1.6 copy-start.23
  210.3 19.5 %collective-permute-start.28 = (bf16[2,256,768]{2,1,0:T(8,128)(2,1)S(1)}, bf16[2,256,768]{2,1,0:T(8,128)(2,1)S(1)}, u32[]{:S(2)}, u32[]{:S(2)}) collective-permute-start(bf16[2,256,768]{2,1,0:T(8,128)(2,1)S(1)} %sum_down.1), channel_id=1, source_target_pairs={{0,48},{1,49},{2,50},{3,51},{4,52},{5,53},{6,54},{7,55},{8,56},{9,... | collective-permute-start | bytes 2359304 | tf_op jit(solution)/shard_map/ppermute | solution.py:24
  211.7 15.9 %copy-start.34 = (bf16[4,96,2048]{2,1,0:T(8,128)(2,1)S(1)}, bf16[4,96,2048]{2,1,0:T(8,128)(2,1)}, u32[]{:S(2)}) copy-start(bf16[4,96,2048]{2,1,0:T(8,128)(2,1)} %get-tuple-element.50) | copy-start | bytes 4718596
  211.8 17.9 %collective-permute-start.26 = (bf16[2,256,768]{2,1,0:T(8,128)(2,1)S(1)}, bf16[2,256,768]{2,1,0:T(8,128)(2,1)S(1)}, u32[]{:S(2)}, u32[]{:S(2)}) collective-permute-start(bf16[2,256,768]{2,1,0:T(8,128)(2,1)S(1)} %sum_up.1), channel_id=1, source_target_pairs={{0,16},{1,17},{2,18},{3,19},{4,20},{5,21},{6,22},{7,23},{8,24},{9,... | collective-permute-start | bytes 2359304 | tf_op jit(solution)/shard_map/ppermute | solution.py:24
  226.6 17.6 %collective-permute-start.24 = (bf16[2,4,144,256]{3,2,1,0:T(8,128)(2,1)}, bf16[2,4,144,256]{3,2,1,0:T(8,128)(2,1)}, u32[]{:S(2)}, u32[]{:S(2)}) collective-permute-start(bf16[2,4,144,256]{3,2,1,0:T(8,128)(2,1)} %pad_maximum_fusion.2.spare_ref), channel_id=1, source_target_pairs={{0,1},{1,0},{2,3},{3,2},{4,5},{5,4},{6,7},{7,6},{8,9},{9,8},{10,11... | collective-permute-start | bytes 1769480 | tf_op jit(solution)/shard_map/ppermute | solution.py:24
  227.5 2.3 copy-start.31
  227.5 2.3 copy-start.32
  227.5 2.4 copy-start.33
  231.4 22.8 %collective-permute-start.29 = (bf16[256,1536]{1,0:T(8,128)(2,1)}, bf16[256,1536]{1,0:T(8,128)(2,1)}, u32[]{:S(2)}, u32[]{:S(2)}) collective-permute-start(bf16[256,1536]{1,0:T(8,128)(2,1)} %get-tuple-element.58), channel_id=1, source_target_pairs={{0,64},{1,65},{2,66},{3,67},{4,68},{5,69},{6,70},{7,71},{8,72},{9,... | collective-permute-start | bytes 2359304 | tf_op jit(solution)/shard_map/ppermute | solution.py:24
  233.7 10.6 %collective-permute-start.31 = (bf16[96,2048]{1,0:T(8,128)(2,1)}, bf16[96,2048]{1,0:T(8,128)(2,1)}, u32[]{:S(2)}, u32[]{:S(2)}) collective-permute-start(bf16[96,2048]{1,0:T(8,128)(2,1)} %get-tuple-element.56), channel_id=1, source_target_pairs={{0,16},{1,17},{2,18},{3,19},{4,20},{5,21},{6,22},{7,23},{8,24},{9,... | collective-permute-start | bytes 1179656 | tf_op jit(solution)/shard_map/ppermute | solution.py:24
  233.7 17.7 %collective-permute-start.32 = (bf16[96,2048]{1,0:T(8,128)(2,1)}, bf16[96,2048]{1,0:T(8,128)(2,1)}, u32[]{:S(2)}, u32[]{:S(2)}) collective-permute-start(bf16[96,2048]{1,0:T(8,128)(2,1)} %get-tuple-element.55), channel_id=1, source_target_pairs={{0,32},{1,33},{2,34},{3,35},{4,36},{5,37},{6,38},{7,39},{8,40},{9,... | collective-permute-start | bytes 1179656 | tf_op jit(solution)/shard_map/ppermute | solution.py:24
  236.0 18.2 %collective-permute-start.33 = (bf16[96,2048]{1,0:T(8,128)(2,1)}, bf16[96,2048]{1,0:T(8,128)(2,1)}, u32[]{:S(2)}, u32[]{:S(2)}) collective-permute-start(bf16[96,2048]{1,0:T(8,128)(2,1)} %get-tuple-element.54), channel_id=1, source_target_pairs={{0,48},{1,49},{2,50},{3,51},{4,52},{5,53},{6,54},{7,55},{8,56},{9,... | collective-permute-start | bytes 1179656 | tf_op jit(solution)/shard_map/ppermute | solution.py:24
  237.2 1.3 copy-start.5
  239.7 14.5 %copy-start.16 = (bf16[96,2048]{1,0:T(8,128)(2,1)S(1)}, bf16[96,2048]{1,0:T(8,128)(2,1)}, u32[]{:S(2)}) copy-start(bf16[96,2048]{1,0:T(8,128)(2,1)} %get-tuple-element.57.d0_ref) | copy-start | bytes 1179652
  254.2 1.2 copy-start.21
  (7 other events, 6.1 us)

commit v2 on v1

--- a/solution.py
+++ b/solution.py
@@ -398,30 +398,30 @@
         (recv, pick_x, pick_g, w_in, w_out, spares[0]),
         in_specs=[VMEM] * 5 + [AFTER],
     )
-    (result,) = call(
-        result_kernel,
-        "home_rows",
-        (shape(640, 2048),),
-        (active, grad_hidden, back_x, back_g, w_in, w_out, near_part),
-        in_specs=[VMEM] * 6 + [AFTER],
-    )
-    returned = lax.all_to_all(result, "expert", split_axis=0, concat_axis=0, tiled=True)
-    spare = sum_after(
-        [spares[0]] + [hop(spares[s], dz=s) for s in (1, 2, 3)], [result], "sum_z"
-    )
-    spare = total(spare[0], hop(spare[1], dh=1))
-    spare = total(spare[0], *[hop(spare[s], dy=s) for s in (1, 2, 3)])
     half = shape(2, 256, 768)
     in_own, up_a, dn_b, to_up, to_dn, out_own, out_far = call(
         grads_kernel,
         "home_grads",
         (shape(2, 256, 1536),) + (half,) * 2 + (shape(2, 2, 256, 768),) * 2 + (shape(4, 96, 2048),) * 2,
-        (here, active, grad_hidden, rows_x, rows_g, spare),
+        (here, active, grad_hidden, rows_x, rows_g, near_part),
         in_specs=[SMEM] + [VMEM] * 4 + [AFTER],
     )
+    spare = sum_after(
+        [spares[0]] + [hop(spares[s], dz=s) for s in (1, 2, 3)], [in_own], "sum_z"
+    )
+    (result,) = call(
+        result_kernel,
+        "home_rows",
+        (shape(640, 2048),),
+        (active, grad_hidden, back_x, back_g, w_in, w_out, spare),
+        in_specs=[VMEM] * 6 + [AFTER],
+    )
+    returned = lax.all_to_all(result, "expert", split_axis=0, concat_axis=0, tiled=True)
+    spare = total(spare[0], hop(spare[1], dh=1))
+    spare = total(spare[0], *[hop(spare[s], dy=s) for s in (1, 2, 3)])
 
     from_dn, from_up = hop(to_up, dy=1), hop(to_dn, dy=3)
-    out_far = hop(out_far, dh=1)
+    out_sum = total(out_own, hop(out_far, dh=1))
     mixed, token_grad = call(
         unpack_kernel,
         "unpack_rows",
@@ -433,19 +433,18 @@
         stack_kernel,
         "stack_z",
         (shape(4, 144, 256),),
-        (spare, *[hop(spare, dz=s) for s in (1, 2, 3)]),
-        in_specs=[VMEM] * 4,
+        (spare, *[hop(spare, dz=s) for s in (1, 2, 3)], returned, out_sum),
+        in_specs=[VMEM] * 4 + [AFTER] * 2,
     )
     spare = jnp.stack([spare, hop(spare, dl=1)])
     more = hop(spare, dc=1)
-    up_a = hop(sum_after([up_a, from_dn[0]], [returned], "sum_up"), dy=1)
-    dn_b = hop(sum_after([dn_b, from_up[1]], [returned], "sum_down"), dy=3)
+    up_a = hop(sum_after([up_a, from_dn[0]], [result], "sum_up"), dy=1)
+    dn_b = hop(sum_after([dn_b, from_up[1]], [result], "sum_down"), dy=3)
     up_b, dn_a = from_dn[1], from_up[0]
     in_sum = total(
         in_own, jnp.concatenate([up_a, up_b], axis=2), jnp.concatenate([dn_a, dn_b], axis=2)
     )
     in_got = hop(in_sum[1], dh=1)
-    out_sum = total(out_own, out_far)
     out_parts = [out_sum[0]] + [hop(out_sum[s], dy=s) for s in (1, 2, 3)]
 
     grad_gate_up, grad_down = call(

time: 261 us -> 262 us (level)
  waiting for transfers between devices: 109 us -> 92.6 us
  starting transfers between devices: 55.8 us -> 67 us
  local copies, waits for them, and re-layouts: 24.9 us -> 28.9 us
    ppermute x34, waiting for transfers between devices: 108 us -> 87.6 us  [hop(): return lax.ppermute(x, AXES, pairs)]
    ppermute x34, starting transfers between devices: 44.2 us -> 54 us  [hop(): return lax.ppermute(x, AXES, pairs)]
    all_to_all x1, waiting for transfers between devices: 0.01 us -> 3.66 us  [shards(): lax.all_to_all(result, 'expert', split_axis=0, concat_axis=0, tiled=True)]
    unnamed x71 -> x59, local copies, waits for them, and re-layouts: 19.1 us -> 22.4 us
  transfers between devices with their start and end apart: 36 -> 36, of which waited for: 18 -> 16; matrix products, arithmetic and copies ran while one was open for 6% -> 6% of each run, Pallas kernels for 13% -> 14%
where the time goes in v2:
time: 262 us; the launch traced here: 261 us
  waiting for transfers between devices  92.6 us (35%)
  starting transfers between devices  67 us (26%)
  Pallas kernels  54.1 us (21%)
  local copies, waits for them, and re-layouts  28.9 us (11%)
  other arithmetic  13.7 us (5%)
  between operations  4.35 us (2%)
    ppermute x34, waiting for transfers between devices, hop(): return lax.ppermute(x, AXES, pairs)  87.6 us
    ppermute x34, starting transfers between devices, hop(): return lax.ppermute(x, AXES, pairs)  54 us
    pallas_call x12, Pallas kernels, call(): pl.pallas_call(kernel, out_shape=outs, in_specs=in_specs or [VMEM] * len(...  51.1 us
    unnamed x59, local copies, waits for them, and re-layouts  22.4 us
    convert_element_type x5, other arithmetic, total(): return out.astype(dtype)  7.92 us
    all_to_all x1, starting transfers between devices, shards(): lax.all_to_all(result, 'expert', split_axis=0, concat_axis=0, tiled=True)  6.82 us
    all_to_all x1, starting transfers between devices, shards(): lax.all_to_all(send, 'expert', split_axis=0, concat_axis=0, tiled=True)  6.2 us
  transfers between devices with their start and end apart: 36, of which 16 were waited for; matrix products, arithmetic and copies ran while one was open for 6% of the time, Pallas kernels for 14%

profile of v2, /device:TPU:1, one launch (start us, length us, event | category | flops | bytes accessed | tf_op | source)
XLA Modules:
  0.0 260.7 jit_solution(16906366379588974972)
XLA Ops:
  1.9 2.8 %copy-done = bf16[1,2048,1536]{2,1,0:T(8,128)(2,1)S(1)} copy-done((bf16[1,2048,1536]{2,1,0:T(8,128)(2,1)S(1)}, bf16[1,2048,1536]{2,1,0:T(8,128)(2,1)}, u32[]{:S(2)}) %copy-start) | copy-done | bytes 6291480
  4.6 1.9 copy-done.1
  6.5 1.2 copy-done.9
  10.5 3.0 %route.1 = (bf16[2,2,576,256]{3,2,1,0:T(8,128)(2,1)}, bf16[160,2048]{1,0:T(8,128)(2,1)S(1)}, s32[2,256]{1,0:T(2,128)S(1)}, s32[1,1]{1,0:T(1,128)}) custom-call(s32[5]{0:T(128)S(1)} %stack.50.here_ref, s32[2,256]{1,0:T(2,128)S(1)} %bitcast.88, s32[2,256]{1,0:T(2,128)S(1)} %bitcast.89, s32[2,256]{1,0:T(2,128)S(1)} %bitcast.90, f32[2,256]{1,0:T(2,128)S(1)} %bitcast.86, ...), custom_call_target="tpu_custom_call" | custom-call | flops 1000000 | bytes 100000 | tf_op jit(solution)/shard_map/route/pallas_call | solution.py:127
  13.6 1.1 slice_bitcast_fusion.7
  14.7 1.5 collective-permute-start
  18.1 1.1 bitcast_select_fusion
  19.3 1.4 collective-permute-start.1
  21.3 6.6 %collective-permute-done.1.refs_1_ = bf16[576,256]{1,0:T(8,128)(2,1)S(1)} collective-permute-done((bf16[576,256]{1,0:T(8,128)(2,1)S(1)}, bf16[576,256]{1,0:T(8,128)(2,1)S(1)}, u32[]{:S(2)}, u32[]{:S(2)}) %collective-permute-start.1) | collective-permute-done | bytes 294944 | tf_op jit(solution)/shard_map/ppermute | solution.py:24
  28.6 1.7 collective-permute-start.2
  30.4 3.3 %collective-permute-start.3 = (bf16[576,256]{1,0:T(8,128)(2,1)}, bf16[576,256]{1,0:T(8,128)(2,1)}, u32[]{:S(2)}, u32[]{:S(2)}) collective-permute-start(bf16[576,256]{1,0:T(8,128)(2,1)} %fusion.4), channel_id=1, source_target_pairs={{0,8},{1,9},{2,10},{3,11},{4,12},{5,13},{6,14},{7,15},{8,0},{9,1},... | collective-permute-start | bytes 884744 | tf_op jit(solution)/shard_map/ppermute | solution.py:24
  34.5 1.3 collective-permute-start.6
  35.8 3.5 %collective-permute-done.2 = bf16[576,256]{1,0:T(8,128)(2,1)S(1)} collective-permute-done((bf16[576,256]{1,0:T(8,128)(2,1)}, bf16[576,256]{1,0:T(8,128)(2,1)S(1)}, u32[]{:S(2)}, u32[]{:S(2)}) %collective-permute-start.2) | collective-permute-done | bytes 294944 | tf_op jit(solution)/shard_map/ppermute | solution.py:24
  39.2 7.3 %collective-permute-done.3 = bf16[576,256]{1,0:T(8,128)(2,1)} collective-permute-done((bf16[576,256]{1,0:T(8,128)(2,1)}, bf16[576,256]{1,0:T(8,128)(2,1)}, u32[]{:S(2)}, u32[]{:S(2)}) %collective-permute-start.3) | collective-permute-done | bytes 294944 | tf_op jit(solution)/shard_map/ppermute | solution.py:24
  47.5 2.8 %collective-permute-start.5 = (bf16[576,256]{1,0:T(8,128)(2,1)S(1)}, bf16[576,256]{1,0:T(8,128)(2,1)S(1)}, u32[]{:S(2)}, u32[]{:S(2)}) collective-permute-start(bf16[576,256]{1,0:T(8,128)(2,1)S(1)} %select_select_fusion), channel_id=1, source_target_pairs={{0,64},{1,65},{2,66},{3,67},{4,68},{5,69},{6,70},{7,71},{8,72},{9,... | collective-permute-start | bytes 884744 | tf_op jit(solution)/shard_map/ppermute | solution.py:24
  50.4 7.8 %collective-permute-done.5 = bf16[576,256]{1,0:T(8,128)(2,1)S(1)} collective-permute-done((bf16[576,256]{1,0:T(8,128)(2,1)S(1)}, bf16[576,256]{1,0:T(8,128)(2,1)S(1)}, u32[]{:S(2)}, u32[]{:S(2)}) %collective-permute-start.5) | collective-permute-done | bytes 294944 | tf_op jit(solution)/shard_map/ppermute | solution.py:24
  58.3 3.1 %pack_rows.1 = bf16[640,2048]{1,0:T(8,128)(2,1)} custom-call(s32[2,256]{1,0:T(2,128)S(1)} %get-tuple-element.29.pos_ref, f32[2,256]{1,0:T(2,128)S(1)} %bitcast.87, bf16[256,2048]{1,0:T(8,128)(2,1)S(1)} %copy-done.8, bf16[256,2048]{1,0:T(8,128)(2,1)S(1)} %copy-done.10, bf16[2,576,256]{2,1,0:T(8,128)(2,1)S(1)} %pad_maximum_fusion.1.refs_0_.w0_ref, ...), custom_call_target="tpu_custom_call" | custom-call | flops 1000000 | bytes 100000 | tf_op jit(solution)/shard_map/pack_rows/pallas_call | solution.py:44
  61.4 6.2 %all-to-all-start = ((bf16[16,40,2048]{2,1,0:T(8,128)(2,1)}), bf16[16,40,2048]{2,1,0:T(8,128)(2,1)}, u32[]{:S(2)}, u32[]{:S(2)}) async-start(bf16[16,40,2048]{2,1,0:T(8,128)(2,1)} %bitcast.18), calls=%async_computation | async-start | bytes 5242880 | tf_op jit(solution)/shard_map/all_to_all | solution.py:368
  67.6 1.2 pad_maximum_fusion
  69.0 2.7 %collective-permute-start.10 = (bf16[2,576,256]{2,1,0:T(8,128)(2,1)S(1)}, bf16[2,576,256]{2,1,0:T(8,128)(2,1)S(1)}, u32[]{:S(2)}, u32[]{:S(2)}) collective-permute-start(bf16[2,576,256]{2,1,0:T(8,128)(2,1)S(1)} %pad_maximum_fusion.1.refs_0_.w0_ref), channel_id=1, source_target_pairs={{0,48},{1,49},{2,50},{3,51},{4,52},{5,53},{6,54},{7,55},{8,56},{9,... | collective-permute-start | bytes 1769480 | tf_op jit(solution)/shard_map/ppermute | solution.py:24
  71.8 1.7 collective-permute-start.9
  74.2 22.6 %collective-permute-done.10.w3_ref = bf16[2,576,256]{2,1,0:T(8,128)(2,1)S(1)} collective-permute-done((bf16[2,576,256]{2,1,0:T(8,128)(2,1)S(1)}, bf16[2,576,256]{2,1,0:T(8,128)(2,1)S(1)}, u32[]{:S(2)}, u32[]{:S(2)}) %collective-permute-start.10) | collective-permute-done | bytes 589856 | tf_op jit(solution)/shard_map/ppermute | solution.py:24
  97.6 1.6 collective-permute-done.9.w2_ref
  99.1 1.4 all-to-all-done
  101.6 7.6 %hot_expert.1 = (bf16[2,160,2048]{2,1,0:T(8,128)(2,1)}, bf16[2,160,2048]{2,1,0:T(8,128)(2,1)}, bf16[2,4,144,256]{3,2,1,0:T(8,128)(2,1)S(1)}, bf16[2,4,144,256]{3...) custom-call(s32[6]{0:T(128)S(1)} %concatenate.10.here_ref, ...), custom_call_target="tpu_custom_call" | custom-call | flops 1000000 | bytes 100000 | tf_op jit(solution)/shard_map/hot_expert/pallas_call | solution.py:44
  109.2 1.7 collective-permute-start.14
  110.9 2.9 %collective-permute-done.14 = bf16[2,160,2048]{2,1,0:T(8,128)(2,1)S(1)} collective-permute-done((bf16[2,160,2048]{2,1,0:T(8,128)(2,1)}, bf16[2,160,2048]{2,1,0:T(8,128)(2,1)S(1)}, u32[]{:S(2)}, u32[]{:S(2)}) %collective-permute-start.14) | collective-permute-done | bytes 1310752 | tf_op jit(solution)/shard_map/ppermute | solution.py:24
  113.7 1.8 add_convert_fusion.2.hot_a_ref
  116.7 1.5 collective-permute-start.15
  118.2 1.3 collective-permute-start.11
  119.5 2.4 collective-permute-start.12
  121.9 1.2 collective-permute-start.13
  123.2 9.1 %home_hidden.1 = (bf16[320,768]{1,0:T(8,128)(2,1)S(1)}, bf16[320,1536]{1,0:T(8,128)(2,1)S(1)}, bf16[320,2048]{1,0:T(8,128)(2,1)S(1)}, bf16[320,2048]{1,0:T(8,128)(2,1)S(1)}) custom-call(bf16[640,2048]{1,0:T(8,128)(2,1)} %bitcast.19.after_ref.recv_ref, bf16[80,160]{1,0:T(8,128)(2,1)S(1)} %get-tuple-element.67.pick_x_ref, ...), custom_call_target="tpu_custom_call" | custom-call | flops 1000000 | bytes 100000 | tf_op jit(solution)/shard_map/home_hidden/pallas_call | solution.py:44
  133.3 9.4 %home_grads.1 = (bf16[2,256,1536]{2,1,0:T(8,128)(2,1)}, bf16[2,256,768]{2,1,0:T(8,128)(2,1)S(1)}, bf16[2,256,768]{2,1,0:T(8,128)(2,1)S(1)}, bf16[2,2,256,768]{3,...) custom-call(s32[6]{0:T(128)S(1)} %concatenate.10.here_ref, ...), custom_call_target="tpu_custom_call" | custom-call | flops 1000000 | bytes 100000 | tf_op jit(solution)/shard_map/home_grads/pallas_call | solution.py:44
  144.5 1.3 collective-permute-start.28
  146.0 2.2 collective-permute-start.23
  148.2 1.4 copy-done.6
  149.9 1.3 collective-permute-start.16
  151.4 12.1 %home_rows.1.refs_2_ = bf16[640,2048]{1,0:T(8,128)(2,1)} custom-call(bf16[320,768]{1,0:T(8,128)(2,1)S(1)} %get-tuple-element.34.act_ref, bf16[320,1536]{1,0:T(8,128)(2,1)S(1)} %get-tuple-element.35.gh_ref, bf16[320,640]{1,0:T(8,128)(2,1)S(1)} %get-tuple-element.69.pick_x_ref, bf16[320,640]{1,0:T(8,128)(2,1)S(1)} %get-tuple-element.70.pick_g_ref, ...), custom_call_target="tpu_custom_call" | custom-call | flops 1000000 | bytes 100000 | tf_op jit(solution)/shard_map/home_rows/pallas_call | solution.py:44
  163.5 6.8 %all-to-all-start.1 = ((bf16[16,40,2048]{2,1,0:T(8,128)(2,1)}), bf16[16,40,2048]{2,1,0:T(8,128)(2,1)S(1)}, u32[]{:S(2)}, u32[]{:S(2)}) async-start(bf16[16,40,2048]{2,1,0:T(8,128)(2,1)} %bitcast.24), calls=%async_computation.1 | async-start | bytes 5242880 | tf_op jit(solution)/shard_map/all_to_all | solution.py:419
  170.3 17.7 %collective-permute-done.16 = bf16[4,144,256]{2,1,0:T(8,128)(2,1)} collective-permute-done((bf16[4,144,256]{2,1,0:T(8,128)(2,1)S(1)}, bf16[4,144,256]{2,1,0:T(8,128)(2,1)}, u32[]{:S(2)}, u32[]{:S(2)}) %collective-permute-start.16) | collective-permute-done | bytes 294944 | tf_op jit(solution)/shard_map/ppermute | solution.py:24
  189.5 3.7 %collective-permute-start.18 = (bf16[144,256]{1,0:T(8,128)(2,1)S(1)}, bf16[144,256]{1,0:T(8,128)(2,1)S(1)}, u32[]{:S(2)}, u32[]{:S(2)}) collective-permute-start(bf16[144,256]{1,0:T(8,128)(2,1)S(1)} %get-tuple-element.66), channel_id=1, source_target_pairs={{0,32},{1,33},{2,34},{3,35},{4,36},{5,37},{6,38},{7,39},{8,40},{9,... | collective-permute-start | bytes 221192 | tf_op jit(solution)/shard_map/ppermute | solution.py:24
  193.2 1.5 slice_bitcast_fusion.3
  195.3 1.5 slice_bitcast_fusion.5
  197.0 1.5 collective-permute-start.27
  198.6 2.4 collective-permute-start.21
  202.0 3.4 %add_convert_fusion.1.refs_5_ = bf16[4,96,2048]{2,1,0:T(8,128)(2,1)} fusion(bf16[4,96,2048]{2,1,0:T(8,128)(2,1)} %collective-permute-done.23, bf16[4,96,2048]{2,1,0:T(8,128)(2,1)S(1)} %copy-done.28), kind=kLoop, calls=%fused_computation.1 | loop fusion | flops 3145728 | bytes 4718592 | tf_op jit(solution)/shard_map/convert_element_type | solution.py:35
  205.4 6.2 %collective-permute-done.29 = bf16[2,256,768]{2,1,0:T(8,128)(2,1)S(1)} collective-permute-done((bf16[2,256,768]{2,1,0:T(8,128)(2,1)S(1)}, bf16[2,256,768]{2,1,0:T(8,128)(2,1)S(1)}, u32[]{:S(2)}, u32[]{:S(2)}) %collective-permute-start.29) | collective-permute-done | bytes 786464 | tf_op jit(solution)/shard_map/ppermute | solution.py:24
  212.1 1.7 add_convert_fusion
  213.8 3.7 %all-to-all-done.1 = bf16[16,40,2048]{2,1,0:T(8,128)(2,1)S(1)} async-done(((bf16[16,40,2048]{2,1,0:T(8,128)(2,1)}), bf16[16,40,2048]{2,1,0:T(8,128)(2,1)S(1)}, u32[]{:S(2)}, u32[]{:S(2)}) %all-to-all-start.1) | async-done | bytes 2621472 | tf_op jit(solution)/shard_map/all_to_all | solution.py:419
  217.5 1.4 copy-done.2
  221.3 2.1 collective-permute-start.30
  223.4 1.2 collective-permute-done.24
  225.5 7.4 %collective-permute-start.25 = (bf16[2,4,144,256]{3,2,1,0:T(8,128)(2,1)}, bf16[2,4,144,256]{3,2,1,0:T(8,128)(2,1)}, u32[]{:S(2)}, u32[]{:S(2)}) collective-permute-start(bf16[2,4,144,256]{3,2,1,0:T(8,128)(2,1)} %pad_maximum_fusion.2.spare_ref), channel_id=1, source_target_pairs={{0,1},{1,0},{2,3},{3,2},{4,5},{5,4},{6,7},{7,6},{8,9},{9,8},{10,11... | collective-permute-start | bytes 1769480 | tf_op jit(solution)/shard_map/ppermute | solution.py:24
  232.8 1.2 slice_bitcast_fusion.8
  234.5 1.9 collective-permute-start.32
  236.4 1.8 collective-permute-start.33
  238.3 1.3 copy-done.5
  239.7 1.1 copy-done.12
  240.7 4.6 %unpack_rows.1 = (bf16[256,2048]{1,0:T(8,128)(2,1)}, bf16[256,2048]{1,0:T(8,128)(2,1)}) custom-call(s32[2,256]{1,0:T(2,128)S(1)} %get-tuple-element.29.pos_ref, f32[256,2]{1,0:T(8,128)S(1)} %copy.12.gate_ref, bf16[640,2048]{1,0:T(8,128)(2,1)S(1)} %bitcast.82, bf16[2,160,2048]{2,1,0:T(8,128)(2,1)S(1)} %copy-done.5, bf16[160,2048]{1,0:T(8,128)(2,1)S(1)} %copy-done.12), custom_call_target="tpu_custom_call" | custom-call | flops 1000000 | bytes 100000 | tf_op jit(solution)/shard_map/unpack_rows/pallas_call | solution.py:44
  245.3 1.2 collective-permute-done.31.d1_ref
  246.5 8.0 %collective-permute-done.32.d2_ref = bf16[96,2048]{1,0:T(8,128)(2,1)} collective-permute-done((bf16[96,2048]{1,0:T(8,128)(2,1)}, bf16[96,2048]{1,0:T(8,128)(2,1)}, u32[]{:S(2)}, u32[]{:S(2)}) %collective-permute-start.32) | collective-permute-done | bytes 393248 | tf_op jit(solution)/shard_map/ppermute | solution.py:24
  255.0 1.2 copy-done.15
  256.2 4.5 %finish_grads.1 = (f32[256,1536]{1,0:T(8,128)}, f32[96,2048]{1,0:T(8,128)}) custom-call(s32[6]{0:T(128)S(1)} %concatenate.10.here_ref, bf16[2,4,144,256]{3,2,1,0:T(8,128)(2,1)} %pad_maximum_fusion.2.spare_ref, bf16[2,4,144,256]{3,2,1,0:T(8,128)(2,1)} %collective-permute-done.25.more_ref, bf16[768,768]{1,0:T(8,128)(2,1)} %copy-done.3, ...), custom_call_target="tpu_custom_call" | custom-call | flops 1000000 | bytes 100000 | tf_op jit(solution)/shard_map/finish_grads/pallas_call | solution.py:44
  (110 shorter events, 21.7 us)
Async XLA Ops:
  0.6 1.2 copy-start.8
  1.2 12.4 %copy-start.3 = (bf16[768,768]{1,0:T(8,128)(2,1)}, bf16[768,768]{1,0:T(8,128)(2,1)S(1)}, u32[]{:S(2)}) copy-start(bf16[768,768]{1,0:T(8,128)(2,1)S(1)} %fusion.pick_ref) | copy-start | bytes 3538948
  1.9 2.8 %copy-start = (bf16[1,2048,1536]{2,1,0:T(8,128)(2,1)S(1)}, bf16[1,2048,1536]{2,1,0:T(8,128)(2,1)}, u32[]{:S(2)}) copy-start(bf16[1,2048,1536]{2,1,0:T(8,128)(2,1)} %param.11) | copy-start | bytes 18874372
  4.6 1.9 copy-start.1
  6.5 1.2 copy-start.9
  7.8 0.7 copy-start.22
  9.1 0.7 copy-start.25
  9.8 0.7 copy-start.26
  14.7 3.4 %collective-permute-start = (bf16[2,576,256]{2,1,0:T(8,128)(2,1)S(1)}, bf16[2,576,256]{2,1,0:T(8,128)(2,1)S(1)}, u32[]{:S(2)}, u32[]{:S(2)}) collective-permute-start(bf16[2,576,256]{2,1,0:T(8,128)(2,1)S(1)} %slice_bitcast_fusion.7), channel_id=1, source_target_pairs={{0,1},{1,0},{2,3},{3,2},{4,5},{5,4},{6,7},{7,6},{8,9},{9,8},{10,11... | collective-permute-start | bytes 1769480 | tf_op jit(solution)/shard_map/ppermute | solution.py:24
  19.3 8.6 %collective-permute-start.1 = (bf16[576,256]{1,0:T(8,128)(2,1)S(1)}, bf16[576,256]{1,0:T(8,128)(2,1)S(1)}, u32[]{:S(2)}, u32[]{:S(2)}) collective-permute-start(bf16[576,256]{1,0:T(8,128)(2,1)S(1)} %slice_bitcast_fusion.14), channel_id=1, source_target_pairs={{0,2},{1,3},{2,0},{3,1},{4,6},{5,7},{6,4},{7,5},{8,10},{9,11},{10,... | collective-permute-start | bytes 884744 | tf_op jit(solution)/shard_map/ppermute | solution.py:24
  28.6 10.6 %collective-permute-start.2 = (bf16[576,256]{1,0:T(8,128)(2,1)}, bf16[576,256]{1,0:T(8,128)(2,1)S(1)}, u32[]{:S(2)}, u32[]{:S(2)}) collective-permute-start(bf16[576,256]{1,0:T(8,128)(2,1)} %fusion.4), channel_id=1, source_target_pairs={{0,4},{1,5},{2,6},{3,7},{4,8},{5,9},{6,10},{7,11},{8,12},{9,13},{1... | collective-permute-start | bytes 884744 | tf_op jit(solution)/shard_map/ppermute | solution.py:24
  30.4 16.1 %collective-permute-start.3 = (bf16[576,256]{1,0:T(8,128)(2,1)}, bf16[576,256]{1,0:T(8,128)(2,1)}, u32[]{:S(2)}, u32[]{:S(2)}) collective-permute-start(bf16[576,256]{1,0:T(8,128)(2,1)} %fusion.4), channel_id=1, source_target_pairs={{0,8},{1,9},{2,10},{3,11},{4,12},{5,13},{6,14},{7,15},{8,0},{9,1},... | collective-permute-start | bytes 884744 | tf_op jit(solution)/shard_map/ppermute | solution.py:24
  33.7 12.8 %collective-permute-start.4 = (bf16[576,256]{1,0:T(8,128)(2,1)}, bf16[576,256]{1,0:T(8,128)(2,1)}, u32[]{:S(2)}, u32[]{:S(2)}) collective-permute-start(bf16[576,256]{1,0:T(8,128)(2,1)} %fusion.4), channel_id=1, source_target_pairs={{0,12},{1,13},{2,14},{3,15},{4,0},{5,1},{6,2},{7,3},{8,4},{9,5},{1... | collective-permute-start | bytes 884744 | tf_op jit(solution)/shard_map/ppermute | solution.py:24
  34.4 23.8 %copy-start.10 = (bf16[256,2048]{1,0:T(8,128)(2,1)S(1)}, bf16[256,2048]{1,0:T(8,128)(2,1)}, u32[]{:S(2)}) copy-start(bf16[256,2048]{1,0:T(8,128)(2,1)} %cot_ref.3) | copy-start | bytes 3145732
  34.5 23.8 %copy-start.23 = (f32[256,2]{0,1:T(2,128)S(1)}, f32[256,2]{0,1:T(2,128)}, u32[]{:S(2)}) copy-start(f32[256,2]{0,1:T(2,128)} %param.10) | copy-start | bytes 6148
  34.5 23.8 %collective-permute-start.6 = (bf16[160,2048]{1,0:T(8,128)(2,1)S(1)}, bf16[160,2048]{1,0:T(8,128)(2,1)S(1)}, u32[]{:S(2)}, u32[]{:S(2)}) collective-permute-start(bf16[160,2048]{1,0:T(8,128)(2,1)S(1)} %keep_rows.1.own_ref), channel_id=1, source_target_pairs={{0,2},{1,3},{2,0},{3,1},{4,6},{5,7},{6,4},{7,5},{8,10},{9,11},{10,... | collective-permute-start | bytes 1966088 | tf_op jit(solution)/shard_map/ppermute | solution.py:24
  47.5 10.7 %collective-permute-start.5 = (bf16[576,256]{1,0:T(8,128)(2,1)S(1)}, bf16[576,256]{1,0:T(8,128)(2,1)S(1)}, u32[]{:S(2)}, u32[]{:S(2)}) collective-permute-start(bf16[576,256]{1,0:T(8,128)(2,1)S(1)} %select_select_fusion), channel_id=1, source_target_pairs={{0,64},{1,65},{2,66},{3,67},{4,68},{5,69},{6,70},{7,71},{8,72},{9,... | collective-permute-start | bytes 884744 | tf_op jit(solution)/shard_map/ppermute | solution.py:24
  61.4 39.1 %all-to-all-start = ((bf16[16,40,2048]{2,1,0:T(8,128)(2,1)}), bf16[16,40,2048]{2,1,0:T(8,128)(2,1)}, u32[]{:S(2)}, u32[]{:S(2)}) async-start(bf16[16,40,2048]{2,1,0:T(8,128)(2,1)} %bitcast.18), calls=%async_computation | async-start | bytes 5242880 | tf_op jit(solution)/shard_map/all_to_all | solution.py:368
  68.8 30.4 %collective-permute-start.7 = (bf16[2,160,2048]{2,1,0:T(8,128)(2,1)}, bf16[2,160,2048]{2,1,0:T(8,128)(2,1)}, u32[]{:S(2)}, u32[]{:S(2)}) collective-permute-start(bf16[2,160,2048]{2,1,0:T(8,128)(2,1)} %pad_maximum_fusion), channel_id=1, source_target_pairs={{0,1},{1,0},{2,3},{3,2},{4,5},{5,4},{6,7},{7,6},{8,9},{9,8},{10,11... | collective-permute-start | bytes 3932168 | tf_op jit(solution)/shard_map/ppermute | solution.py:24
  69.0 27.7 %collective-permute-start.10 = (bf16[2,576,256]{2,1,0:T(8,128)(2,1)S(1)}, bf16[2,576,256]{2,1,0:T(8,128)(2,1)S(1)}, u32[]{:S(2)}, u32[]{:S(2)}) collective-permute-start(bf16[2,576,256]{2,1,0:T(8,128)(2,1)S(1)} %pad_maximum_fusion.1.refs_0_.w0_ref), channel_id=1, source_target_pairs={{0,48},{1,49},{2,50},{3,51},{4,52},{5,53},{6,54},{7,55},{8,56},{9,... | collective-permute-start | bytes 1769480 | tf_op jit(solution)/shard_map/ppermute | solution.py:24
  71.8 25.0 %collective-permute-start.8 = (bf16[2,576,256]{2,1,0:T(8,128)(2,1)S(1)}, bf16[2,576,256]{2,1,0:T(8,128)(2,1)S(1)}, u32[]{:S(2)}, u32[]{:S(2)}) collective-permute-start(bf16[2,576,256]{2,1,0:T(8,128)(2,1)S(1)} %pad_maximum_fusion.1.refs_0_.w0_ref), channel_id=1, source_target_pairs={{0,16},{1,17},{2,18},{3,19},{4,20},{5,21},{6,22},{7,23},{8,24},{9,... | collective-permute-start | bytes 1769480 | tf_op jit(solution)/shard_map/ppermute | solution.py:24
  71.8 27.4 %collective-permute-start.9 = (bf16[2,576,256]{2,1,0:T(8,128)(2,1)S(1)}, bf16[2,576,256]{2,1,0:T(8,128)(2,1)}, u32[]{:S(2)}, u32[]{:S(2)}) collective-permute-start(bf16[2,576,256]{2,1,0:T(8,128)(2,1)S(1)} %pad_maximum_fusion.1.refs_0_.w0_ref), channel_id=1, source_target_pairs={{0,32},{1,33},{2,34},{3,35},{4,36},{5,37},{6,38},{7,39},{8,40},{9,... | collective-permute-start | bytes 1769480 | tf_op jit(solution)/shard_map/ppermute | solution.py:24
  96.8 0.8 copy-start.20
  100.5 1.1 copy-start.21
  109.2 4.5 %collective-permute-start.14 = (bf16[2,160,2048]{2,1,0:T(8,128)(2,1)}, bf16[2,160,2048]{2,1,0:T(8,128)(2,1)S(1)}, u32[]{:S(2)}, u32[]{:S(2)}) collective-permute-start(bf16[2,160,2048]{2,1,0:T(8,128)(2,1)} %get-tuple-element.42), channel_id=1, source_target_pairs={{0,1},{1,0},{2,3},{3,2},{4,5},{5,4},{6,7},{7,6},{8,9},{9,8},{10,11... | collective-permute-start | bytes 3932168 | tf_op jit(solution)/shard_map/ppermute | solution.py:24
  115.6 1.1 copy-start.4
  116.7 16.6 %collective-permute-start.15 = (bf16[160,2048]{1,0:T(8,128)(2,1)S(1)}, bf16[160,2048]{1,0:T(8,128)(2,1)S(1)}, u32[]{:S(2)}, u32[]{:S(2)}) collective-permute-start(bf16[160,2048]{1,0:T(8,128)(2,1)S(1)} %slice_bitcast_fusion.6), channel_id=1, source_target_pairs={{0,2},{1,3},{2,0},{3,1},{4,6},{5,7},{6,4},{7,5},{8,10},{9,11},{10,... | collective-permute-start | bytes 1966088 | tf_op jit(solution)/shard_map/ppermute | solution.py:24
  118.2 27.8 %collective-permute-start.11 = (bf16[2,4,144,256]{3,2,1,0:T(8,128)(2,1)S(1)}, bf16[2,4,144,256]{3,2,1,0:T(8,128)(2,1)S(1)}, u32[]{:S(2)}, u32[]{:S(2)}) collective-permute-start(bf16[2,4,144,256]{3,2,1,0:T(8,128)(2,1)S(1)} %get-tuple-element.36), channel_id=1, source_target_pairs={{0,4},{1,5},{2,6},{3,7},{4,8},{5,9},{6,10},{7,11},{8,12},{9,13},{1... | collective-permute-start | bytes 1769480 | tf_op jit(solution)/shard_map/ppermute | solution.py:24
  119.5 28.7 %collective-permute-start.12 = (bf16[2,4,144,256]{3,2,1,0:T(8,128)(2,1)S(1)}, bf16[2,4,144,256]{3,2,1,0:T(8,128)(2,1)S(1)}, u32[]{:S(2)}, u32[]{:S(2)}) collective-permute-start(bf16[2,4,144,256]{3,2,1,0:T(8,128)(2,1)S(1)} %get-tuple-element.37), channel_id=1, source_target_pairs={{0,8},{1,9},{2,10},{3,11},{4,12},{5,13},{6,14},{7,15},{8,0},{9,1},... | collective-permute-start | bytes 1769480 | tf_op jit(solution)/shard_map/ppermute | solution.py:24
  121.9 26.2 %collective-permute-start.13 = (bf16[2,4,144,256]{3,2,1,0:T(8,128)(2,1)S(1)}, bf16[2,4,144,256]{3,2,1,0:T(8,128)(2,1)S(1)}, u32[]{:S(2)}, u32[]{:S(2)}) collective-permute-start(bf16[2,4,144,256]{3,2,1,0:T(8,128)(2,1)S(1)} %get-tuple-element.38), channel_id=1, source_target_pairs={{0,12},{1,13},{2,14},{3,15},{4,0},{5,1},{6,2},{7,3},{8,4},{9,5},{1... | collective-permute-start | bytes 1769480 | tf_op jit(solution)/shard_map/ppermute | solution.py:24
  132.2 1.1 copy-start.14
  133.3 9.4 %copy-start.11 = (bf16[160,2048]{1,0:T(8,128)(2,1)}, bf16[160,2048]{1,0:T(8,128)(2,1)S(1)}, u32[]{:S(2)}) copy-start(bf16[160,2048]{1,0:T(8,128)(2,1)S(1)} %collective-permute-done.15.refs_0_.hot_b_ref) | copy-start | bytes 1966084
  142.7 0.9 copy-start.16
  143.6 0.9 copy-start.18
  144.5 48.7 %collective-permute-start.28 = (bf16[2,2,256,768]{3,2,1,0:T(8,128)(2,1)}, bf16[2,2,256,768]{3,2,1,0:T(8,128)(2,1)}, u32[]{:S(2)}, u32[]{:S(2)}) collective-permute-start(bf16[2,2,256,768]{3,2,1,0:T(8,128)(2,1)} %get-tuple-element.50), channel_id=1, source_target_pairs={{0,48},{1,49},{2,50},{3,51},{4,52},{5,53},{6,54},{7,55},{8,56},{9,... | collective-permute-start | bytes 4718600 | tf_op jit(solution)/shard_map/ppermute | solution.py:24
  145.8 49.2 %collective-permute-start.26 = (bf16[2,2,256,768]{3,2,1,0:T(8,128)(2,1)}, bf16[2,2,256,768]{3,2,1,0:T(8,128)(2,1)}, u32[]{:S(2)}, u32[]{:S(2)}) collective-permute-start(bf16[2,2,256,768]{3,2,1,0:T(8,128)(2,1)} %get-tuple-element.49), channel_id=1, source_target_pairs={{0,16},{1,17},{2,18},{3,19},{4,20},{5,21},{6,22},{7,23},{8,24},{9,... | collective-permute-start | bytes 4718600 | tf_op jit(solution)/shard_map/ppermute | solution.py:24
  146.0 55.1 %collective-permute-start.23 = (bf16[4,96,2048]{2,1,0:T(8,128)(2,1)}, bf16[4,96,2048]{2,1,0:T(8,128)(2,1)}, u32[]{:S(2)}, u32[]{:S(2)}) collective-permute-start(bf16[4,96,2048]{2,1,0:T(8,128)(2,1)} %get-tuple-element.47), channel_id=1, source_target_pairs={{0,64},{1,65},{2,66},{3,67},{4,68},{5,69},{6,70},{7,71},{8,72},{9,... | collective-permute-start | bytes 4718600 | tf_op jit(solution)/shard_map/ppermute | solution.py:24
  148.2 1.4 copy-start.6
  149.9 38.2 %collective-permute-start.16 = (bf16[4,144,256]{2,1,0:T(8,128)(2,1)S(1)}, bf16[4,144,256]{2,1,0:T(8,128)(2,1)}, u32[]{:S(2)}, u32[]{:S(2)}) collective-permute-start(bf16[4,144,256]{2,1,0:T(8,128)(2,1)S(1)} %slice_bitcast_fusion.12), channel_id=1, source_target_pairs={{0,64},{1,65},{2,66},{3,67},{4,68},{5,69},{6,70},{7,71},{8,72},{9,... | collective-permute-start | bytes 884744 | tf_op jit(solution)/shard_map/ppermute | solution.py:24
  163.5 54.0 %all-to-all-start.1 = ((bf16[16,40,2048]{2,1,0:T(8,128)(2,1)}), bf16[16,40,2048]{2,1,0:T(8,128)(2,1)S(1)}, u32[]{:S(2)}, u32[]{:S(2)}) async-start(bf16[16,40,2048]{2,1,0:T(8,128)(2,1)} %bitcast.24), calls=%async_computation.1 | async-start | bytes 5242880 | tf_op jit(solution)/shard_map/all_to_all | solution.py:419
  189.1 7.8 %collective-permute-start.17 = (bf16[144,256]{1,0:T(8,128)(2,1)S(1)}, bf16[144,256]{1,0:T(8,128)(2,1)S(1)}, u32[]{:S(2)}, u32[]{:S(2)}) collective-permute-start(bf16[144,256]{1,0:T(8,128)(2,1)S(1)} %get-tuple-element.64), channel_id=1, source_target_pairs={{0,16},{1,17},{2,18},{3,19},{4,20},{5,21},{6,22},{7,23},{8,24},{9,... | collective-permute-start | bytes 221192 | tf_op jit(solution)/shard_map/ppermute | solution.py:24
  189.5 9.0 %collective-permute-start.18 = (bf16[144,256]{1,0:T(8,128)(2,1)S(1)}, bf16[144,256]{1,0:T(8,128)(2,1)S(1)}, u32[]{:S(2)}, u32[]{:S(2)}) collective-permute-start(bf16[144,256]{1,0:T(8,128)(2,1)S(1)} %get-tuple-element.66), channel_id=1, source_target_pairs={{0,32},{1,33},{2,34},{3,35},{4,36},{5,37},{6,38},{7,39},{8,40},{9,... | collective-permute-start | bytes 221192 | tf_op jit(solution)/shard_map/ppermute | solution.py:24
  193.1 1.6 copy-start.19
  193.1 5.4 %collective-permute-start.19 = (bf16[144,256]{1,0:T(8,128)(2,1)S(1)}, bf16[144,256]{1,0:T(8,128)(2,1)S(1)}, u32[]{:S(2)}, u32[]{:S(2)}) collective-permute-start(bf16[144,256]{1,0:T(8,128)(2,1)S(1)} %get-tuple-element.65), channel_id=1, source_target_pairs={{0,48},{1,49},{2,50},{3,51},{4,52},{5,53},{6,54},{7,55},{8,56},{9,... | collective-permute-start | bytes 221192 | tf_op jit(solution)/shard_map/ppermute | solution.py:24
  194.9 1.8 copy-start.17
  195.0 16.6 %collective-permute-start.29 = (bf16[2,256,768]{2,1,0:T(8,128)(2,1)S(1)}, bf16[2,256,768]{2,1,0:T(8,128)(2,1)S(1)}, u32[]{:S(2)}, u32[]{:S(2)}) collective-permute-start(bf16[2,256,768]{2,1,0:T(8,128)(2,1)S(1)} %sum_down.1), channel_id=1, source_target_pairs={{0,48},{1,49},{2,50},{3,51},{4,52},{5,53},{6,54},{7,55},{8,56},{9,... | collective-permute-start | bytes 2359304 | tf_op jit(solution)/shard_map/ppermute | solution.py:24
  196.8 5.3 %copy-start.28 = (bf16[4,96,2048]{2,1,0:T(8,128)(2,1)S(1)}, bf16[4,96,2048]{2,1,0:T(8,128)(2,1)}, u32[]{:S(2)}) copy-start(bf16[4,96,2048]{2,1,0:T(8,128)(2,1)} %get-tuple-element.46) | copy-start | bytes 4718596
  197.0 15.2 %collective-permute-start.27 = (bf16[2,256,768]{2,1,0:T(8,128)(2,1)S(1)}, bf16[2,256,768]{2,1,0:T(8,128)(2,1)S(1)}, u32[]{:S(2)}, u32[]{:S(2)}) collective-permute-start(bf16[2,256,768]{2,1,0:T(8,128)(2,1)S(1)} %sum_up.1), channel_id=1, source_target_pairs={{0,16},{1,17},{2,18},{3,19},{4,20},{5,21},{6,22},{7,23},{8,24},{9,... | collective-permute-start | bytes 2359304 | tf_op jit(solution)/shard_map/ppermute | solution.py:24
  198.6 15.3 %collective-permute-start.20 = (bf16[144,256]{1,0:T(8,128)(2,1)S(1)}, bf16[144,256]{1,0:T(8,128)(2,1)S(1)}, u32[]{:S(2)}, u32[]{:S(2)}) collective-permute-start(bf16[144,256]{1,0:T(8,128)(2,1)S(1)} %fusion.7.refs_0_), channel_id=1, source_target_pairs={{0,4},{1,5},{2,6},{3,7},{4,8},{5,9},{6,10},{7,11},{8,12},{9,13},{1... | collective-permute-start | bytes 221192 | tf_op jit(solution)/shard_map/ppermute | solution.py:24
  198.6 15.2 %collective-permute-start.21 = (bf16[144,256]{1,0:T(8,128)(2,1)S(1)}, bf16[144,256]{1,0:T(8,128)(2,1)S(1)}, u32[]{:S(2)}, u32[]{:S(2)}) collective-permute-start(bf16[144,256]{1,0:T(8,128)(2,1)S(1)} %fusion.7.refs_0_), channel_id=1, source_target_pairs={{0,8},{1,9},{2,10},{3,11},{4,12},{5,13},{6,14},{7,15},{8,0},{9,1},... | collective-permute-start | bytes 221192 | tf_op jit(solution)/shard_map/ppermute | solution.py:24
  201.1 12.8 %collective-permute-start.22 = (bf16[144,256]{1,0:T(8,128)(2,1)S(1)}, bf16[144,256]{1,0:T(8,128)(2,1)S(1)}, u32[]{:S(2)}, u32[]{:S(2)}) collective-permute-start(bf16[144,256]{1,0:T(8,128)(2,1)S(1)} %fusion.7.refs_0_), channel_id=1, source_target_pairs={{0,12},{1,13},{2,14},{3,15},{4,0},{5,1},{6,2},{7,3},{8,4},{9,5},{1... | collective-permute-start | bytes 221192 | tf_op jit(solution)/shard_map/ppermute | solution.py:24
  202.0 10.1 %copy-start.7 = (bf16[2,256,1536]{2,1,0:T(8,128)(2,1)S(1)}, bf16[2,256,1536]{2,1,0:T(8,128)(2,1)}, u32[]{:S(2)}) copy-start(bf16[2,256,1536]{2,1,0:T(8,128)(2,1)} %get-tuple-element.43.refs_4_) | copy-start | bytes 4718596
  217.5 1.4 copy-start.2
  218.9 1.4 copy-start.27
  218.9 5.7 %collective-permute-start.24 = (bf16[4,144,256]{2,1,0:T(8,128)(2,1)S(1)}, bf16[4,144,256]{2,1,0:T(8,128)(2,1)S(1)}, u32[]{:S(2)}, u32[]{:S(2)}) collective-permute-start(bf16[4,144,256]{2,1,0:T(8,128)(2,1)S(1)} %stack_z.1), channel_id=1, source_target_pairs={{0,2},{1,3},{2,0},{3,1},{4,6},{5,7},{6,4},{7,5},{8,10},{9,11},{10,... | collective-permute-start | bytes 884744 | tf_op jit(solution)/shard_map/ppermute | solution.py:24
  221.3 33.7 %collective-permute-start.30 = (bf16[256,1536]{1,0:T(8,128)(2,1)}, bf16[256,1536]{1,0:T(8,128)(2,1)}, u32[]{:S(2)}, u32[]{:S(2)}) collective-permute-start(bf16[256,1536]{1,0:T(8,128)(2,1)} %get-tuple-element.58), channel_id=1, source_target_pairs={{0,64},{1,65},{2,66},{3,67},{4,68},{5,69},{6,70},{7,71},{8,72},{9,... | collective-permute-start | bytes 2359304 | tf_op jit(solution)/shard_map/ppermute | solution.py:24
  225.5 29.5 %collective-permute-start.25 = (bf16[2,4,144,256]{3,2,1,0:T(8,128)(2,1)}, bf16[2,4,144,256]{3,2,1,0:T(8,128)(2,1)}, u32[]{:S(2)}, u32[]{:S(2)}) collective-permute-start(bf16[2,4,144,256]{3,2,1,0:T(8,128)(2,1)} %pad_maximum_fusion.2.spare_ref), channel_id=1, source_target_pairs={{0,1},{1,0},{2,3},{3,2},{4,5},{5,4},{6,7},{7,6},{8,9},{9,8},{10,11... | collective-permute-start | bytes 1769480 | tf_op jit(solution)/shard_map/ppermute | solution.py:24
  234.0 12.5 %collective-permute-start.31 = (bf16[96,2048]{1,0:T(8,128)(2,1)}, bf16[96,2048]{1,0:T(8,128)(2,1)}, u32[]{:S(2)}, u32[]{:S(2)}) collective-permute-start(bf16[96,2048]{1,0:T(8,128)(2,1)} %get-tuple-element.56), channel_id=1, source_target_pairs={{0,16},{1,17},{2,18},{3,19},{4,20},{5,21},{6,22},{7,23},{8,24},{9,... | collective-permute-start | bytes 1179656 | tf_op jit(solution)/shard_map/ppermute | solution.py:24
  234.5 20.0 %collective-permute-start.32 = (bf16[96,2048]{1,0:T(8,128)(2,1)}, bf16[96,2048]{1,0:T(8,128)(2,1)}, u32[]{:S(2)}, u32[]{:S(2)}) collective-permute-start(bf16[96,2048]{1,0:T(8,128)(2,1)} %get-tuple-element.55), channel_id=1, source_target_pairs={{0,32},{1,33},{2,34},{3,35},{4,36},{5,37},{6,38},{7,39},{8,40},{9,... | collective-permute-start | bytes 1179656 | tf_op jit(solution)/shard_map/ppermute | solution.py:24
  236.4 18.6 %collective-permute-start.33 = (bf16[96,2048]{1,0:T(8,128)(2,1)}, bf16[96,2048]{1,0:T(8,128)(2,1)}, u32[]{:S(2)}, u32[]{:S(2)}) collective-permute-start(bf16[96,2048]{1,0:T(8,128)(2,1)} %get-tuple-element.54), channel_id=1, source_target_pairs={{0,48},{1,49},{2,50},{3,51},{4,52},{5,53},{6,54},{7,55},{8,56},{9,... | collective-permute-start | bytes 1179656 | tf_op jit(solution)/shard_map/ppermute | solution.py:24
  238.3 1.3 copy-start.5
  239.6 1.1 copy-start.12
  240.7 14.2 %copy-start.13 = (bf16[96,2048]{1,0:T(8,128)(2,1)S(1)}, bf16[96,2048]{1,0:T(8,128)(2,1)}, u32[]{:S(2)}) copy-start(bf16[96,2048]{1,0:T(8,128)(2,1)} %get-tuple-element.57.d0_ref) | copy-start | bytes 1179652
  255.0 1.2 copy-start.15
  (1 other events, 0.7 us)

commit v3 on v2

--- a/solution.py
+++ b/solution.py
@@ -398,16 +398,17 @@
         (recv, pick_x, pick_g, w_in, w_out, spares[0]),
         in_specs=[VMEM] * 5 + [AFTER],
     )
+    from_z = [hop(spares[s], dz=s) for s in (1, 2, 3)]
     half = shape(2, 256, 768)
     in_own, up_a, dn_b, to_up, to_dn, out_own, out_far = call(
         grads_kernel,
         "home_grads",
         (shape(2, 256, 1536),) + (half,) * 2 + (shape(2, 2, 256, 768),) * 2 + (shape(4, 96, 2048),) * 2,
-        (here, active, grad_hidden, rows_x, rows_g, near_part),
-        in_specs=[SMEM] + [VMEM] * 4 + [AFTER],
+        (here, active, grad_hidden, rows_x, rows_g, near_part, from_z[0], from_z[2]),
+        in_specs=[SMEM] + [VMEM] * 4 + [AFTER] * 3,
     )
     spare = sum_after(
-        [spares[0]] + [hop(spares[s], dz=s) for s in (1, 2, 3)], [in_own], "sum_z"
+        [spares[0]] + from_z, [in_own], "sum_z"
     )
     (result,) = call(
         result_kernel,
@@ -417,11 +418,21 @@
         in_specs=[VMEM] * 6 + [AFTER],
     )
     returned = lax.all_to_all(result, "expert", split_axis=0, concat_axis=0, tiled=True)
-    spare = total(spare[0], hop(spare[1], dh=1))
-    spare = total(spare[0], *[hop(spare[s], dy=s) for s in (1, 2, 3)])
 
     from_dn, from_up = hop(to_up, dy=1), hop(to_dn, dy=3)
     out_sum = total(out_own, hop(out_far, dh=1))
+    up_a = sum_after([up_a, from_dn[0]], [result], "sum_up")
+    dn_b = sum_after([dn_b, from_up[1]], [result], "sum_down")
+    spare = sum_after([spare[0], hop(spare[1], dh=1)], [up_a, dn_b], "sum_x")
+    up_a, dn_b = hop(up_a, dy=1), hop(dn_b, dy=3)
+    up_b, dn_a = from_dn[1], from_up[0]
+    in_sum = total(
+        in_own, jnp.concatenate([up_a, up_b], axis=2), jnp.concatenate([dn_a, dn_b], axis=2)
+    )
+    in_got = hop(in_sum[1], dh=1)
+    out_parts = [out_sum[0]] + [hop(out_sum[s], dy=s) for s in (1, 2, 3)]
+    spare = total(spare[0], *[hop(spare[s], dy=s) for s in (1, 2, 3)])
+
     mixed, token_grad = call(
         unpack_kernel,
         "unpack_rows",
@@ -433,20 +444,11 @@
         stack_kernel,
         "stack_z",
         (shape(4, 144, 256),),
-        (spare, *[hop(spare, dz=s) for s in (1, 2, 3)], returned, out_sum),
-        in_specs=[VMEM] * 4 + [AFTER] * 2,
+        (spare, *[hop(spare, dz=s) for s in (1, 2, 3)], returned, in_got, *out_parts),
+        in_specs=[VMEM] * 4 + [AFTER] * 6,
     )
     spare = jnp.stack([spare, hop(spare, dl=1)])
     more = hop(spare, dc=1)
-    up_a = hop(sum_after([up_a, from_dn[0]], [result], "sum_up"), dy=1)
-    dn_b = hop(sum_after([dn_b, from_up[1]], [result], "sum_down"), dy=3)
-    up_b, dn_a = from_dn[1], from_up[0]
-    in_sum = total(
-        in_own, jnp.concatenate([up_a, up_b], axis=2), jnp.concatenate([dn_a, dn_b], axis=2)
-    )
-    in_got = hop(in_sum[1], dh=1)
-    out_parts = [out_sum[0]] + [hop(out_sum[s], dy=s) for s in (1, 2, 3)]
-
     grad_gate_up, grad_down = call(
         finish_kernel,
         "finish_grads",

time: 262 us -> 263 us (level)
  waiting for transfers between devices: 92.6 us -> 97.8 us
  other arithmetic: 13.7 us -> 9.71 us
    ppermute x34, waiting for transfers between devices: 87.6 us -> 96.4 us  [hop(): return lax.ppermute(x, AXES, pairs)]
    all_to_all x1, waiting for transfers between devices: 3.66 us -> 0.01 us  [shards(): lax.all_to_all(result, 'expert', split_axis=0, concat_axis=0, tiled=True)]
    convert_element_type x5 -> x4, other arithmetic: 7.92 us -> 4.57 us  [total(): return out.astype(dtype)]
    unnamed x59 -> x79, local copies, waits for them, and re-layouts: 22.4 us -> 25.3 us
    pallas_call x12 -> x13, Pallas kernels: 51.1 us -> 50.8 us  [call(): pl.pallas_call(kernel, out_shape=outs, in_specs=in_specs or [VMEM] * len(...]
  transfers between devices with their start and end apart: 36 -> 36, of which waited for: 16 -> 16; matrix products, arithmetic and copies ran while one was open for 6% -> 4% of each run, Pallas kernels for 14% -> 10%
where the time goes in v3:
time: 263 us; the launch traced here: 262 us
  waiting for transfers between devices  97.8 us (37%)
  starting transfers between devices  65.7 us (25%)
  Pallas kernels  53.8 us (20%)
  local copies, waits for them, and re-layouts  31.1 us (12%)
  other arithmetic  9.71 us (4%)
  between operations  4.11 us (2%)
    ppermute x34, waiting for transfers between devices, hop(): return lax.ppermute(x, AXES, pairs)  96.4 us
    ppermute x34, starting transfers between devices, hop(): return lax.ppermute(x, AXES, pairs)  52 us
    pallas_call x13, Pallas kernels, call(): pl.pallas_call(kernel, out_shape=outs, in_specs=in_specs or [VMEM] * len(...  50.8 us
    unnamed x79, local copies, waits for them, and re-layouts  25.3 us
    all_to_all x1, starting transfers between devices, shards(): lax.all_to_all(result, 'expert', split_axis=0, concat_axis=0, tiled=True)  7.08 us
    all_to_all x1, starting transfers between devices, shards(): lax.all_to_all(send, 'expert', split_axis=0, concat_axis=0, tiled=True)  6.62 us
  transfers between devices with their start and end apart: 36, of which 16 were waited for; matrix products, arithmetic and copies ran while one was open for 4% of the time, Pallas kernels for 10%

profile of v3, /device:TPU:1, one launch (start us, length us, event | category | flops | bytes accessed | tf_op | source)
XLA Modules:
  0.0 262.3 jit_solution(809894992019883046)
XLA Ops:
  1.9 2.8 %copy-done = bf16[1,2048,1536]{2,1,0:T(8,128)(2,1)S(1)} copy-done((bf16[1,2048,1536]{2,1,0:T(8,128)(2,1)S(1)}, bf16[1,2048,1536]{2,1,0:T(8,128)(2,1)}, u32[]{:S(2)}) %copy-start) | copy-done | bytes 6291480
  4.6 1.9 copy-done.1
  6.5 1.2 copy-done.8
  10.5 3.0 %route.1 = (bf16[2,2,576,256]{3,2,1,0:T(8,128)(2,1)}, bf16[160,2048]{1,0:T(8,128)(2,1)S(1)}, s32[2,256]{1,0:T(2,128)S(1)}, s32[1,1]{1,0:T(1,128)}) custom-call(s32[5]{0:T(128)S(1)} %stack.50.here_ref, s32[2,256]{1,0:T(2,128)S(1)} %bitcast.85, s32[2,256]{1,0:T(2,128)S(1)} %bitcast.86, s32[2,256]{1,0:T(2,128)S(1)} %bitcast.87, f32[2,256]{1,0:T(2,128)S(1)} %bitcast.83, ...), custom_call_target="tpu_custom_call" | custom-call | flops 1000000 | bytes 100000 | tf_op jit(solution)/shard_map/route/pallas_call | solution.py:127
  13.6 1.1 slice_bitcast_fusion.7
  14.7 1.5 collective-permute-start
  17.9 1.1 bitcast_select_fusion
  19.1 1.4 collective-permute-start.1
  21.1 6.4 %collective-permute-done.1.refs_1_ = bf16[576,256]{1,0:T(8,128)(2,1)S(1)} collective-permute-done((bf16[576,256]{1,0:T(8,128)(2,1)S(1)}, bf16[576,256]{1,0:T(8,128)(2,1)S(1)}, u32[]{:S(2)}, u32[]{:S(2)}) %collective-permute-start.1) | collective-permute-done | bytes 294944 | tf_op jit(solution)/shard_map/ppermute | solution.py:24
  27.5 1.8 collective-permute-start.2
  29.3 3.3 %collective-permute-start.3 = (bf16[576,256]{1,0:T(8,128)(2,1)S(1)}, bf16[576,256]{1,0:T(8,128)(2,1)}, u32[]{:S(2)}, u32[]{:S(2)}) collective-permute-start(bf16[576,256]{1,0:T(8,128)(2,1)S(1)} %fusion.3), channel_id=1, source_target_pairs={{0,8},{1,9},{2,10},{3,11},{4,12},{5,13},{6,14},{7,15},{8,0},{9,1},... | collective-permute-start | bytes 884744 | tf_op jit(solution)/shard_map/ppermute | solution.py:24
  33.4 1.3 collective-permute-start.6
  34.7 3.0 %collective-permute-done.2 = bf16[576,256]{1,0:T(8,128)(2,1)S(1)} collective-permute-done((bf16[576,256]{1,0:T(8,128)(2,1)S(1)}, bf16[576,256]{1,0:T(8,128)(2,1)S(1)}, u32[]{:S(2)}, u32[]{:S(2)}) %collective-permute-start.2) | collective-permute-done | bytes 294944 | tf_op jit(solution)/shard_map/ppermute | solution.py:24
  37.7 7.3 %collective-permute-done.3 = bf16[576,256]{1,0:T(8,128)(2,1)} collective-permute-done((bf16[576,256]{1,0:T(8,128)(2,1)S(1)}, bf16[576,256]{1,0:T(8,128)(2,1)}, u32[]{:S(2)}, u32[]{:S(2)}) %collective-permute-start.3) | collective-permute-done | bytes 294944 | tf_op jit(solution)/shard_map/ppermute | solution.py:24
  46.0 2.8 %collective-permute-start.5 = (bf16[576,256]{1,0:T(8,128)(2,1)S(1)}, bf16[576,256]{1,0:T(8,128)(2,1)S(1)}, u32[]{:S(2)}, u32[]{:S(2)}) collective-permute-start(bf16[576,256]{1,0:T(8,128)(2,1)S(1)} %select_select_fusion), channel_id=1, source_target_pairs={{0,64},{1,65},{2,66},{3,67},{4,68},{5,69},{6,70},{7,71},{8,72},{9,... | collective-permute-start | bytes 884744 | tf_op jit(solution)/shard_map/ppermute | solution.py:24
  48.9 7.8 %collective-permute-done.5 = bf16[576,256]{1,0:T(8,128)(2,1)S(1)} collective-permute-done((bf16[576,256]{1,0:T(8,128)(2,1)S(1)}, bf16[576,256]{1,0:T(8,128)(2,1)S(1)}, u32[]{:S(2)}, u32[]{:S(2)}) %collective-permute-start.5) | collective-permute-done | bytes 294944 | tf_op jit(solution)/shard_map/ppermute | solution.py:24
  56.8 3.1 %pack_rows.1 = bf16[640,2048]{1,0:T(8,128)(2,1)} custom-call(s32[2,256]{1,0:T(2,128)S(1)} %get-tuple-element.29.pos_ref, f32[2,256]{1,0:T(2,128)S(1)} %bitcast.84, bf16[256,2048]{1,0:T(8,128)(2,1)S(1)} %copy-done.7, bf16[256,2048]{1,0:T(8,128)(2,1)S(1)} %copy-done.9, bf16[2,576,256]{2,1,0:T(8,128)(2,1)S(1)} %pad_maximum_fusion.1.refs_0_.w0_ref, ...), custom_call_target="tpu_custom_call" | custom-call | flops 1000000 | bytes 100000 | tf_op jit(solution)/shard_map/pack_rows/pallas_call | solution.py:44
  59.9 6.6 %all-to-all-start = ((bf16[16,40,2048]{2,1,0:T(8,128)(2,1)}), bf16[16,40,2048]{2,1,0:T(8,128)(2,1)}, u32[]{:S(2)}, u32[]{:S(2)}) async-start(bf16[16,40,2048]{2,1,0:T(8,128)(2,1)} %bitcast.18), calls=%async_computation | async-start | bytes 5242880 | tf_op jit(solution)/shard_map/all_to_all | solution.py:368
  66.6 1.2 pad_maximum_fusion
  68.0 2.7 %collective-permute-start.10 = (bf16[2,576,256]{2,1,0:T(8,128)(2,1)S(1)}, bf16[2,576,256]{2,1,0:T(8,128)(2,1)S(1)}, u32[]{:S(2)}, u32[]{:S(2)}) collective-permute-start(bf16[2,576,256]{2,1,0:T(8,128)(2,1)S(1)} %pad_maximum_fusion.1.refs_0_.w0_ref), channel_id=1, source_target_pairs={{0,48},{1,49},{2,50},{3,51},{4,52},{5,53},{6,54},{7,55},{8,56},{9,... | collective-permute-start | bytes 1769480 | tf_op jit(solution)/shard_map/ppermute | solution.py:24
  70.7 1.7 collective-permute-start.9
  73.0 22.7 %collective-permute-done.10.w3_ref = bf16[2,576,256]{2,1,0:T(8,128)(2,1)S(1)} collective-permute-done((bf16[2,576,256]{2,1,0:T(8,128)(2,1)S(1)}, bf16[2,576,256]{2,1,0:T(8,128)(2,1)S(1)}, u32[]{:S(2)}, u32[]{:S(2)}) %collective-permute-start.10) | collective-permute-done | bytes 589856 | tf_op jit(solution)/shard_map/ppermute | solution.py:24
  95.7 2.4 collective-permute-done.9.w2_ref
  98.1 1.4 all-to-all-done
  99.5 7.6 %hot_expert.1 = (bf16[2,160,2048]{2,1,0:T(8,128)(2,1)}, bf16[2,160,2048]{2,1,0:T(8,128)(2,1)}, bf16[2,4,144,256]{3,2,1,0:T(8,128)(2,1)S(1)}, bf16[2,4,144,256]{3...) custom-call(s32[6]{0:T(128)S(1)} %concatenate.10.here_ref, ...), custom_call_target="tpu_custom_call" | custom-call | flops 1000000 | bytes 100000 | tf_op jit(solution)/shard_map/hot_expert/pallas_call | solution.py:44
  107.9 2.9 %collective-permute-done.14 = bf16[2,160,2048]{2,1,0:T(8,128)(2,1)S(1)} collective-permute-done((bf16[2,160,2048]{2,1,0:T(8,128)(2,1)}, bf16[2,160,2048]{2,1,0:T(8,128)(2,1)S(1)}, u32[]{:S(2)}, u32[]{:S(2)}) %collective-permute-start.14) | collective-permute-done | bytes 1310752 | tf_op jit(solution)/shard_map/ppermute | solution.py:24
  110.8 1.8 add_convert_fusion.2.hot_a_ref
  113.7 1.5 collective-permute-start.15
  115.2 1.2 collective-permute-start.11
  116.4 1.5 collective-permute-start.13
  118.0 9.1 %home_hidden.1 = (bf16[320,768]{1,0:T(8,128)(2,1)S(1)}, bf16[320,1536]{1,0:T(8,128)(2,1)S(1)}, bf16[320,2048]{1,0:T(8,128)(2,1)S(1)}, bf16[320,2048]{1,0:T(8,128)(2,1)S(1)}) custom-call(bf16[640,2048]{1,0:T(8,128)(2,1)} %bitcast.19.after_ref.recv_ref, bf16[80,160]{1,0:T(8,128)(2,1)S(1)} %get-tuple-element.69.pick_x_ref, ...), custom_call_target="tpu_custom_call" | custom-call | flops 1000000 | bytes 100000 | tf_op jit(solution)/shard_map/home_hidden/pallas_call | solution.py:44
  128.1 2.5 collective-permute-done.11.refs_1_
  130.6 9.4 %home_grads.1 = (bf16[2,256,1536]{2,1,0:T(8,128)(2,1)}, bf16[2,256,768]{2,1,0:T(8,128)(2,1)S(1)}, bf16[2,256,768]{2,1,0:T(8,128)(2,1)S(1)}, bf16[2,2,256,768]{3,...) custom-call(s32[6]{0:T(128)S(1)} %concatenate.10.here_ref, ...), custom_call_target="tpu_custom_call" | custom-call | flops 1000000 | bytes 100000 | tf_op jit(solution)/shard_map/home_grads/pallas_call | solution.py:44
  140.9 1.7 collective-permute-start.18
  142.7 1.8 collective-permute-start.12
  144.5 2.0 collective-permute-start.28
  146.7 10.6 %collective-permute-done.12.refs_2_ = bf16[2,4,144,256]{3,2,1,0:T(8,128)(2,1)S(1)} collective-permute-done((bf16[2,4,144,256]{3,2,1,0:T(8,128)(2,1)S(1)}, bf16[2,4,144,256]{3,2,1,0:T(8,128)(2,1)S(1)}, u32[]{:S(2)}, u32[]{:S(2)}) %collective-permute-start.12) | collective-permute-done | bytes 589856 | tf_op jit(solution)/shard_map/ppermute | solution.py:24
  157.3 1.4 copy-done.5
  159.1 1.9 collective-permute-start.16
  160.9 12.1 %home_rows.1.refs_2_ = bf16[640,2048]{1,0:T(8,128)(2,1)} custom-call(bf16[320,768]{1,0:T(8,128)(2,1)S(1)} %get-tuple-element.34.act_ref, bf16[320,1536]{1,0:T(8,128)(2,1)S(1)} %get-tuple-element.35.gh_ref, bf16[320,640]{1,0:T(8,128)(2,1)S(1)} %get-tuple-element.71.pick_x_ref, bf16[320,640]{1,0:T(8,128)(2,1)S(1)} %get-tuple-element.72.pick_g_ref, ...), custom_call_target="tpu_custom_call" | custom-call | flops 1000000 | bytes 100000 | tf_op jit(solution)/shard_map/home_rows/pallas_call | solution.py:44
  173.0 7.1 %all-to-all-start.1 = ((bf16[16,40,2048]{2,1,0:T(8,128)(2,1)}), bf16[16,40,2048]{2,1,0:T(8,128)(2,1)S(1)}, u32[]{:S(2)}, u32[]{:S(2)}) async-start(bf16[16,40,2048]{2,1,0:T(8,128)(2,1)} %bitcast.24), calls=%async_computation.1 | async-start | bytes 5242880 | tf_op jit(solution)/shard_map/all_to_all | solution.py:420
  180.1 1.5 slice_bitcast_fusion.2
  181.9 2.8 %collective-permute-start.26 = (bf16[2,256,768]{2,1,0:T(8,128)(2,1)S(1)}, bf16[2,256,768]{2,1,0:T(8,128)(2,1)S(1)}, u32[]{:S(2)}, u32[]{:S(2)}) collective-permute-start(bf16[2,256,768]{2,1,0:T(8,128)(2,1)S(1)} %sum_down.1.refs_3_), channel_id=1, source_target_pairs={{0,48},{1,49},{2,50},{3,51},{4,52},{5,53},{6,54},{7,55},{8,56},{9,... | collective-permute-start | bytes 2359304 | tf_op jit(solution)/shard_map/ppermute | solution.py:24
  184.7 1.5 slice_bitcast_fusion.3
  186.6 3.8 %collective-permute-start.20 = (bf16[144,256]{1,0:T(8,128)(2,1)S(1)}, bf16[144,256]{1,0:T(8,128)(2,1)S(1)}, u32[]{:S(2)}, u32[]{:S(2)}) collective-permute-start(bf16[144,256]{1,0:T(8,128)(2,1)S(1)} %get-tuple-element.68), channel_id=1, source_target_pairs={{0,32},{1,33},{2,34},{3,35},{4,36},{5,37},{6,38},{7,39},{8,40},{9,... | collective-permute-start | bytes 221192 | tf_op jit(solution)/shard_map/ppermute | solution.py:24
  190.5 2.2 add_convert_fusion
  192.7 10.3 %collective-permute-done.26 = bf16[2,256,768]{2,1,0:T(8,128)(2,1)S(1)} collective-permute-done((bf16[2,256,768]{2,1,0:T(8,128)(2,1)S(1)}, bf16[2,256,768]{2,1,0:T(8,128)(2,1)S(1)}, u32[]{:S(2)}, u32[]{:S(2)}) %collective-permute-start.26) | collective-permute-done | bytes 786464 | tf_op jit(solution)/shard_map/ppermute | solution.py:24
  203.0 3.4 %collective-permute-done.25 = bf16[2,256,768]{2,1,0:T(8,128)(2,1)S(1)} collective-permute-done((bf16[2,256,768]{2,1,0:T(8,128)(2,1)S(1)}, bf16[2,256,768]{2,1,0:T(8,128)(2,1)S(1)}, u32[]{:S(2)}, u32[]{:S(2)}) %collective-permute-start.25) | collective-permute-done | bytes 786464 | tf_op jit(solution)/shard_map/ppermute | solution.py:24
  207.0 1.2 slice_bitcast_fusion
  208.2 2.2 collective-permute-start.27
  210.7 1.3 collective-permute-start.30
  212.0 1.4 collective-permute-start.31
  213.5 1.1 collective-permute-start.22
  214.6 4.5 %collective-permute-done.22.refs_1_ = bf16[144,256]{1,0:T(8,128)(2,1)S(1)} collective-permute-done((bf16[144,256]{1,0:T(8,128)(2,1)S(1)}, bf16[144,256]{1,0:T(8,128)(2,1)S(1)}, u32[]{:S(2)}, u32[]{:S(2)}) %collective-permute-start.22) | collective-permute-done | bytes 73760 | tf_op jit(solution)/shard_map/ppermute | solution.py:24
  219.0 1.3 collective-permute-start.23
  220.4 4.4 %collective-permute-done.23.refs_2_ = bf16[144,256]{1,0:T(8,128)(2,1)S(1)} collective-permute-done((bf16[144,256]{1,0:T(8,128)(2,1)S(1)}, bf16[144,256]{1,0:T(8,128)(2,1)S(1)}, u32[]{:S(2)}, u32[]{:S(2)}) %collective-permute-start.23) | collective-permute-done | bytes 73760 | tf_op jit(solution)/shard_map/ppermute | solution.py:24
  225.8 3.7 %collective-permute-done.24.refs_3_ = bf16[144,256]{1,0:T(8,128)(2,1)S(1)} collective-permute-done((bf16[144,256]{1,0:T(8,128)(2,1)S(1)}, bf16[144,256]{1,0:T(8,128)(2,1)S(1)}, u32[]{:S(2)}, u32[]{:S(2)}) %collective-permute-start.24) | collective-permute-done | bytes 73760 | tf_op jit(solution)/shard_map/ppermute | solution.py:24
  236.5 4.6 %collective-permute-done.32 = bf16[4,144,256]{2,1,0:T(8,128)(2,1)S(1)} collective-permute-done((bf16[4,144,256]{2,1,0:T(8,128)(2,1)S(1)}, bf16[4,144,256]{2,1,0:T(8,128)(2,1)S(1)}, u32[]{:S(2)}, u32[]{:S(2)}) %collective-permute-start.32) | collective-permute-done | bytes 294944 | tf_op jit(solution)/shard_map/ppermute | solution.py:24
  242.0 6.4 %collective-permute-start.33 = (bf16[2,4,144,256]{3,2,1,0:T(8,128)(2,1)}, bf16[2,4,144,256]{3,2,1,0:T(8,128)(2,1)}, u32[]{:S(2)}, u32[]{:S(2)}) collective-permute-start(bf16[2,4,144,256]{3,2,1,0:T(8,128)(2,1)} %pad_maximum_fusion.2.spare_ref), channel_id=1, source_target_pairs={{0,1},{1,0},{2,3},{3,2},{4,5},{5,4},{6,7},{7,6},{8,9},{9,8},{10,11... | collective-permute-start | bytes 1769480 | tf_op jit(solution)/shard_map/ppermute | solution.py:24
  249.2 1.3 copy-done.4
  250.5 1.1 copy-done.12
  252.3 4.6 %unpack_rows.1 = (bf16[256,2048]{1,0:T(8,128)(2,1)}, bf16[256,2048]{1,0:T(8,128)(2,1)}) custom-call(s32[2,256]{1,0:T(2,128)S(1)} %copy-done.32, f32[256,2]{1,0:T(8,128)S(1)} %copy.12.gate_ref, bf16[640,2048]{1,0:T(8,128)(2,1)S(1)} %bitcast.79, bf16[2,160,2048]{2,1,0:T(8,128)(2,1)S(1)} %copy-done.4, bf16[160,2048]{1,0:T(8,128)(2,1)S(1)} %copy-done.12), custom_call_target="tpu_custom_call" | custom-call | flops 1000000 | bytes 100000 | tf_op jit(solution)/shard_map/unpack_rows/pallas_call | solution.py:44
  256.9 1.2 copy-done.20
  258.1 4.2 %finish_grads.1 = (f32[256,1536]{1,0:T(8,128)}, f32[96,2048]{1,0:T(8,128)}) custom-call(s32[6]{0:T(128)S(1)} %copy-done.34, bf16[2,4,144,256]{3,2,1,0:T(8,128)(2,1)} %pad_maximum_fusion.2.spare_ref, bf16[2,4,144,256]{3,2,1,0:T(8,128)(2,1)} %collective-permute-done.33.more_ref, bf16[768,768]{1,0:T(8,128)(2,1)} %copy-done.2, bf16[256,1536]{1,0:T(8,128)(2,1)S(1)} %copy-done.10, ...), custom_call_target="tpu_custom_call" | custom-call | flops 1000000 | bytes 100000 | tf_op jit(solution)/shard_map/finish_grads/pallas_call | solution.py:44
  (130 shorter events, 22.7 us)
Async XLA Ops:
  0.6 1.2 copy-start.7
  1.2 12.4 %copy-start.2 = (bf16[768,768]{1,0:T(8,128)(2,1)}, bf16[768,768]{1,0:T(8,128)(2,1)S(1)}, u32[]{:S(2)}) copy-start(bf16[768,768]{1,0:T(8,128)(2,1)S(1)} %fusion.pick_ref) | copy-start | bytes 3538948
  1.9 2.8 %copy-start = (bf16[1,2048,1536]{2,1,0:T(8,128)(2,1)S(1)}, bf16[1,2048,1536]{2,1,0:T(8,128)(2,1)}, u32[]{:S(2)}) copy-start(bf16[1,2048,1536]{2,1,0:T(8,128)(2,1)} %param.11) | copy-start | bytes 18874372
  4.6 1.9 copy-start.1
  6.5 1.2 copy-start.8
  13.6 43.2 %copy-start.31 = (s32[2,256]{1,0:T(2,128)}, s32[2,256]{1,0:T(2,128)S(1)}, u32[]{:S(2)}) copy-start(s32[2,256]{1,0:T(2,128)S(1)} %get-tuple-element.29.pos_ref) | copy-start | bytes 6148
  14.7 3.2 %collective-permute-start = (bf16[2,576,256]{2,1,0:T(8,128)(2,1)S(1)}, bf16[2,576,256]{2,1,0:T(8,128)(2,1)S(1)}, u32[]{:S(2)}, u32[]{:S(2)}) collective-permute-start(bf16[2,576,256]{2,1,0:T(8,128)(2,1)S(1)} %slice_bitcast_fusion.7), channel_id=1, source_target_pairs={{0,1},{1,0},{2,3},{3,2},{4,5},{5,4},{6,7},{7,6},{8,9},{9,8},{10,11... | collective-permute-start | bytes 1769480 | tf_op jit(solution)/shard_map/ppermute | solution.py:24
  19.1 8.4 %collective-permute-start.1 = (bf16[576,256]{1,0:T(8,128)(2,1)S(1)}, bf16[576,256]{1,0:T(8,128)(2,1)S(1)}, u32[]{:S(2)}, u32[]{:S(2)}) collective-permute-start(bf16[576,256]{1,0:T(8,128)(2,1)S(1)} %slice_bitcast_fusion.14), channel_id=1, source_target_pairs={{0,2},{1,3},{2,0},{3,1},{4,6},{5,7},{6,4},{7,5},{8,10},{9,11},{10,... | collective-permute-start | bytes 884744 | tf_op jit(solution)/shard_map/ppermute | solution.py:24
  27.5 10.2 %collective-permute-start.2 = (bf16[576,256]{1,0:T(8,128)(2,1)S(1)}, bf16[576,256]{1,0:T(8,128)(2,1)S(1)}, u32[]{:S(2)}, u32[]{:S(2)}) collective-permute-start(bf16[576,256]{1,0:T(8,128)(2,1)S(1)} %fusion.3), channel_id=1, source_target_pairs={{0,4},{1,5},{2,6},{3,7},{4,8},{5,9},{6,10},{7,11},{8,12},{9,13},{1... | collective-permute-start | bytes 884744 | tf_op jit(solution)/shard_map/ppermute | solution.py:24
  29.3 15.7 %collective-permute-start.3 = (bf16[576,256]{1,0:T(8,128)(2,1)S(1)}, bf16[576,256]{1,0:T(8,128)(2,1)}, u32[]{:S(2)}, u32[]{:S(2)}) collective-permute-start(bf16[576,256]{1,0:T(8,128)(2,1)S(1)} %fusion.3), channel_id=1, source_target_pairs={{0,8},{1,9},{2,10},{3,11},{4,12},{5,13},{6,14},{7,15},{8,0},{9,1},... | collective-permute-start | bytes 884744 | tf_op jit(solution)/shard_map/ppermute | solution.py:24
  32.6 12.4 %collective-permute-start.4 = (bf16[576,256]{1,0:T(8,128)(2,1)S(1)}, bf16[576,256]{1,0:T(8,128)(2,1)}, u32[]{:S(2)}, u32[]{:S(2)}) collective-permute-start(bf16[576,256]{1,0:T(8,128)(2,1)S(1)} %fusion.3), channel_id=1, source_target_pairs={{0,12},{1,13},{2,14},{3,15},{4,0},{5,1},{6,2},{7,3},{8,4},{9,5},{1... | collective-permute-start | bytes 884744 | tf_op jit(solution)/shard_map/ppermute | solution.py:24
  33.4 23.4 %copy-start.9 = (bf16[256,2048]{1,0:T(8,128)(2,1)S(1)}, bf16[256,2048]{1,0:T(8,128)(2,1)}, u32[]{:S(2)}) copy-start(bf16[256,2048]{1,0:T(8,128)(2,1)} %cot_ref.3) | copy-start | bytes 3145732
  33.4 23.4 %copy-start.30 = (f32[256,2]{0,1:T(2,128)S(1)}, f32[256,2]{0,1:T(2,128)}, u32[]{:S(2)}) copy-start(f32[256,2]{0,1:T(2,128)} %param.10) | copy-start | bytes 6148
  33.4 23.4 %collective-permute-start.6 = (bf16[160,2048]{1,0:T(8,128)(2,1)S(1)}, bf16[160,2048]{1,0:T(8,128)(2,1)S(1)}, u32[]{:S(2)}, u32[]{:S(2)}) collective-permute-start(bf16[160,2048]{1,0:T(8,128)(2,1)S(1)} %keep_rows.1.own_ref), channel_id=1, source_target_pairs={{0,2},{1,3},{2,0},{3,1},{4,6},{5,7},{6,4},{7,5},{8,10},{9,11},{10,... | collective-permute-start | bytes 1966088 | tf_op jit(solution)/shard_map/ppermute | solution.py:24
  46.0 10.7 %collective-permute-start.5 = (bf16[576,256]{1,0:T(8,128)(2,1)S(1)}, bf16[576,256]{1,0:T(8,128)(2,1)S(1)}, u32[]{:S(2)}, u32[]{:S(2)}) collective-permute-start(bf16[576,256]{1,0:T(8,128)(2,1)S(1)} %select_select_fusion), channel_id=1, source_target_pairs={{0,64},{1,65},{2,66},{3,67},{4,68},{5,69},{6,70},{7,71},{8,72},{9,... | collective-permute-start | bytes 884744 | tf_op jit(solution)/shard_map/ppermute | solution.py:24
  59.9 39.5 %all-to-all-start = ((bf16[16,40,2048]{2,1,0:T(8,128)(2,1)}), bf16[16,40,2048]{2,1,0:T(8,128)(2,1)}, u32[]{:S(2)}, u32[]{:S(2)}) async-start(bf16[16,40,2048]{2,1,0:T(8,128)(2,1)} %bitcast.18), calls=%async_computation | async-start | bytes 5242880 | tf_op jit(solution)/shard_map/all_to_all | solution.py:368
  67.7 30.4 %collective-permute-start.7 = (bf16[2,160,2048]{2,1,0:T(8,128)(2,1)}, bf16[2,160,2048]{2,1,0:T(8,128)(2,1)}, u32[]{:S(2)}, u32[]{:S(2)}) collective-permute-start(bf16[2,160,2048]{2,1,0:T(8,128)(2,1)} %pad_maximum_fusion), channel_id=1, source_target_pairs={{0,1},{1,0},{2,3},{3,2},{4,5},{5,4},{6,7},{7,6},{8,9},{9,8},{10,11... | collective-permute-start | bytes 3932168 | tf_op jit(solution)/shard_map/ppermute | solution.py:24
  68.0 27.7 %collective-permute-start.10 = (bf16[2,576,256]{2,1,0:T(8,128)(2,1)S(1)}, bf16[2,576,256]{2,1,0:T(8,128)(2,1)S(1)}, u32[]{:S(2)}, u32[]{:S(2)}) collective-permute-start(bf16[2,576,256]{2,1,0:T(8,128)(2,1)S(1)} %pad_maximum_fusion.1.refs_0_.w0_ref), channel_id=1, source_target_pairs={{0,48},{1,49},{2,50},{3,51},{4,52},{5,53},{6,54},{7,55},{8,56},{9,... | collective-permute-start | bytes 1769480 | tf_op jit(solution)/shard_map/ppermute | solution.py:24
  70.7 25.0 %collective-permute-start.8 = (bf16[2,576,256]{2,1,0:T(8,128)(2,1)S(1)}, bf16[2,576,256]{2,1,0:T(8,128)(2,1)S(1)}, u32[]{:S(2)}, u32[]{:S(2)}) collective-permute-start(bf16[2,576,256]{2,1,0:T(8,128)(2,1)S(1)} %pad_maximum_fusion.1.refs_0_.w0_ref), channel_id=1, source_target_pairs={{0,16},{1,17},{2,18},{3,19},{4,20},{5,21},{6,22},{7,23},{8,24},{9,... | collective-permute-start | bytes 1769480 | tf_op jit(solution)/shard_map/ppermute | solution.py:24
  70.7 27.4 %collective-permute-start.9 = (bf16[2,576,256]{2,1,0:T(8,128)(2,1)S(1)}, bf16[2,576,256]{2,1,0:T(8,128)(2,1)}, u32[]{:S(2)}, u32[]{:S(2)}) collective-permute-start(bf16[2,576,256]{2,1,0:T(8,128)(2,1)S(1)} %pad_maximum_fusion.1.refs_0_.w0_ref), channel_id=1, source_target_pairs={{0,32},{1,33},{2,34},{3,35},{4,36},{5,37},{6,38},{7,39},{8,40},{9,... | collective-permute-start | bytes 1769480 | tf_op jit(solution)/shard_map/ppermute | solution.py:24
  73.0 57.6 %copy-start.33 = (s32[6]{0:T(128)}, s32[6]{0:T(128)S(1)}, u32[]{:S(2)}) copy-start(s32[6]{0:T(128)S(1)} %concatenate.10.here_ref) | copy-start | bytes 76
  107.1 3.7 %collective-permute-start.14 = (bf16[2,160,2048]{2,1,0:T(8,128)(2,1)}, bf16[2,160,2048]{2,1,0:T(8,128)(2,1)S(1)}, u32[]{:S(2)}, u32[]{:S(2)}) collective-permute-start(bf16[2,160,2048]{2,1,0:T(8,128)(2,1)} %get-tuple-element.42), channel_id=1, source_target_pairs={{0,1},{1,0},{2,3},{3,2},{4,5},{5,4},{6,7},{7,6},{8,9},{9,8},{10,11... | collective-permute-start | bytes 3932168 | tf_op jit(solution)/shard_map/ppermute | solution.py:24
  112.6 1.1 copy-start.3
  113.7 16.9 %collective-permute-start.15 = (bf16[160,2048]{1,0:T(8,128)(2,1)S(1)}, bf16[160,2048]{1,0:T(8,128)(2,1)S(1)}, u32[]{:S(2)}, u32[]{:S(2)}) collective-permute-start(bf16[160,2048]{1,0:T(8,128)(2,1)S(1)} %slice_bitcast_fusion.6), channel_id=1, source_target_pairs={{0,2},{1,3},{2,0},{3,1},{4,6},{5,7},{6,4},{7,5},{8,10},{9,11},{10,... | collective-permute-start | bytes 1966088 | tf_op jit(solution)/shard_map/ppermute | solution.py:24
  115.2 15.4 %collective-permute-start.11 = (bf16[2,4,144,256]{3,2,1,0:T(8,128)(2,1)S(1)}, bf16[2,4,144,256]{3,2,1,0:T(8,128)(2,1)S(1)}, u32[]{:S(2)}, u32[]{:S(2)}) collective-permute-start(bf16[2,4,144,256]{3,2,1,0:T(8,128)(2,1)S(1)} %get-tuple-element.36), channel_id=1, source_target_pairs={{0,4},{1,5},{2,6},{3,7},{4,8},{5,9},{6,10},{7,11},{8,12},{9,13},{1... | collective-permute-start | bytes 1769480 | tf_op jit(solution)/shard_map/ppermute | solution.py:24
  116.4 14.2 %collective-permute-start.13 = (bf16[2,4,144,256]{3,2,1,0:T(8,128)(2,1)S(1)}, bf16[2,4,144,256]{3,2,1,0:T(8,128)(2,1)S(1)}, u32[]{:S(2)}, u32[]{:S(2)}) collective-permute-start(bf16[2,4,144,256]{3,2,1,0:T(8,128)(2,1)S(1)} %get-tuple-element.38), channel_id=1, source_target_pairs={{0,12},{1,13},{2,14},{3,15},{4,0},{5,1},{6,2},{7,3},{8,4},{9,5},{1... | collective-permute-start | bytes 1769480 | tf_op jit(solution)/shard_map/ppermute | solution.py:24
  127.0 1.1 copy-start.19
  130.6 9.4 %copy-start.11 = (bf16[160,2048]{1,0:T(8,128)(2,1)}, bf16[160,2048]{1,0:T(8,128)(2,1)S(1)}, u32[]{:S(2)}) copy-start(bf16[160,2048]{1,0:T(8,128)(2,1)S(1)} %collective-permute-done.15.refs_0_.hot_b_ref) | copy-start | bytes 1966084
  140.9 16.4 %copy-start.21 = (bf16[2,256,768]{2,1,0:T(8,128)(2,1)}, bf16[2,256,768]{2,1,0:T(8,128)(2,1)S(1)}, u32[]{:S(2)}) copy-start(bf16[2,256,768]{2,1,0:T(8,128)(2,1)S(1)} %get-tuple-element.46.refs_0_) | copy-start | bytes 2359300
  140.9 39.2 %collective-permute-start.18 = (bf16[2,2,256,768]{3,2,1,0:T(8,128)(2,1)}, bf16[2,2,256,768]{3,2,1,0:T(8,128)(2,1)}, u32[]{:S(2)}, u32[]{:S(2)}) collective-permute-start(bf16[2,2,256,768]{3,2,1,0:T(8,128)(2,1)} %get-tuple-element.49), channel_id=1, source_target_pairs={{0,48},{1,49},{2,50},{3,51},{4,52},{5,53},{6,54},{7,55},{8,56},{9,... | collective-permute-start | bytes 4718600 | tf_op jit(solution)/shard_map/ppermute | solution.py:24
  142.7 42.0 %collective-permute-start.17 = (bf16[2,2,256,768]{3,2,1,0:T(8,128)(2,1)}, bf16[2,2,256,768]{3,2,1,0:T(8,128)(2,1)}, u32[]{:S(2)}, u32[]{:S(2)}) collective-permute-start(bf16[2,2,256,768]{3,2,1,0:T(8,128)(2,1)} %get-tuple-element.47), channel_id=1, source_target_pairs={{0,16},{1,17},{2,18},{3,19},{4,20},{5,21},{6,22},{7,23},{8,24},{9,... | collective-permute-start | bytes 4718600 | tf_op jit(solution)/shard_map/ppermute | solution.py:24
  142.7 14.6 %collective-permute-start.12 = (bf16[2,4,144,256]{3,2,1,0:T(8,128)(2,1)S(1)}, bf16[2,4,144,256]{3,2,1,0:T(8,128)(2,1)S(1)}, u32[]{:S(2)}, u32[]{:S(2)}) collective-permute-start(bf16[2,4,144,256]{3,2,1,0:T(8,128)(2,1)S(1)} %get-tuple-element.37), channel_id=1, source_target_pairs={{0,8},{1,9},{2,10},{3,11},{4,12},{5,13},{6,14},{7,15},{8,0},{9,1},... | collective-permute-start | bytes 1769480 | tf_op jit(solution)/shard_map/ppermute | solution.py:24
  144.5 46.0 %collective-permute-start.28 = (bf16[4,96,2048]{2,1,0:T(8,128)(2,1)}, bf16[4,96,2048]{2,1,0:T(8,128)(2,1)}, u32[]{:S(2)}, u32[]{:S(2)}) collective-permute-start(bf16[4,96,2048]{2,1,0:T(8,128)(2,1)} %get-tuple-element.51), channel_id=1, source_target_pairs={{0,64},{1,65},{2,66},{3,67},{4,68},{5,69},{6,70},{7,71},{8,72},{9,... | collective-permute-start | bytes 4718600 | tf_op jit(solution)/shard_map/ppermute | solution.py:24
  157.3 1.4 copy-start.5
  159.1 27.4 %collective-permute-start.16 = (bf16[4,144,256]{2,1,0:T(8,128)(2,1)S(1)}, bf16[4,144,256]{2,1,0:T(8,128)(2,1)S(1)}, u32[]{:S(2)}, u32[]{:S(2)}) collective-permute-start(bf16[4,144,256]{2,1,0:T(8,128)(2,1)S(1)} %get-tuple-element.64), channel_id=1, source_target_pairs={{0,64},{1,65},{2,66},{3,67},{4,68},{5,69},{6,70},{7,71},{8,72},{9,... | collective-permute-start | bytes 884744 | tf_op jit(solution)/shard_map/ppermute | solution.py:24
  173.0 58.6 %all-to-all-start.1 = ((bf16[16,40,2048]{2,1,0:T(8,128)(2,1)}), bf16[16,40,2048]{2,1,0:T(8,128)(2,1)S(1)}, u32[]{:S(2)}, u32[]{:S(2)}) async-start(bf16[16,40,2048]{2,1,0:T(8,128)(2,1)} %bitcast.24), calls=%async_computation.1 | async-start | bytes 5242880 | tf_op jit(solution)/shard_map/all_to_all | solution.py:420
  180.1 1.6 copy-start.24
  181.9 4.3 %copy-start.22 = (bf16[2,256,768]{2,1,0:T(8,128)(2,1)S(1)}, bf16[2,256,768]{2,1,0:T(8,128)(2,1)}, u32[]{:S(2)}) copy-start(bf16[2,256,768]{2,1,0:T(8,128)(2,1)} %copy-done.21) | copy-start | bytes 2359300
  181.9 21.1 %collective-permute-start.26 = (bf16[2,256,768]{2,1,0:T(8,128)(2,1)S(1)}, bf16[2,256,768]{2,1,0:T(8,128)(2,1)S(1)}, u32[]{:S(2)}, u32[]{:S(2)}) collective-permute-start(bf16[2,256,768]{2,1,0:T(8,128)(2,1)S(1)} %sum_down.1.refs_3_), channel_id=1, source_target_pairs={{0,48},{1,49},{2,50},{3,51},{4,52},{5,53},{6,54},{7,55},{8,56},{9,... | collective-permute-start | bytes 2359304 | tf_op jit(solution)/shard_map/ppermute | solution.py:24
  186.4 4.1 %copy-start.38 = (bf16[4,96,2048]{2,1,0:T(8,128)(2,1)S(1)}, bf16[4,96,2048]{2,1,0:T(8,128)(2,1)}, u32[]{:S(2)}) copy-start(bf16[4,96,2048]{2,1,0:T(8,128)(2,1)} %get-tuple-element.50) | copy-start | bytes 4718596
  186.4 20.0 %collective-permute-start.25 = (bf16[2,256,768]{2,1,0:T(8,128)(2,1)S(1)}, bf16[2,256,768]{2,1,0:T(8,128)(2,1)S(1)}, u32[]{:S(2)}, u32[]{:S(2)}) collective-permute-start(bf16[2,256,768]{2,1,0:T(8,128)(2,1)S(1)} %sum_up.1.refs_2_), channel_id=1, source_target_pairs={{0,16},{1,17},{2,18},{3,19},{4,20},{5,21},{6,22},{7,23},{8,24},{9,... | collective-permute-start | bytes 2359304 | tf_op jit(solution)/shard_map/ppermute | solution.py:24
  186.6 24.1 %collective-permute-start.19 = (bf16[144,256]{1,0:T(8,128)(2,1)S(1)}, bf16[144,256]{1,0:T(8,128)(2,1)S(1)}, u32[]{:S(2)}, u32[]{:S(2)}) collective-permute-start(bf16[144,256]{1,0:T(8,128)(2,1)S(1)} %get-tuple-element.66), channel_id=1, source_target_pairs={{0,16},{1,17},{2,18},{3,19},{4,20},{5,21},{6,22},{7,23},{8,24},{9,... | collective-permute-start | bytes 221192 | tf_op jit(solution)/shard_map/ppermute | solution.py:24
  186.6 25.3 %collective-permute-start.20 = (bf16[144,256]{1,0:T(8,128)(2,1)S(1)}, bf16[144,256]{1,0:T(8,128)(2,1)S(1)}, u32[]{:S(2)}, u32[]{:S(2)}) collective-permute-start(bf16[144,256]{1,0:T(8,128)(2,1)S(1)} %get-tuple-element.68), channel_id=1, source_target_pairs={{0,32},{1,33},{2,34},{3,35},{4,36},{5,37},{6,38},{7,39},{8,40},{9,... | collective-permute-start | bytes 221192 | tf_op jit(solution)/shard_map/ppermute | solution.py:24
  190.5 22.9 %collective-permute-start.21 = (bf16[144,256]{1,0:T(8,128)(2,1)S(1)}, bf16[144,256]{1,0:T(8,128)(2,1)S(1)}, u32[]{:S(2)}, u32[]{:S(2)}) collective-permute-start(bf16[144,256]{1,0:T(8,128)(2,1)S(1)} %get-tuple-element.67), channel_id=1, source_target_pairs={{0,48},{1,49},{2,50},{3,51},{4,52},{5,53},{6,54},{7,55},{8,56},{9,... | collective-permute-start | bytes 221192 | tf_op jit(solution)/shard_map/ppermute | solution.py:24
  190.5 15.9 %copy-start.6 = (bf16[2,256,1536]{2,1,0:T(8,128)(2,1)S(1)}, bf16[2,256,1536]{2,1,0:T(8,128)(2,1)}, u32[]{:S(2)}) copy-start(bf16[2,256,1536]{2,1,0:T(8,128)(2,1)} %get-tuple-element.43.refs_4_) | copy-start | bytes 4718596
  208.2 23.4 %collective-permute-start.27 = (bf16[256,1536]{1,0:T(8,128)(2,1)}, bf16[256,1536]{1,0:T(8,128)(2,1)}, u32[]{:S(2)}, u32[]{:S(2)}) collective-permute-start(bf16[256,1536]{1,0:T(8,128)(2,1)} %get-tuple-element.55), channel_id=1, source_target_pairs={{0,64},{1,65},{2,66},{3,67},{4,68},{5,69},{6,70},{7,71},{8,72},{9,... | collective-permute-start | bytes 2359304 | tf_op jit(solution)/shard_map/ppermute | solution.py:24
  210.6 19.5 %collective-permute-start.29 = (bf16[96,2048]{1,0:T(8,128)(2,1)S(1)}, bf16[96,2048]{1,0:T(8,128)(2,1)S(1)}, u32[]{:S(2)}, u32[]{:S(2)}) collective-permute-start(bf16[96,2048]{1,0:T(8,128)(2,1)S(1)} %get-tuple-element.58), channel_id=1, source_target_pairs={{0,16},{1,17},{2,18},{3,19},{4,20},{5,21},{6,22},{7,23},{8,24},{9,... | collective-permute-start | bytes 1179656 | tf_op jit(solution)/shard_map/ppermute | solution.py:24
  210.7 19.4 %collective-permute-start.30 = (bf16[96,2048]{1,0:T(8,128)(2,1)S(1)}, bf16[96,2048]{1,0:T(8,128)(2,1)S(1)}, u32[]{:S(2)}, u32[]{:S(2)}) collective-permute-start(bf16[96,2048]{1,0:T(8,128)(2,1)S(1)} %get-tuple-element.57), channel_id=1, source_target_pairs={{0,32},{1,33},{2,34},{3,35},{4,36},{5,37},{6,38},{7,39},{8,40},{9,... | collective-permute-start | bytes 1179656 | tf_op jit(solution)/shard_map/ppermute | solution.py:24
  212.0 18.9 %collective-permute-start.31 = (bf16[96,2048]{1,0:T(8,128)(2,1)S(1)}, bf16[96,2048]{1,0:T(8,128)(2,1)S(1)}, u32[]{:S(2)}, u32[]{:S(2)}) collective-permute-start(bf16[96,2048]{1,0:T(8,128)(2,1)S(1)} %get-tuple-element.56), channel_id=1, source_target_pairs={{0,48},{1,49},{2,50},{3,51},{4,52},{5,53},{6,54},{7,55},{8,56},{9,... | collective-permute-start | bytes 1179656 | tf_op jit(solution)/shard_map/ppermute | solution.py:24
  213.5 5.6 %collective-permute-start.22 = (bf16[144,256]{1,0:T(8,128)(2,1)S(1)}, bf16[144,256]{1,0:T(8,128)(2,1)S(1)}, u32[]{:S(2)}, u32[]{:S(2)}) collective-permute-start(bf16[144,256]{1,0:T(8,128)(2,1)S(1)} %fusion.6.refs_0_), channel_id=1, source_target_pairs={{0,4},{1,5},{2,6},{3,7},{4,8},{5,9},{6,10},{7,11},{8,12},{9,13},{1... | collective-permute-start | bytes 221192 | tf_op jit(solution)/shard_map/ppermute | solution.py:24
  219.0 5.7 %collective-permute-start.23 = (bf16[144,256]{1,0:T(8,128)(2,1)S(1)}, bf16[144,256]{1,0:T(8,128)(2,1)S(1)}, u32[]{:S(2)}, u32[]{:S(2)}) collective-permute-start(bf16[144,256]{1,0:T(8,128)(2,1)S(1)} %fusion.6.refs_0_), channel_id=1, source_target_pairs={{0,8},{1,9},{2,10},{3,11},{4,12},{5,13},{6,14},{7,15},{8,0},{9,1},... | collective-permute-start | bytes 221192 | tf_op jit(solution)/shard_map/ppermute | solution.py:24
  225.4 4.1 %collective-permute-start.24 = (bf16[144,256]{1,0:T(8,128)(2,1)S(1)}, bf16[144,256]{1,0:T(8,128)(2,1)S(1)}, u32[]{:S(2)}, u32[]{:S(2)}) collective-permute-start(bf16[144,256]{1,0:T(8,128)(2,1)S(1)} %fusion.6.refs_0_), channel_id=1, source_target_pairs={{0,12},{1,13},{2,14},{3,15},{4,0},{5,1},{6,2},{7,3},{8,4},{9,5},{1... | collective-permute-start | bytes 221192 | tf_op jit(solution)/shard_map/ppermute | solution.py:24
  231.6 1.0 copy-start.14
  232.6 1.0 copy-start.17
  233.6 0.9 copy-start.26
  235.4 5.7 %collective-permute-start.32 = (bf16[4,144,256]{2,1,0:T(8,128)(2,1)S(1)}, bf16[4,144,256]{2,1,0:T(8,128)(2,1)S(1)}, u32[]{:S(2)}, u32[]{:S(2)}) collective-permute-start(bf16[4,144,256]{2,1,0:T(8,128)(2,1)S(1)} %stack_z.1), channel_id=1, source_target_pairs={{0,2},{1,3},{2,0},{3,1},{4,6},{5,7},{6,4},{7,5},{8,10},{9,11},{10,... | collective-permute-start | bytes 884744 | tf_op jit(solution)/shard_map/ppermute | solution.py:24
  242.0 14.8 %collective-permute-start.33 = (bf16[2,4,144,256]{3,2,1,0:T(8,128)(2,1)}, bf16[2,4,144,256]{3,2,1,0:T(8,128)(2,1)}, u32[]{:S(2)}, u32[]{:S(2)}) collective-permute-start(bf16[2,4,144,256]{3,2,1,0:T(8,128)(2,1)} %pad_maximum_fusion.2.spare_ref), channel_id=1, source_target_pairs={{0,1},{1,0},{2,3},{3,2},{4,5},{5,4},{6,7},{7,6},{8,9},{9,8},{10,11... | collective-permute-start | bytes 1769480 | tf_op jit(solution)/shard_map/ppermute | solution.py:24
  249.2 1.3 copy-start.4
  250.5 1.1 copy-start.12
  252.3 4.6 %copy-start.10 = (bf16[256,1536]{1,0:T(8,128)(2,1)S(1)}, bf16[256,1536]{1,0:T(8,128)(2,1)}, u32[]{:S(2)}) copy-start(bf16[256,1536]{1,0:T(8,128)(2,1)} %get-tuple-element.54.in_ref) | copy-start | bytes 2359300
  252.3 4.6 %copy-start.15 = (bf16[96,2048]{1,0:T(8,128)(2,1)S(1)}, bf16[96,2048]{1,0:T(8,128)(2,1)}, u32[]{:S(2)}) copy-start(bf16[96,2048]{1,0:T(8,128)(2,1)} %copy-done.13) | copy-start | bytes 1179652
  252.3 4.6 %copy-start.18 = (bf16[96,2048]{1,0:T(8,128)(2,1)S(1)}, bf16[96,2048]{1,0:T(8,128)(2,1)}, u32[]{:S(2)}) copy-start(bf16[96,2048]{1,0:T(8,128)(2,1)} %copy-done.16) | copy-start | bytes 1179652
  252.3 4.6 %copy-start.34 = (s32[6]{0:T(128)S(1)}, s32[6]{0:T(128)}, u32[]{:S(2)}) copy-start(s32[6]{0:T(128)} %copy-done.33) | copy-start | bytes 76
  256.9 1.2 copy-start.20
  (11 other events, 7.9 us)

commit v4 on v3

--- a/solution.py
+++ b/solution.py
@@ -444,7 +444,7 @@
         stack_kernel,
         "stack_z",
         (shape(4, 144, 256),),
-        (spare, *[hop(spare, dz=s) for s in (1, 2, 3)], returned, in_got, *out_parts),
+        (spare, *[hop(spare, dz=s) for s in (1, 2, 3)], mixed, in_got, *out_parts),
         in_specs=[VMEM] * 4 + [AFTER] * 6,
     )
     spare = jnp.stack([spare, hop(spare, dl=1)])

time: 263 us -> 259 us (0.985)
  local copies, waits for them, and re-layouts: 31.1 us -> 25.5 us
    unnamed x79 -> x61, local copies, waits for them, and re-layouts: 25.3 us -> 18.7 us
  transfers between devices with their start and end apart: 36 -> 36, of which waited for: 16 -> 16; matrix products, arithmetic and copies ran while one was open for 4% -> 5% of each run, Pallas kernels for 10% -> 10%
where the time goes in v4:
time: 259 us; the launch traced here: 258 us
  waiting for transfers between devices  96.5 us (37%)
  starting transfers between devices  66.8 us (26%)
  Pallas kernels  54.7 us (21%)
  local copies, waits for them, and re-layouts  25.5 us (10%)
  other arithmetic  10.2 us (4%)
  between operations  4.4 us (2%)
    ppermute x34, waiting for transfers between devices, hop(): return lax.ppermute(x, AXES, pairs)  95.1 us
    ppermute x34, starting transfers between devices, hop(): return lax.ppermute(x, AXES, pairs)  53.7 us
    pallas_call x13, Pallas kernels, call(): pl.pallas_call(kernel, out_shape=outs, in_specs=in_specs or [VMEM] * len(...  51.7 us
    unnamed x61, local copies, waits for them, and re-layouts  18.7 us
    all_to_all x1, starting transfers between devices, shards(): lax.all_to_all(result, 'expert', split_axis=0, concat_axis=0, tiled=True)  7.07 us
    all_to_all x1, starting transfers between devices, shards(): lax.all_to_all(send, 'expert', split_axis=0, concat_axis=0, tiled=True)  6.11 us
    convert_element_type x4, other arithmetic, total(): return out.astype(dtype)  5.2 us
  transfers between devices with their start and end apart: 36, of which 16 were waited for; matrix products, arithmetic and copies ran while one was open for 5% of the time, Pallas kernels for 10%

profile of v4, /device:TPU:1, one launch (start us, length us, event | category | flops | bytes accessed | tf_op | source)
XLA Modules:
  0.0 258.2 jit_solution(3276066437488475530)
XLA Ops:
  1.9 2.8 %copy-done = bf16[1,2048,1536]{2,1,0:T(8,128)(2,1)S(1)} copy-done((bf16[1,2048,1536]{2,1,0:T(8,128)(2,1)S(1)}, bf16[1,2048,1536]{2,1,0:T(8,128)(2,1)}, u32[]{:S(2)}) %copy-start) | copy-done | bytes 6291480
  4.6 1.9 copy-done.1
  6.5 1.2 copy-done.8
  10.5 3.0 %route.1 = (bf16[2,2,576,256]{3,2,1,0:T(8,128)(2,1)}, bf16[160,2048]{1,0:T(8,128)(2,1)S(1)}, s32[2,256]{1,0:T(2,128)S(1)}, s32[1,1]{1,0:T(1,128)}) custom-call(s32[5]{0:T(128)S(1)} %stack.50.here_ref, s32[2,256]{1,0:T(2,128)S(1)} %bitcast.84, s32[2,256]{1,0:T(2,128)S(1)} %bitcast.85, s32[2,256]{1,0:T(2,128)S(1)} %bitcast.86, f32[2,256]{1,0:T(2,128)S(1)} %bitcast.82, ...), custom_call_target="tpu_custom_call" | custom-call | flops 1000000 | bytes 100000 | tf_op jit(solution)/shard_map/route/pallas_call | solution.py:127
  13.6 1.1 slice_bitcast_fusion.7
  14.7 1.5 collective-permute-start
  18.1 1.1 bitcast_select_fusion
  19.2 1.4 collective-permute-start.1
  21.3 6.6 %collective-permute-done.1.refs_1_ = bf16[576,256]{1,0:T(8,128)(2,1)S(1)} collective-permute-done((bf16[576,256]{1,0:T(8,128)(2,1)S(1)}, bf16[576,256]{1,0:T(8,128)(2,1)S(1)}, u32[]{:S(2)}, u32[]{:S(2)}) %collective-permute-start.1) | collective-permute-done | bytes 294944 | tf_op jit(solution)/shard_map/ppermute | solution.py:24
  28.7 1.7 collective-permute-start.2
  30.4 3.3 %collective-permute-start.3 = (bf16[576,256]{1,0:T(8,128)(2,1)}, bf16[576,256]{1,0:T(8,128)(2,1)}, u32[]{:S(2)}, u32[]{:S(2)}) collective-permute-start(bf16[576,256]{1,0:T(8,128)(2,1)} %fusion.3), channel_id=1, source_target_pairs={{0,8},{1,9},{2,10},{3,11},{4,12},{5,13},{6,14},{7,15},{8,0},{9,1},... | collective-permute-start | bytes 884744 | tf_op jit(solution)/shard_map/ppermute | solution.py:24
  34.5 1.3 collective-permute-start.6
  35.8 3.5 %collective-permute-done.2 = bf16[576,256]{1,0:T(8,128)(2,1)S(1)} collective-permute-done((bf16[576,256]{1,0:T(8,128)(2,1)}, bf16[576,256]{1,0:T(8,128)(2,1)S(1)}, u32[]{:S(2)}, u32[]{:S(2)}) %collective-permute-start.2) | collective-permute-done | bytes 294944 | tf_op jit(solution)/shard_map/ppermute | solution.py:24
  39.2 7.3 %collective-permute-done.3 = bf16[576,256]{1,0:T(8,128)(2,1)} collective-permute-done((bf16[576,256]{1,0:T(8,128)(2,1)}, bf16[576,256]{1,0:T(8,128)(2,1)}, u32[]{:S(2)}, u32[]{:S(2)}) %collective-permute-start.3) | collective-permute-done | bytes 294944 | tf_op jit(solution)/shard_map/ppermute | solution.py:24
  46.5 1.1 select_select_fusion
  47.6 2.8 %collective-permute-start.5 = (bf16[576,256]{1,0:T(8,128)(2,1)S(1)}, bf16[576,256]{1,0:T(8,128)(2,1)S(1)}, u32[]{:S(2)}, u32[]{:S(2)}) collective-permute-start(bf16[576,256]{1,0:T(8,128)(2,1)S(1)} %select_select_fusion), channel_id=1, source_target_pairs={{0,64},{1,65},{2,66},{3,67},{4,68},{5,69},{6,70},{7,71},{8,72},{9,... | collective-permute-start | bytes 884744 | tf_op jit(solution)/shard_map/ppermute | solution.py:24
  50.5 7.8 %collective-permute-done.5 = bf16[576,256]{1,0:T(8,128)(2,1)S(1)} collective-permute-done((bf16[576,256]{1,0:T(8,128)(2,1)S(1)}, bf16[576,256]{1,0:T(8,128)(2,1)S(1)}, u32[]{:S(2)}, u32[]{:S(2)}) %collective-permute-start.5) | collective-permute-done | bytes 294944 | tf_op jit(solution)/shard_map/ppermute | solution.py:24
  58.4 3.1 %pack_rows.1 = bf16[640,2048]{1,0:T(8,128)(2,1)} custom-call(s32[2,256]{1,0:T(2,128)S(1)} %get-tuple-element.29.pos_ref, f32[2,256]{1,0:T(2,128)S(1)} %bitcast.83, bf16[256,2048]{1,0:T(8,128)(2,1)S(1)} %copy-done.7, bf16[256,2048]{1,0:T(8,128)(2,1)S(1)} %copy-done.9, bf16[2,576,256]{2,1,0:T(8,128)(2,1)S(1)} %pad_maximum_fusion.1.refs_0_.w0_ref, ...), custom_call_target="tpu_custom_call" | custom-call | flops 1000000 | bytes 100000 | tf_op jit(solution)/shard_map/pack_rows/pallas_call | solution.py:44
  61.5 6.1 %all-to-all-start = ((bf16[16,40,2048]{2,1,0:T(8,128)(2,1)}), bf16[16,40,2048]{2,1,0:T(8,128)(2,1)}, u32[]{:S(2)}, u32[]{:S(2)}) async-start(bf16[16,40,2048]{2,1,0:T(8,128)(2,1)} %bitcast.18), calls=%async_computation | async-start | bytes 5242880 | tf_op jit(solution)/shard_map/all_to_all | solution.py:368
  67.6 1.2 pad_maximum_fusion
  69.1 2.7 %collective-permute-start.10 = (bf16[2,576,256]{2,1,0:T(8,128)(2,1)S(1)}, bf16[2,576,256]{2,1,0:T(8,128)(2,1)S(1)}, u32[]{:S(2)}, u32[]{:S(2)}) collective-permute-start(bf16[2,576,256]{2,1,0:T(8,128)(2,1)S(1)} %pad_maximum_fusion.1.refs_0_.w0_ref), channel_id=1, source_target_pairs={{0,48},{1,49},{2,50},{3,51},{4,52},{5,53},{6,54},{7,55},{8,56},{9,... | collective-permute-start | bytes 1769480 | tf_op jit(solution)/shard_map/ppermute | solution.py:24
  71.8 1.7 collective-permute-start.9
  74.2 22.6 %collective-permute-done.10.w3_ref = bf16[2,576,256]{2,1,0:T(8,128)(2,1)S(1)} collective-permute-done((bf16[2,576,256]{2,1,0:T(8,128)(2,1)S(1)}, bf16[2,576,256]{2,1,0:T(8,128)(2,1)S(1)}, u32[]{:S(2)}, u32[]{:S(2)}) %collective-permute-start.10) | collective-permute-done | bytes 589856 | tf_op jit(solution)/shard_map/ppermute | solution.py:24
  96.8 2.4 collective-permute-done.9.w2_ref
  99.2 1.4 all-to-all-done
  100.6 7.6 %hot_expert.1 = (bf16[2,160,2048]{2,1,0:T(8,128)(2,1)}, bf16[2,160,2048]{2,1,0:T(8,128)(2,1)}, bf16[2,4,144,256]{3,2,1,0:T(8,128)(2,1)S(1)}, bf16[2,4,144,256]{3...) custom-call(s32[6]{0:T(128)S(1)} %concatenate.10.here_ref, ...), custom_call_target="tpu_custom_call" | custom-call | flops 1000000 | bytes 100000 | tf_op jit(solution)/shard_map/hot_expert/pallas_call | solution.py:44
  109.0 2.9 %collective-permute-done.14 = bf16[2,160,2048]{2,1,0:T(8,128)(2,1)S(1)} collective-permute-done((bf16[2,160,2048]{2,1,0:T(8,128)(2,1)}, bf16[2,160,2048]{2,1,0:T(8,128)(2,1)S(1)}, u32[]{:S(2)}, u32[]{:S(2)}) %collective-permute-start.14) | collective-permute-done | bytes 1310752 | tf_op jit(solution)/shard_map/ppermute | solution.py:24
  111.9 1.8 add_convert_fusion.2.hot_a_ref
  114.8 1.5 collective-permute-start.15
  116.3 1.2 collective-permute-start.11
  117.5 1.5 collective-permute-start.13
  119.1 9.1 %home_hidden.1 = (bf16[320,768]{1,0:T(8,128)(2,1)S(1)}, bf16[320,1536]{1,0:T(8,128)(2,1)S(1)}, bf16[320,2048]{1,0:T(8,128)(2,1)S(1)}, bf16[320,2048]{1,0:T(8,128)(2,1)S(1)}) custom-call(bf16[640,2048]{1,0:T(8,128)(2,1)} %bitcast.19.after_ref.recv_ref, bf16[80,160]{1,0:T(8,128)(2,1)S(1)} %get-tuple-element.69.pick_x_ref, ...), custom_call_target="tpu_custom_call" | custom-call | flops 1000000 | bytes 100000 | tf_op jit(solution)/shard_map/home_hidden/pallas_call | solution.py:44
  129.2 2.5 collective-permute-done.11.refs_1_
  131.7 9.4 %home_grads.1 = (bf16[2,256,1536]{2,1,0:T(8,128)(2,1)}, bf16[2,256,768]{2,1,0:T(8,128)(2,1)S(1)}, bf16[2,256,768]{2,1,0:T(8,128)(2,1)S(1)}, bf16[2,2,256,768]{3,...) custom-call(s32[6]{0:T(128)S(1)} %concatenate.10.here_ref, ...), custom_call_target="tpu_custom_call" | custom-call | flops 1000000 | bytes 100000 | tf_op jit(solution)/shard_map/home_grads/pallas_call | solution.py:44
  142.0 1.8 collective-permute-start.18
  143.8 1.8 collective-permute-start.12
  145.6 2.1 collective-permute-start.28
  147.9 10.5 %collective-permute-done.12.refs_2_ = bf16[2,4,144,256]{3,2,1,0:T(8,128)(2,1)S(1)} collective-permute-done((bf16[2,4,144,256]{3,2,1,0:T(8,128)(2,1)S(1)}, bf16[2,4,144,256]{3,2,1,0:T(8,128)(2,1)S(1)}, u32[]{:S(2)}, u32[]{:S(2)}) %collective-permute-start.12) | collective-permute-done | bytes 589856 | tf_op jit(solution)/shard_map/ppermute | solution.py:24
  158.4 1.4 copy-done.5
  160.2 1.9 collective-permute-start.16
  162.1 12.1 %home_rows.1.refs_2_ = bf16[640,2048]{1,0:T(8,128)(2,1)} custom-call(bf16[320,768]{1,0:T(8,128)(2,1)S(1)} %get-tuple-element.34.act_ref, bf16[320,1536]{1,0:T(8,128)(2,1)S(1)} %get-tuple-element.35.gh_ref, bf16[320,640]{1,0:T(8,128)(2,1)S(1)} %get-tuple-element.71.pick_x_ref, bf16[320,640]{1,0:T(8,128)(2,1)S(1)} %get-tuple-element.72.pick_g_ref, ...), custom_call_target="tpu_custom_call" | custom-call | flops 1000000 | bytes 100000 | tf_op jit(solution)/shard_map/home_rows/pallas_call | solution.py:44
  174.2 7.1 %all-to-all-start.1 = ((bf16[16,40,2048]{2,1,0:T(8,128)(2,1)}), bf16[16,40,2048]{2,1,0:T(8,128)(2,1)S(1)}, u32[]{:S(2)}, u32[]{:S(2)}) async-start(bf16[16,40,2048]{2,1,0:T(8,128)(2,1)} %bitcast.24), calls=%async_computation.1 | async-start | bytes 5242880 | tf_op jit(solution)/shard_map/all_to_all | solution.py:420
  181.3 1.5 slice_bitcast_fusion.2
  183.1 2.8 %collective-permute-start.26 = (bf16[2,256,768]{2,1,0:T(8,128)(2,1)S(1)}, bf16[2,256,768]{2,1,0:T(8,128)(2,1)S(1)}, u32[]{:S(2)}, u32[]{:S(2)}) collective-permute-start(bf16[2,256,768]{2,1,0:T(8,128)(2,1)S(1)} %sum_down.1.refs_3_), channel_id=1, source_target_pairs={{0,48},{1,49},{2,50},{3,51},{4,52},{5,53},{6,54},{7,55},{8,56},{9,... | collective-permute-start | bytes 2359304 | tf_op jit(solution)/shard_map/ppermute | solution.py:24
  185.9 1.5 slice_bitcast_fusion.3
  187.8 3.8 %collective-permute-start.20 = (bf16[144,256]{1,0:T(8,128)(2,1)S(1)}, bf16[144,256]{1,0:T(8,128)(2,1)S(1)}, u32[]{:S(2)}, u32[]{:S(2)}) collective-permute-start(bf16[144,256]{1,0:T(8,128)(2,1)S(1)} %get-tuple-element.68), channel_id=1, source_target_pairs={{0,32},{1,33},{2,34},{3,35},{4,36},{5,37},{6,38},{7,39},{8,40},{9,... | collective-permute-start | bytes 221192 | tf_op jit(solution)/shard_map/ppermute | solution.py:24
  191.7 2.2 add_convert_fusion
  193.9 10.3 %collective-permute-done.26 = bf16[2,256,768]{2,1,0:T(8,128)(2,1)S(1)} collective-permute-done((bf16[2,256,768]{2,1,0:T(8,128)(2,1)S(1)}, bf16[2,256,768]{2,1,0:T(8,128)(2,1)S(1)}, u32[]{:S(2)}, u32[]{:S(2)}) %collective-permute-start.26) | collective-permute-done | bytes 786464 | tf_op jit(solution)/shard_map/ppermute | solution.py:24
  204.2 3.4 %collective-permute-done.25 = bf16[2,256,768]{2,1,0:T(8,128)(2,1)S(1)} collective-permute-done((bf16[2,256,768]{2,1,0:T(8,128)(2,1)S(1)}, bf16[2,256,768]{2,1,0:T(8,128)(2,1)S(1)}, u32[]{:S(2)}, u32[]{:S(2)}) %collective-permute-start.25) | collective-permute-done | bytes 786464 | tf_op jit(solution)/shard_map/ppermute | solution.py:24
  208.2 1.2 slice_bitcast_fusion
  209.4 2.1 collective-permute-start.27
  211.5 1.1 slice_bitcast_fusion.8
  212.6 1.3 collective-permute-start.30
  214.0 1.4 collective-permute-start.31
  217.1 4.4 %collective-permute-done.22.refs_1_ = bf16[144,256]{1,0:T(8,128)(2,1)S(1)} collective-permute-done((bf16[144,256]{1,0:T(8,128)(2,1)}, bf16[144,256]{1,0:T(8,128)(2,1)S(1)}, u32[]{:S(2)}, u32[]{:S(2)}) %collective-permute-start.22) | collective-permute-done | bytes 73760 | tf_op jit(solution)/shard_map/ppermute | solution.py:24
  222.2 1.7 collective-permute-start.23
  223.8 4.0 %collective-permute-done.23.refs_2_ = bf16[144,256]{1,0:T(8,128)(2,1)S(1)} collective-permute-done((bf16[144,256]{1,0:T(8,128)(2,1)}, bf16[144,256]{1,0:T(8,128)(2,1)S(1)}, u32[]{:S(2)}, u32[]{:S(2)}) %collective-permute-start.23) | collective-permute-done | bytes 73760 | tf_op jit(solution)/shard_map/ppermute | solution.py:24
  228.6 1.3 copy-done.4
  231.0 4.6 %unpack_rows.1 = (bf16[256,2048]{1,0:T(8,128)(2,1)}, bf16[256,2048]{1,0:T(8,128)(2,1)}) custom-call(s32[2,256]{1,0:T(2,128)S(1)} %get-tuple-element.29.pos_ref, f32[256,2]{1,0:T(8,128)S(1)} %copy.12.gate_ref, bf16[640,2048]{1,0:T(8,128)(2,1)S(1)} %bitcast.78, bf16[2,160,2048]{2,1,0:T(8,128)(2,1)S(1)} %copy-done.4, bf16[160,2048]{1,0:T(8,128)(2,1)S(1)} %copy-done.14), custom_call_target="tpu_custom_call" | custom-call | flops 1000000 | bytes 100000 | tf_op jit(solution)/shard_map/unpack_rows/pallas_call | solution.py:44
  235.7 1.2 copy-done.10
  238.3 5.2 %collective-permute-done.32 = bf16[4,144,256]{2,1,0:T(8,128)(2,1)S(1)} collective-permute-done((bf16[4,144,256]{2,1,0:T(8,128)(2,1)S(1)}, bf16[4,144,256]{2,1,0:T(8,128)(2,1)S(1)}, u32[]{:S(2)}, u32[]{:S(2)}) %collective-permute-start.32) | collective-permute-done | bytes 294944 | tf_op jit(solution)/shard_map/ppermute | solution.py:24
  243.6 8.9 %collective-permute-start.33 = (bf16[2,4,144,256]{3,2,1,0:T(8,128)(2,1)S(1)}, bf16[2,4,144,256]{3,2,1,0:T(8,128)(2,1)S(1)}, u32[]{:S(2)}, u32[]{:S(2)}) collective-permute-start(bf16[2,4,144,256]{3,2,1,0:T(8,128)(2,1)S(1)} %pad_maximum_fusion.2.spare_ref), channel_id=1, source_target_pairs={{0,1},{1,0},{2,3},{3,2},{4,5},{5,4},{6,7},{7,6},{8,9},{9,8},{10,11... | collective-permute-start | bytes 1769480 | tf_op jit(solution)/shard_map/ppermute | solution.py:24
  252.5 1.6 collective-permute-done.33.more_ref
  254.2 4.0 %finish_grads.1 = (f32[256,1536]{1,0:T(8,128)}, f32[96,2048]{1,0:T(8,128)}) custom-call(s32[6]{0:T(128)S(1)} %concatenate.10.here_ref, bf16[2,4,144,256]{3,2,1,0:T(8,128)(2,1)S(1)} %pad_maximum_fusion.2.spare_ref, bf16[2,4,144,256]{3,2,1,0:T(8,128)(2,1)S(1)} %collective-permute-done.33.more_ref, bf16[768,768]{1,0:T(8,128)(2,1)} %copy-done.2, ...), custom_call_target="tpu_custom_call" | custom-call | flops 1000000 | bytes 100000 | tf_op jit(solution)/shard_map/finish_grads/pallas_call | solution.py:44
  (112 shorter events, 17.4 us)
Async XLA Ops:
  0.6 1.2 copy-start.7
  1.2 12.4 %copy-start.2 = (bf16[768,768]{1,0:T(8,128)(2,1)}, bf16[768,768]{1,0:T(8,128)(2,1)S(1)}, u32[]{:S(2)}) copy-start(bf16[768,768]{1,0:T(8,128)(2,1)S(1)} %fusion.pick_ref) | copy-start | bytes 3538948
  1.9 2.8 %copy-start = (bf16[1,2048,1536]{2,1,0:T(8,128)(2,1)S(1)}, bf16[1,2048,1536]{2,1,0:T(8,128)(2,1)}, u32[]{:S(2)}) copy-start(bf16[1,2048,1536]{2,1,0:T(8,128)(2,1)} %param.11) | copy-start | bytes 18874372
  4.6 1.9 copy-start.1
  6.5 1.2 copy-start.8
  7.8 0.7 copy-start.24
  8.4 0.7 copy-start.26
  9.1 0.7 copy-start.27
  9.8 0.7 copy-start.28
  14.7 3.4 %collective-permute-start = (bf16[2,576,256]{2,1,0:T(8,128)(2,1)S(1)}, bf16[2,576,256]{2,1,0:T(8,128)(2,1)S(1)}, u32[]{:S(2)}, u32[]{:S(2)}) collective-permute-start(bf16[2,576,256]{2,1,0:T(8,128)(2,1)S(1)} %slice_bitcast_fusion.7), channel_id=1, source_target_pairs={{0,1},{1,0},{2,3},{3,2},{4,5},{5,4},{6,7},{7,6},{8,9},{9,8},{10,11... | collective-permute-start | bytes 1769480 | tf_op jit(solution)/shard_map/ppermute | solution.py:24
  19.2 8.7 %collective-permute-start.1 = (bf16[576,256]{1,0:T(8,128)(2,1)S(1)}, bf16[576,256]{1,0:T(8,128)(2,1)S(1)}, u32[]{:S(2)}, u32[]{:S(2)}) collective-permute-start(bf16[576,256]{1,0:T(8,128)(2,1)S(1)} %slice_bitcast_fusion.14), channel_id=1, source_target_pairs={{0,2},{1,3},{2,0},{3,1},{4,6},{5,7},{6,4},{7,5},{8,10},{9,11},{10,... | collective-permute-start | bytes 884744 | tf_op jit(solution)/shard_map/ppermute | solution.py:24
  28.7 10.6 %collective-permute-start.2 = (bf16[576,256]{1,0:T(8,128)(2,1)}, bf16[576,256]{1,0:T(8,128)(2,1)S(1)}, u32[]{:S(2)}, u32[]{:S(2)}) collective-permute-start(bf16[576,256]{1,0:T(8,128)(2,1)} %fusion.3), channel_id=1, source_target_pairs={{0,4},{1,5},{2,6},{3,7},{4,8},{5,9},{6,10},{7,11},{8,12},{9,13},{1... | collective-permute-start | bytes 884744 | tf_op jit(solution)/shard_map/ppermute | solution.py:24
  30.4 16.2 %collective-permute-start.3 = (bf16[576,256]{1,0:T(8,128)(2,1)}, bf16[576,256]{1,0:T(8,128)(2,1)}, u32[]{:S(2)}, u32[]{:S(2)}) collective-permute-start(bf16[576,256]{1,0:T(8,128)(2,1)} %fusion.3), channel_id=1, source_target_pairs={{0,8},{1,9},{2,10},{3,11},{4,12},{5,13},{6,14},{7,15},{8,0},{9,1},... | collective-permute-start | bytes 884744 | tf_op jit(solution)/shard_map/ppermute | solution.py:24
  33.7 12.9 %collective-permute-start.4 = (bf16[576,256]{1,0:T(8,128)(2,1)}, bf16[576,256]{1,0:T(8,128)(2,1)}, u32[]{:S(2)}, u32[]{:S(2)}) collective-permute-start(bf16[576,256]{1,0:T(8,128)(2,1)} %fusion.3), channel_id=1, source_target_pairs={{0,12},{1,13},{2,14},{3,15},{4,0},{5,1},{6,2},{7,3},{8,4},{9,5},{1... | collective-permute-start | bytes 884744 | tf_op jit(solution)/shard_map/ppermute | solution.py:24
  34.5 23.9 %copy-start.9 = (bf16[256,2048]{1,0:T(8,128)(2,1)S(1)}, bf16[256,2048]{1,0:T(8,128)(2,1)}, u32[]{:S(2)}) copy-start(bf16[256,2048]{1,0:T(8,128)(2,1)} %cot_ref.3) | copy-start | bytes 3145732
  34.5 23.9 %copy-start.25 = (f32[256,2]{0,1:T(2,128)S(1)}, f32[256,2]{0,1:T(2,128)}, u32[]{:S(2)}) copy-start(f32[256,2]{0,1:T(2,128)} %param.10) | copy-start | bytes 6148
  34.5 23.9 %collective-permute-start.6 = (bf16[160,2048]{1,0:T(8,128)(2,1)S(1)}, bf16[160,2048]{1,0:T(8,128)(2,1)S(1)}, u32[]{:S(2)}, u32[]{:S(2)}) collective-permute-start(bf16[160,2048]{1,0:T(8,128)(2,1)S(1)} %keep_rows.1.own_ref), channel_id=1, source_target_pairs={{0,2},{1,3},{2,0},{3,1},{4,6},{5,7},{6,4},{7,5},{8,10},{9,11},{10,... | collective-permute-start | bytes 1966088 | tf_op jit(solution)/shard_map/ppermute | solution.py:24
  47.6 10.7 %collective-permute-start.5 = (bf16[576,256]{1,0:T(8,128)(2,1)S(1)}, bf16[576,256]{1,0:T(8,128)(2,1)S(1)}, u32[]{:S(2)}, u32[]{:S(2)}) collective-permute-start(bf16[576,256]{1,0:T(8,128)(2,1)S(1)} %select_select_fusion), channel_id=1, source_target_pairs={{0,64},{1,65},{2,66},{3,67},{4,68},{5,69},{6,70},{7,71},{8,72},{9,... | collective-permute-start | bytes 884744 | tf_op jit(solution)/shard_map/ppermute | solution.py:24
  61.5 39.0 %all-to-all-start = ((bf16[16,40,2048]{2,1,0:T(8,128)(2,1)}), bf16[16,40,2048]{2,1,0:T(8,128)(2,1)}, u32[]{:S(2)}, u32[]{:S(2)}) async-start(bf16[16,40,2048]{2,1,0:T(8,128)(2,1)} %bitcast.18), calls=%async_computation | async-start | bytes 5242880 | tf_op jit(solution)/shard_map/all_to_all | solution.py:368
  68.8 30.4 %collective-permute-start.7 = (bf16[2,160,2048]{2,1,0:T(8,128)(2,1)}, bf16[2,160,2048]{2,1,0:T(8,128)(2,1)}, u32[]{:S(2)}, u32[]{:S(2)}) collective-permute-start(bf16[2,160,2048]{2,1,0:T(8,128)(2,1)} %pad_maximum_fusion), channel_id=1, source_target_pairs={{0,1},{1,0},{2,3},{3,2},{4,5},{5,4},{6,7},{7,6},{8,9},{9,8},{10,11... | collective-permute-start | bytes 3932168 | tf_op jit(solution)/shard_map/ppermute | solution.py:24
  69.1 27.7 %collective-permute-start.10 = (bf16[2,576,256]{2,1,0:T(8,128)(2,1)S(1)}, bf16[2,576,256]{2,1,0:T(8,128)(2,1)S(1)}, u32[]{:S(2)}, u32[]{:S(2)}) collective-permute-start(bf16[2,576,256]{2,1,0:T(8,128)(2,1)S(1)} %pad_maximum_fusion.1.refs_0_.w0_ref), channel_id=1, source_target_pairs={{0,48},{1,49},{2,50},{3,51},{4,52},{5,53},{6,54},{7,55},{8,56},{9,... | collective-permute-start | bytes 1769480 | tf_op jit(solution)/shard_map/ppermute | solution.py:24
  71.8 25.0 %collective-permute-start.8 = (bf16[2,576,256]{2,1,0:T(8,128)(2,1)S(1)}, bf16[2,576,256]{2,1,0:T(8,128)(2,1)S(1)}, u32[]{:S(2)}, u32[]{:S(2)}) collective-permute-start(bf16[2,576,256]{2,1,0:T(8,128)(2,1)S(1)} %pad_maximum_fusion.1.refs_0_.w0_ref), channel_id=1, source_target_pairs={{0,16},{1,17},{2,18},{3,19},{4,20},{5,21},{6,22},{7,23},{8,24},{9,... | collective-permute-start | bytes 1769480 | tf_op jit(solution)/shard_map/ppermute | solution.py:24
  71.8 27.4 %collective-permute-start.9 = (bf16[2,576,256]{2,1,0:T(8,128)(2,1)S(1)}, bf16[2,576,256]{2,1,0:T(8,128)(2,1)}, u32[]{:S(2)}, u32[]{:S(2)}) collective-permute-start(bf16[2,576,256]{2,1,0:T(8,128)(2,1)S(1)} %pad_maximum_fusion.1.refs_0_.w0_ref), channel_id=1, source_target_pairs={{0,32},{1,33},{2,34},{3,35},{4,36},{5,37},{6,38},{7,39},{8,40},{9,... | collective-permute-start | bytes 1769480 | tf_op jit(solution)/shard_map/ppermute | solution.py:24
  108.2 3.7 %collective-permute-start.14 = (bf16[2,160,2048]{2,1,0:T(8,128)(2,1)}, bf16[2,160,2048]{2,1,0:T(8,128)(2,1)S(1)}, u32[]{:S(2)}, u32[]{:S(2)}) collective-permute-start(bf16[2,160,2048]{2,1,0:T(8,128)(2,1)} %get-tuple-element.42), channel_id=1, source_target_pairs={{0,1},{1,0},{2,3},{3,2},{4,5},{5,4},{6,7},{7,6},{8,9},{9,8},{10,11... | collective-permute-start | bytes 3932168 | tf_op jit(solution)/shard_map/ppermute | solution.py:24
  113.7 1.1 copy-start.3
  114.8 16.9 %collective-permute-start.15 = (bf16[160,2048]{1,0:T(8,128)(2,1)S(1)}, bf16[160,2048]{1,0:T(8,128)(2,1)S(1)}, u32[]{:S(2)}, u32[]{:S(2)}) collective-permute-start(bf16[160,2048]{1,0:T(8,128)(2,1)S(1)} %slice_bitcast_fusion.6), channel_id=1, source_target_pairs={{0,2},{1,3},{2,0},{3,1},{4,6},{5,7},{6,4},{7,5},{8,10},{9,11},{10,... | collective-permute-start | bytes 1966088 | tf_op jit(solution)/shard_map/ppermute | solution.py:24
  116.3 15.4 %collective-permute-start.11 = (bf16[2,4,144,256]{3,2,1,0:T(8,128)(2,1)S(1)}, bf16[2,4,144,256]{3,2,1,0:T(8,128)(2,1)S(1)}, u32[]{:S(2)}, u32[]{:S(2)}) collective-permute-start(bf16[2,4,144,256]{3,2,1,0:T(8,128)(2,1)S(1)} %get-tuple-element.36), channel_id=1, source_target_pairs={{0,4},{1,5},{2,6},{3,7},{4,8},{5,9},{6,10},{7,11},{8,12},{9,13},{1... | collective-permute-start | bytes 1769480 | tf_op jit(solution)/shard_map/ppermute | solution.py:24
  117.5 14.2 %collective-permute-start.13 = (bf16[2,4,144,256]{3,2,1,0:T(8,128)(2,1)S(1)}, bf16[2,4,144,256]{3,2,1,0:T(8,128)(2,1)S(1)}, u32[]{:S(2)}, u32[]{:S(2)}) collective-permute-start(bf16[2,4,144,256]{3,2,1,0:T(8,128)(2,1)S(1)} %get-tuple-element.38), channel_id=1, source_target_pairs={{0,12},{1,13},{2,14},{3,15},{4,0},{5,1},{6,2},{7,3},{8,4},{9,5},{1... | collective-permute-start | bytes 1769480 | tf_op jit(solution)/shard_map/ppermute | solution.py:24
  128.2 1.1 copy-start.15
  131.7 9.4 %copy-start.13 = (bf16[160,2048]{1,0:T(8,128)(2,1)}, bf16[160,2048]{1,0:T(8,128)(2,1)S(1)}, u32[]{:S(2)}) copy-start(bf16[160,2048]{1,0:T(8,128)(2,1)S(1)} %collective-permute-done.15.refs_0_.hot_b_ref) | copy-start | bytes 1966084
  141.2 0.9 copy-start.18
  142.0 16.4 %copy-start.16 = (bf16[2,256,768]{2,1,0:T(8,128)(2,1)}, bf16[2,256,768]{2,1,0:T(8,128)(2,1)S(1)}, u32[]{:S(2)}) copy-start(bf16[2,256,768]{2,1,0:T(8,128)(2,1)S(1)} %get-tuple-element.46.refs_0_) | copy-start | bytes 2359300
  142.0 39.3 %collective-permute-start.18 = (bf16[2,2,256,768]{3,2,1,0:T(8,128)(2,1)}, bf16[2,2,256,768]{3,2,1,0:T(8,128)(2,1)}, u32[]{:S(2)}, u32[]{:S(2)}) collective-permute-start(bf16[2,2,256,768]{3,2,1,0:T(8,128)(2,1)} %get-tuple-element.49), channel_id=1, source_target_pairs={{0,48},{1,49},{2,50},{3,51},{4,52},{5,53},{6,54},{7,55},{8,56},{9,... | collective-permute-start | bytes 4718600 | tf_op jit(solution)/shard_map/ppermute | solution.py:24
  143.8 42.1 %collective-permute-start.17 = (bf16[2,2,256,768]{3,2,1,0:T(8,128)(2,1)}, bf16[2,2,256,768]{3,2,1,0:T(8,128)(2,1)}, u32[]{:S(2)}, u32[]{:S(2)}) collective-permute-start(bf16[2,2,256,768]{3,2,1,0:T(8,128)(2,1)} %get-tuple-element.47), channel_id=1, source_target_pairs={{0,16},{1,17},{2,18},{3,19},{4,20},{5,21},{6,22},{7,23},{8,24},{9,... | collective-permute-start | bytes 4718600 | tf_op jit(solution)/shard_map/ppermute | solution.py:24
  143.8 14.6 %collective-permute-start.12 = (bf16[2,4,144,256]{3,2,1,0:T(8,128)(2,1)S(1)}, bf16[2,4,144,256]{3,2,1,0:T(8,128)(2,1)S(1)}, u32[]{:S(2)}, u32[]{:S(2)}) collective-permute-start(bf16[2,4,144,256]{3,2,1,0:T(8,128)(2,1)S(1)} %get-tuple-element.37), channel_id=1, source_target_pairs={{0,8},{1,9},{2,10},{3,11},{4,12},{5,13},{6,14},{7,15},{8,0},{9,1},... | collective-permute-start | bytes 1769480 | tf_op jit(solution)/shard_map/ppermute | solution.py:24
  145.6 46.0 %collective-permute-start.28 = (bf16[4,96,2048]{2,1,0:T(8,128)(2,1)}, bf16[4,96,2048]{2,1,0:T(8,128)(2,1)}, u32[]{:S(2)}, u32[]{:S(2)}) collective-permute-start(bf16[4,96,2048]{2,1,0:T(8,128)(2,1)} %get-tuple-element.51), channel_id=1, source_target_pairs={{0,64},{1,65},{2,66},{3,67},{4,68},{5,69},{6,70},{7,71},{8,72},{9,... | collective-permute-start | bytes 4718600 | tf_op jit(solution)/shard_map/ppermute | solution.py:24
  158.4 1.4 copy-start.5
  160.2 27.4 %collective-permute-start.16 = (bf16[4,144,256]{2,1,0:T(8,128)(2,1)S(1)}, bf16[4,144,256]{2,1,0:T(8,128)(2,1)S(1)}, u32[]{:S(2)}, u32[]{:S(2)}) collective-permute-start(bf16[4,144,256]{2,1,0:T(8,128)(2,1)S(1)} %get-tuple-element.64), channel_id=1, source_target_pairs={{0,64},{1,65},{2,66},{3,67},{4,68},{5,69},{6,70},{7,71},{8,72},{9,... | collective-permute-start | bytes 884744 | tf_op jit(solution)/shard_map/ppermute | solution.py:24
  174.2 54.4 %all-to-all-start.1 = ((bf16[16,40,2048]{2,1,0:T(8,128)(2,1)}), bf16[16,40,2048]{2,1,0:T(8,128)(2,1)S(1)}, u32[]{:S(2)}, u32[]{:S(2)}) async-start(bf16[16,40,2048]{2,1,0:T(8,128)(2,1)} %bitcast.24), calls=%async_computation.1 | async-start | bytes 5242880 | tf_op jit(solution)/shard_map/all_to_all | solution.py:420
  181.3 1.6 copy-start.19
  183.1 4.3 %copy-start.17 = (bf16[2,256,768]{2,1,0:T(8,128)(2,1)S(1)}, bf16[2,256,768]{2,1,0:T(8,128)(2,1)}, u32[]{:S(2)}) copy-start(bf16[2,256,768]{2,1,0:T(8,128)(2,1)} %copy-done.16) | copy-start | bytes 2359300
  183.1 21.1 %collective-permute-start.26 = (bf16[2,256,768]{2,1,0:T(8,128)(2,1)S(1)}, bf16[2,256,768]{2,1,0:T(8,128)(2,1)S(1)}, u32[]{:S(2)}, u32[]{:S(2)}) collective-permute-start(bf16[2,256,768]{2,1,0:T(8,128)(2,1)S(1)} %sum_down.1.refs_3_), channel_id=1, source_target_pairs={{0,48},{1,49},{2,50},{3,51},{4,52},{5,53},{6,54},{7,55},{8,56},{9,... | collective-permute-start | bytes 2359304 | tf_op jit(solution)/shard_map/ppermute | solution.py:24
  187.5 4.1 %copy-start.29 = (bf16[4,96,2048]{2,1,0:T(8,128)(2,1)S(1)}, bf16[4,96,2048]{2,1,0:T(8,128)(2,1)}, u32[]{:S(2)}) copy-start(bf16[4,96,2048]{2,1,0:T(8,128)(2,1)} %get-tuple-element.50) | copy-start | bytes 4718596
  187.5 20.0 %collective-permute-start.25 = (bf16[2,256,768]{2,1,0:T(8,128)(2,1)S(1)}, bf16[2,256,768]{2,1,0:T(8,128)(2,1)S(1)}, u32[]{:S(2)}, u32[]{:S(2)}) collective-permute-start(bf16[2,256,768]{2,1,0:T(8,128)(2,1)S(1)} %sum_up.1.refs_2_), channel_id=1, source_target_pairs={{0,16},{1,17},{2,18},{3,19},{4,20},{5,21},{6,22},{7,23},{8,24},{9,... | collective-permute-start | bytes 2359304 | tf_op jit(solution)/shard_map/ppermute | solution.py:24
  187.7 24.9 %collective-permute-start.19 = (bf16[144,256]{1,0:T(8,128)(2,1)S(1)}, bf16[144,256]{1,0:T(8,128)(2,1)S(1)}, u32[]{:S(2)}, u32[]{:S(2)}) collective-permute-start(bf16[144,256]{1,0:T(8,128)(2,1)S(1)} %get-tuple-element.66), channel_id=1, source_target_pairs={{0,16},{1,17},{2,18},{3,19},{4,20},{5,21},{6,22},{7,23},{8,24},{9,... | collective-permute-start | bytes 221192 | tf_op jit(solution)/shard_map/ppermute | solution.py:24
  187.8 26.1 %collective-permute-start.20 = (bf16[144,256]{1,0:T(8,128)(2,1)S(1)}, bf16[144,256]{1,0:T(8,128)(2,1)S(1)}, u32[]{:S(2)}, u32[]{:S(2)}) collective-permute-start(bf16[144,256]{1,0:T(8,128)(2,1)S(1)} %get-tuple-element.68), channel_id=1, source_target_pairs={{0,32},{1,33},{2,34},{3,35},{4,36},{5,37},{6,38},{7,39},{8,40},{9,... | collective-permute-start | bytes 221192 | tf_op jit(solution)/shard_map/ppermute | solution.py:24
  191.6 23.8 %collective-permute-start.21 = (bf16[144,256]{1,0:T(8,128)(2,1)S(1)}, bf16[144,256]{1,0:T(8,128)(2,1)S(1)}, u32[]{:S(2)}, u32[]{:S(2)}) collective-permute-start(bf16[144,256]{1,0:T(8,128)(2,1)S(1)} %get-tuple-element.67), channel_id=1, source_target_pairs={{0,48},{1,49},{2,50},{3,51},{4,52},{5,53},{6,54},{7,55},{8,56},{9,... | collective-permute-start | bytes 221192 | tf_op jit(solution)/shard_map/ppermute | solution.py:24
  191.7 15.9 %copy-start.6 = (bf16[2,256,1536]{2,1,0:T(8,128)(2,1)S(1)}, bf16[2,256,1536]{2,1,0:T(8,128)(2,1)}, u32[]{:S(2)}) copy-start(bf16[2,256,1536]{2,1,0:T(8,128)(2,1)} %get-tuple-element.43.refs_4_) | copy-start | bytes 4718596
  209.4 26.2 %collective-permute-start.27 = (bf16[256,1536]{1,0:T(8,128)(2,1)}, bf16[256,1536]{1,0:T(8,128)(2,1)}, u32[]{:S(2)}, u32[]{:S(2)}) collective-permute-start(bf16[256,1536]{1,0:T(8,128)(2,1)} %get-tuple-element.55), channel_id=1, source_target_pairs={{0,64},{1,65},{2,66},{3,67},{4,68},{5,69},{6,70},{7,71},{8,72},{9,... | collective-permute-start | bytes 2359304 | tf_op jit(solution)/shard_map/ppermute | solution.py:24
  212.6 23.0 %collective-permute-start.29 = (bf16[96,2048]{1,0:T(8,128)(2,1)}, bf16[96,2048]{1,0:T(8,128)(2,1)S(1)}, u32[]{:S(2)}, u32[]{:S(2)}) collective-permute-start(bf16[96,2048]{1,0:T(8,128)(2,1)} %get-tuple-element.58), channel_id=1, source_target_pairs={{0,16},{1,17},{2,18},{3,19},{4,20},{5,21},{6,22},{7,23},{8,24},{9,... | collective-permute-start | bytes 1179656 | tf_op jit(solution)/shard_map/ppermute | solution.py:24
  212.6 23.0 %collective-permute-start.30 = (bf16[96,2048]{1,0:T(8,128)(2,1)}, bf16[96,2048]{1,0:T(8,128)(2,1)}, u32[]{:S(2)}, u32[]{:S(2)}) collective-permute-start(bf16[96,2048]{1,0:T(8,128)(2,1)} %get-tuple-element.57), channel_id=1, source_target_pairs={{0,32},{1,33},{2,34},{3,35},{4,36},{5,37},{6,38},{7,39},{8,40},{9,... | collective-permute-start | bytes 1179656 | tf_op jit(solution)/shard_map/ppermute | solution.py:24
  214.0 21.6 %collective-permute-start.31 = (bf16[96,2048]{1,0:T(8,128)(2,1)}, bf16[96,2048]{1,0:T(8,128)(2,1)}, u32[]{:S(2)}, u32[]{:S(2)}) collective-permute-start(bf16[96,2048]{1,0:T(8,128)(2,1)} %get-tuple-element.56), channel_id=1, source_target_pairs={{0,48},{1,49},{2,50},{3,51},{4,52},{5,53},{6,54},{7,55},{8,56},{9,... | collective-permute-start | bytes 1179656 | tf_op jit(solution)/shard_map/ppermute | solution.py:24
  216.1 5.5 %collective-permute-start.22 = (bf16[144,256]{1,0:T(8,128)(2,1)}, bf16[144,256]{1,0:T(8,128)(2,1)S(1)}, u32[]{:S(2)}, u32[]{:S(2)}) collective-permute-start(bf16[144,256]{1,0:T(8,128)(2,1)} %fusion.6.refs_0_), channel_id=1, source_target_pairs={{0,4},{1,5},{2,6},{3,7},{4,8},{5,9},{6,10},{7,11},{8,12},{9,13},{1... | collective-permute-start | bytes 221192 | tf_op jit(solution)/shard_map/ppermute | solution.py:24
  222.2 5.7 %collective-permute-start.23 = (bf16[144,256]{1,0:T(8,128)(2,1)}, bf16[144,256]{1,0:T(8,128)(2,1)S(1)}, u32[]{:S(2)}, u32[]{:S(2)}) collective-permute-start(bf16[144,256]{1,0:T(8,128)(2,1)} %fusion.6.refs_0_), channel_id=1, source_target_pairs={{0,8},{1,9},{2,10},{3,11},{4,12},{5,13},{6,14},{7,15},{8,0},{9,1},... | collective-permute-start | bytes 221192 | tf_op jit(solution)/shard_map/ppermute | solution.py:24
  228.5 7.1 %collective-permute-start.24 = (bf16[144,256]{1,0:T(8,128)(2,1)}, bf16[144,256]{1,0:T(8,128)(2,1)}, u32[]{:S(2)}, u32[]{:S(2)}) collective-permute-start(bf16[144,256]{1,0:T(8,128)(2,1)} %fusion.6.refs_0_), channel_id=1, source_target_pairs={{0,12},{1,13},{2,14},{3,15},{4,0},{5,1},{6,2},{7,3},{8,4},{9,5},{1... | collective-permute-start | bytes 221192 | tf_op jit(solution)/shard_map/ppermute | solution.py:24
  228.6 1.3 copy-start.4
  229.9 1.1 copy-start.14
  231.0 4.6 %copy-start.21 = (bf16[144,256]{1,0:T(8,128)(2,1)S(1)}, bf16[144,256]{1,0:T(8,128)(2,1)}, u32[]{:S(2)}) copy-start(bf16[144,256]{1,0:T(8,128)(2,1)} %copy-done.20) | copy-start | bytes 221188
  231.0 4.6 %copy-start.23 = (bf16[144,256]{1,0:T(8,128)(2,1)S(1)}, bf16[144,256]{1,0:T(8,128)(2,1)}, u32[]{:S(2)}) copy-start(bf16[144,256]{1,0:T(8,128)(2,1)} %copy-done.22) | copy-start | bytes 221188
  235.6 1.2 copy-start.10
  236.9 17.3 %copy-start.12 = (bf16[256,1536]{1,0:T(8,128)(2,1)S(1)}, bf16[256,1536]{1,0:T(8,128)(2,1)}, u32[]{:S(2)}) copy-start(bf16[256,1536]{1,0:T(8,128)(2,1)} %get-tuple-element.54.in_ref) | copy-start | bytes 2359300
  237.9 16.3 %copy-start.11 = (bf16[256,2048]{1,0:T(8,128)(2,1)S(1)}, bf16[256,2048]{1,0:T(8,128)(2,1)}, u32[]{:S(2)}) copy-start(bf16[256,2048]{1,0:T(8,128)(2,1)} %get-tuple-element.25.refs_4_.after_ref) | copy-start | bytes 3145732
  237.9 5.7 %collective-permute-start.32 = (bf16[4,144,256]{2,1,0:T(8,128)(2,1)S(1)}, bf16[4,144,256]{2,1,0:T(8,128)(2,1)S(1)}, u32[]{:S(2)}, u32[]{:S(2)}) collective-permute-start(bf16[4,144,256]{2,1,0:T(8,128)(2,1)S(1)} %stack_z.1), channel_id=1, source_target_pairs={{0,2},{1,3},{2,0},{3,1},{4,6},{5,7},{6,4},{7,5},{8,10},{9,11},{10,... | collective-permute-start | bytes 884744 | tf_op jit(solution)/shard_map/ppermute | solution.py:24
  243.6 10.5 %collective-permute-start.33 = (bf16[2,4,144,256]{3,2,1,0:T(8,128)(2,1)S(1)}, bf16[2,4,144,256]{3,2,1,0:T(8,128)(2,1)S(1)}, u32[]{:S(2)}, u32[]{:S(2)}) collective-permute-start(bf16[2,4,144,256]{3,2,1,0:T(8,128)(2,1)S(1)} %pad_maximum_fusion.2.spare_ref), channel_id=1, source_target_pairs={{0,1},{1,0},{2,3},{3,2},{4,5},{5,4},{6,7},{7,6},{8,9},{9,8},{10,11... | collective-permute-start | bytes 1769480 | tf_op jit(solution)/shard_map/ppermute | solution.py:24
  (2 other events, 1.3 us)
